TPU v7x, 32 devices: a whole 2x2x4 slice. The times are simulated.
32 devices in a mesh: dp: 4 (over x, core), wide: 8 (over z, y).
Axes of the slice: x: 2, y: 2, z: 4, core: 2. Of those that a mesh axis runs over, the one named last changes fastest.
Arguments:
- x_in: float32 [4096, 2048], P(('dp', 'wide')), may hold values from -6 to 6
- lengths: int32 [4, 4], P('dp'), may hold values from 1 to 1021, as said below
- modality: int32 [4096], P(('dp', 'wide')), may hold values from 0 to 2, as said below
- norm_gain: float32 [2048], replicated, may hold values from 0.5 to 1.5
- conv_weight: float32 [4, 4096], replicated, may hold values from -3 to 3
- conv_bias: float32 [4096], replicated, may hold values from -3 to 3
- a_log: float32 [16, 4096], replicated, may hold values from -4.6 to 1
- d_skip: float32 [4096], replicated, may hold values from 0.5 to 1.5
- in_master: float32 [2048, 3, 8192], P('dp', None, 'wide'), may hold values from -0.125 to 0.125
- xproj_master: float32 [160, 3, 4096], P('dp', None, 'wide'), may hold values from -0.09375 to 0.09375
- dtproj_master: float32 [128, 3, 4096], P('dp', None, 'wide'), may hold values from -0.5 to 0.5
- dt_bias: float32 [3, 4096], P(None, 'wide'), may hold values from -7 to -2
- out_master: float32 [2048, 3, 4096], P('dp', None, 'wide'), may hold values from -0.375 to 0.375
- cotangent: float32 [4096, 2048], P(('dp', 'wide')), may hold values from -6 to 6
Outputs:
- out: float32 [4096, 2048], P(('dp', 'wide'))
- x_grad: float32 [4096, 2048], P(('dp', 'wide'))
- norm_gain_grad: float32 [2048], replicated
- conv_weight_grad: float32 [4, 4096], replicated
- conv_bias_grad: float32 [4096], replicated
- a_log_grad: float32 [16, 4096], replicated
- d_skip_grad: float32 [4096], replicated
- in_grad: float32 [2048, 3, 8192], P('dp', None, 'wide')
- xproj_grad: float32 [160, 3, 4096], P('dp', None, 'wide')
- dtproj_grad: float32 [128, 3, 4096], P('dp', None, 'wide')
- dt_bias_grad: float32 [3, 4096], P(None, 'wide')
- out_grad: float32 [2048, 3, 4096], P('dp', None, 'wide')
Inputs may be any that keep to these rules, and one draw needn't show every extreme that they name: Row r gives, in order, the lengths of the 4 sequences that fill group r of 1024 positions from its start; fewer than 17 positions at the group's end are padding. In each row one sequence, at a slot drawn from the seed, starts within the first 128 positions and ends within the last 128; each other sequence has at most 32 positions. In each block of 128 positions that one device holds, at most 64 live positions have modality 1 and at most 64 have modality 2; padding positions have modality 0. In every draw, for one index along dp, every device along wide has exactly 64 live positions of modality 1.
All inputs are finite; a program needn't handle non-finite values.
Results may differ from a plain program's by a relative error of at most 0.012.
The roundings to bfloat16 on the way count: a program that leaves them out, or rounds other values in their place, can miss the bound.
Values may be sent and summed in bfloat16 or wider, within the bound.
A program may use at most 384 MiB of HBM per device.

v0:
```python
import jax
import jax.numpy as jnp
from jax import lax
from jax.sharding import PartitionSpec as P

INNER = 4096
STATE = 16
DT_RANK = 128
SCAN_BLOCK = 32


EPSILON = 1e-05


def from_behind(block, axis, distance):
    devices = range(lax.axis_size(axis))
    route = [(i - distance, i) for i in devices if i - distance in devices]
    return lax.ppermute(block, axis, route)


def prefix(shard, axis, combine, identity, reverse):
    peers, place = (lax.axis_size(axis), lax.axis_index(axis))
    everything = jax.tree.map(lambda part: lax.all_gather(part, axis), shard)
    start = jax.tree.map(
        lambda part, zero: jnp.broadcast_to(jnp.asarray(zero, part.dtype), part.shape),
        shard,
        identity,
    )

    def hop(k, before):
        at = peers - 1 - k if reverse else k
        reached = at > place if reverse else at < place
        new = combine(before, jax.tree.map(lambda part: part[at], everything))
        return jax.tree.map(lambda a, b: jnp.where(reached, a, b), new, before)

    return lax.fori_loop(0, peers, hop, start)


def for_sending(shard):
    return jax.tree.map(lambda a: a.astype(jnp.bfloat16) if a.dtype == jnp.float32 else a, shard)


def group_sizes(wide):
    return (wide // 2, wide // 4, wide // 4)


def spread_master(master, wide):
    first, second, third = group_sizes(wide)
    height = master.shape[0]
    columns = master.shape[2]
    parts = []
    for index, repeat in ((0, first), (1, second), (2, third)):
        parts.append(jnp.broadcast_to(master[:, index : index + 1, :], (height, repeat, columns)))
    return jnp.concatenate(parts, axis=1).reshape(height, wide * columns)


def collect_groups(received, wide):
    first, second, third = group_sizes(wide)
    height = received.shape[0]
    blocks = received.reshape(height, wide, received.shape[1] // wide)
    return jnp.stack(
        [
            jnp.sum(blocks[:, :first], axis=1),
            jnp.sum(blocks[:, first : first + second], axis=1),
            jnp.sum(blocks[:, first + second :], axis=1),
        ],
        axis=1,
    )


def plan_routes(modality, living, wide, capacity):
    count = modality.shape[0]
    first, second, third = group_sizes(wide)
    places = jnp.arange(count, dtype=jnp.int32)
    member = (
        (modality[:, None] == jnp.arange(3, dtype=jnp.int32)[None, :]) & living[:, None]
    ).astype(jnp.int32)
    before = jnp.cumsum(member, axis=0) - member
    ordinal = jnp.sum(before * member, axis=1)
    group = jnp.sum(member * jnp.array((first, second, third), jnp.int32)[None, :], axis=1)
    offset = jnp.sum(member * jnp.array((0, first, first + second), jnp.int32)[None, :], axis=1)
    group = jnp.maximum(group, 1)
    slots = wide * capacity
    target = (offset + ordinal % group) * capacity + ordinal // group
    target = jnp.where(living, target, slots)
    source = jnp.full((slots,), count, jnp.int32).at[target].set(places, mode="drop")
    return (living, jnp.minimum(target, slots - 1), source)


def pack_rows(values, source):
    count = values.shape[0]
    picked = jnp.take(values, jnp.minimum(source, count - 1), axis=0)
    return jnp.where((source < count)[:, None], picked, jnp.zeros((), values.dtype))


def unpack_rows(buffer, target, living):
    picked = jnp.take(buffer, target, axis=0)
    return jnp.where(living[:, None], picked, jnp.zeros((), buffer.dtype))


def swap_rows(values):
    return lax.all_to_all(values, "wide", split_axis=0, concat_axis=0, tiled=True)


def to_owner(values, route):
    return swap_rows(pack_rows(values, route[2]))


def to_home(values, route):
    return unpack_rows(swap_rows(values), route[1], route[0])


def swap_rates(steps, maps):
    return (
        lax.all_to_all(steps, "wide", split_axis=0, concat_axis=0, tiled=True),
        lax.all_to_all(maps, "wide", split_axis=0, concat_axis=0, tiled=True),
    )


def rates_home(steps, maps, route):
    steps_back, maps_back = swap_rates(steps, maps)
    return (unpack_rows(steps_back, route[1], route[0]), unpack_rows(maps_back, route[1], route[0]))


def rates_owner(steps, maps, route):
    return swap_rates(pack_rows(steps, route[2]), pack_rows(maps, route[2]))


def contract(left, right, left_dim, right_dim):
    return lax.dot_general(
        left, right, (((left_dim,), (right_dim,)), ((), ())), preferred_element_type=jnp.float32
    )


def segment_of(places, bounds):
    return jnp.sum((places[:, None] >= bounds[None, :]).astype(jnp.int32), axis=1)


def conv_masks(places, bounds, width):
    segment = segment_of(places, bounds)
    masks = []
    for offset in range(width):
        masks.append(
            ((places >= offset) & (segment_of(places - offset, bounds) == segment)).astype(
                jnp.float32
            )
        )
    return masks


def silu_slope(values):
    sigma = jax.nn.sigmoid(values)
    return sigma * (1.0 + values * (1.0 - sigma))


def combine(earlier, later):
    return (earlier[0] * later[0], later[0] * earlier[1] + later[1])


def step_decay(step_row, kept, a_neg):
    return jnp.exp(step_row[None, :] * a_neg) * kept


def blocked(values):
    blocks = values.shape[0] // SCAN_BLOCK
    return values.reshape((blocks, SCAN_BLOCK) + values.shape[1:])


def scan_end(delta, inputs, b_rows, keep, a_neg):

    def one_block(carry, pieces):
        step_size, value, b_part, kept = pieces
        state = carry
        for position in range(SCAN_BLOCK):
            state = (
                step_decay(step_size[position], kept[position], a_neg) * state
                + b_part[position][:, None] * (step_size[position] * value[position])[None, :]
            )
        return (state, None)

    start = jnp.zeros((a_neg.shape[0], delta.shape[1]), jnp.float32)
    final, _ = lax.scan(
        one_block, start, (blocked(delta), blocked(inputs), blocked(b_rows), blocked(keep))
    )
    return final


def scan_forward(delta, inputs, b_rows, c_rows, keep, a_neg, d_skip, start):
    count, inner = delta.shape

    def one_block(carry, pieces):
        step_size, value, b_part, c_part, kept = pieces
        state = carry
        outputs = []
        for position in range(SCAN_BLOCK):
            state = (
                step_decay(step_size[position], kept[position], a_neg) * state
                + b_part[position][:, None] * (step_size[position] * value[position])[None, :]
            )
            outputs.append(
                jnp.sum(c_part[position][:, None] * state, axis=0) + d_skip * value[position]
            )
        return (state, (carry, jnp.stack(outputs, axis=0)))

    _, (heads, results) = lax.scan(
        one_block,
        start,
        (blocked(delta), blocked(inputs), blocked(b_rows), blocked(c_rows), blocked(keep)),
    )
    return (heads, results.reshape(count, inner))


def back_end(delta, c_rows, keep, a_neg, d_out):

    def one_block(carry, pieces):
        step_size, c_part, kept, d_part = pieces
        running = carry
        for position in range(SCAN_BLOCK - 1, -1, -1):
            running = c_part[position][:, None] * d_part[position][None, :] + running
            running = step_decay(step_size[position], kept[position], a_neg) * running
        return (running, None)

    start = jnp.zeros((a_neg.shape[0], delta.shape[1]), jnp.float32)
    final, _ = lax.scan(
        one_block,
        start,
        (blocked(delta), blocked(c_rows), blocked(keep), blocked(d_out)),
        reverse=True,
    )
    return final


def scan_backward(delta, inputs, b_rows, c_rows, keep, a_neg, d_skip, heads, d_out, start):
    count, inner = delta.shape

    def one_block(carry, pieces):
        step_size, value, b_part, c_part, kept, head_state, d_part = pieces
        states = [head_state]
        decays = []
        state = head_state
        for position in range(SCAN_BLOCK):
            decay = step_decay(step_size[position], kept[position], a_neg)
            state = (
                decay * state
                + b_part[position][:, None] * (step_size[position] * value[position])[None, :]
            )
            decays.append(decay)
            states.append(state)
        running = carry
        aneg_sum = jnp.zeros_like(head_state)
        d_steps, d_bs, d_cs, d_values, skip_rows = ([], [], [], [], [])
        for position in range(SCAN_BLOCK - 1, -1, -1):
            d_row = d_part[position]
            d_state = c_part[position][:, None] * d_row[None, :] + running
            weighted = d_state * states[position] * decays[position]
            d_steps.append(
                jnp.sum(
                    weighted * a_neg
                    + d_state * b_part[position][:, None] * value[position][None, :],
                    axis=0,
                )
            )
            aneg_sum = aneg_sum + weighted * step_size[position][None, :]
            d_bs.append(jnp.sum(d_state * (step_size[position] * value[position])[None, :], axis=1))
            d_values.append(
                jnp.sum(d_state * b_part[position][:, None], axis=0) * step_size[position]
                + d_row * d_skip
            )
            d_cs.append(jnp.sum(d_row[None, :] * states[position + 1], axis=1))
            skip_rows.append(d_row * value[position])
            running = decays[position] * d_state
        d_step = jnp.stack(d_steps[::-1], axis=0)
        d_b = jnp.stack(d_bs[::-1], axis=0)
        d_c = jnp.stack(d_cs[::-1], axis=0)
        d_value = jnp.stack(d_values[::-1], axis=0)
        d_skip_part = jnp.sum(jnp.stack(skip_rows, axis=0), axis=0)
        return (running, (d_step, d_b, d_c, d_value, aneg_sum, d_skip_part))

    _, (d_step, d_b, d_c, d_value, d_aneg, d_skip_part) = lax.scan(
        one_block,
        start,
        (
            blocked(delta),
            blocked(inputs),
            blocked(b_rows),
            blocked(c_rows),
            blocked(keep),
            heads,
            blocked(d_out),
        ),
        reverse=True,
    )
    return (
        d_step.reshape(count, inner),
        d_b.reshape(count, -1),
        d_c.reshape(count, -1),
        d_value.reshape(count, inner),
        jnp.sum(d_aneg, axis=0),
        jnp.sum(d_skip_part, axis=0),
    )


def body(
    x_in,
    lengths,
    modality,
    norm_gain,
    conv_weight,
    conv_bias,
    a_log,
    d_skip,
    in_master,
    xproj_master,
    dtproj_master,
    dt_bias,
    out_master,
    cotangent,
):
    wide = lax.axis_size("wide")
    count = x_in.shape[0]
    capacity = 2 * count // wide
    first, second, third = group_sizes(wide)
    where_wide = lax.axis_index("wide")
    width = conv_weight.shape[0]
    start_place = where_wide * count
    places = start_place + jnp.arange(count, dtype=jnp.int32)
    bounds = jnp.cumsum(lengths.reshape(-1))
    living = places < bounds[-1]
    masks = conv_masks(places, bounds, width)
    keep = masks[1]
    full_rows = (
        lax.all_gather(in_master.astype(jnp.bfloat16), "dp", axis=0, tiled=True),
        lax.all_gather(xproj_master.astype(jnp.bfloat16), "dp", axis=0, tiled=True),
        lax.all_gather(dtproj_master.astype(jnp.bfloat16), "dp", axis=0, tiled=True),
        lax.all_gather(out_master.astype(jnp.bfloat16), "dp", axis=0, tiled=True),
    )
    scale = lax.rsqrt(jnp.mean(x_in * x_in, axis=1, keepdims=True) + EPSILON)
    normed = (x_in * scale * norm_gain[None, :]).astype(jnp.bfloat16)
    own = (where_wide >= first).astype(jnp.int32) + (where_wide >= first + second).astype(jnp.int32)
    bias_row = spread_master(dt_bias.astype(jnp.bfloat16)[None], wide)
    w_in, w_x, w_dt, w_out, bias_own = (
        lax.all_to_all(
            spread_master(full_rows[0], wide), "wide", split_axis=1, concat_axis=1, tiled=True
        ),
        lax.all_to_all(
            spread_master(full_rows[1], wide), "wide", split_axis=1, concat_axis=1, tiled=True
        ),
        lax.all_to_all(
            spread_master(full_rows[2], wide), "wide", split_axis=1, concat_axis=1, tiled=True
        ),
        lax.all_to_all(
            spread_master(full_rows[3], wide), "wide", split_axis=1, concat_axis=1, tiled=True
        ),
        lax.all_to_all(bias_row, "wide", split_axis=1, concat_axis=1, tiled=True),
    )
    route = plan_routes(modality, living, wide, capacity)
    normed_owner = to_owner(normed, route)
    mixed = to_home(
        jnp.dot(normed_owner, w_in, preferred_element_type=jnp.float32).astype(jnp.bfloat16), route
    )
    xs_part = mixed[:, :INNER].astype(jnp.float32)
    z_part = mixed[:, INNER:].astype(jnp.float32)
    tail_rows = from_behind(mixed[count - (width - 1) :, :INNER], "wide", 1)
    extended = jnp.concatenate([tail_rows.astype(jnp.float32), xs_part], axis=0)
    pre = conv_bias[None, :]
    for offset in range(width):
        begin = width - 1 - offset
        pre = (
            pre
            + conv_weight[width - 1 - offset][None, :]
            * extended[begin : begin + count]
            * masks[offset][:, None]
        )
    inner_low = jax.nn.silu(pre).astype(jnp.bfloat16)
    inner = inner_low.astype(jnp.float32)
    inner_owner = to_owner(inner_low, route)
    proj = contract(inner_owner, w_x, 1, 1)
    rates_low = proj[:, :DT_RANK].astype(jnp.bfloat16)
    maps_low = proj[:, DT_RANK:].astype(jnp.bfloat16)
    steps_low = (
        jnp.dot(rates_low, w_dt, preferred_element_type=jnp.float32) + bias_own.astype(jnp.float32)
    ).astype(jnp.bfloat16)
    steps_home, maps_home = rates_home(steps_low, maps_low, route)
    steps_value = steps_home.astype(jnp.float32)
    delta = jax.nn.softplus(steps_value)
    b_rows = maps_home[:, :STATE].astype(jnp.float32)
    c_rows = maps_home[:, STATE:].astype(jnp.float32)
    a_neg = -jnp.exp(a_log)
    decay_total = jnp.exp(a_neg * jnp.sum(delta, axis=0)[None, :]) * jnp.min(keep)
    end_state = scan_end(delta, inner, b_rows, keep, a_neg)
    carried = prefix(
        (decay_total, end_state),
        "wide",
        combine,
        (jnp.ones_like(decay_total), jnp.zeros_like(end_state)),
        False,
    )
    heads, y_value = scan_forward(delta, inner, b_rows, c_rows, keep, a_neg, d_skip, carried[1])
    gate = jax.nn.silu(z_part)
    gated_low = (y_value * gate).astype(jnp.bfloat16)
    gated_owner = to_owner(gated_low, route)
    branch = to_home(contract(gated_owner, w_out, 1, 1).astype(jnp.bfloat16), route)
    result = x_in + jnp.where(living[:, None], branch.astype(jnp.float32), 0.0)
    d_branch = jnp.where(living[:, None], cotangent, 0.0).astype(jnp.bfloat16)
    back_owner = to_owner(d_branch, route)
    grad_out = contract(back_owner, gated_owner, 0, 0)
    d_gated = to_home(
        jnp.dot(back_owner, w_out, preferred_element_type=jnp.float32).astype(jnp.bfloat16), route
    ).astype(jnp.float32)
    d_y = d_gated * gate
    d_z = d_gated * y_value * silu_slope(z_part)
    back_value = back_end(delta, c_rows, keep, a_neg, d_y)
    carried_back = prefix(
        (decay_total, back_value),
        "wide",
        combine,
        (jnp.ones_like(decay_total), jnp.zeros_like(back_value)),
        True,
    )
    d_delta, d_b, d_c, d_scan, d_aneg, skip_grad = scan_backward(
        delta, inner, b_rows, c_rows, keep, a_neg, d_skip, heads, d_y, carried_back[1]
    )
    d_steps_low = jnp.where(living[:, None], d_delta * jax.nn.sigmoid(steps_value), 0.0).astype(
        jnp.bfloat16
    )
    d_maps_low = jnp.where(living[:, None], jnp.concatenate([d_b, d_c], axis=1), 0.0).astype(
        jnp.bfloat16
    )
    steps_owner, maps_owner = rates_owner(d_steps_low, d_maps_low, route)
    grad_dt = contract(rates_low, steps_owner, 0, 0)
    bias_sum = jnp.sum(steps_owner.astype(jnp.float32), axis=0)
    d_rates = contract(steps_owner, w_dt, 1, 1)
    d_proj = jnp.concatenate([d_rates.astype(jnp.bfloat16), maps_owner], axis=1)
    grad_x = contract(d_proj, inner_owner, 0, 0)
    d_inner = (
        to_home(
            jnp.dot(d_proj, w_x, preferred_element_type=jnp.float32).astype(jnp.bfloat16), route
        ).astype(jnp.float32)
        + d_scan
    )
    bias_table = jnp.where((jnp.arange(3, dtype=jnp.int32) == own)[:, None], bias_sum[None, :], 0.0)
    d_pre = d_inner * silu_slope(pre)
    head_rows = from_behind(for_sending(d_pre[: width - 1]), "wide", -1)
    further = jnp.concatenate([d_pre, head_rows], axis=0)
    later_places = start_place + jnp.arange(count + width - 1, dtype=jnp.int32)
    later_masks = conv_masks(later_places, bounds, width)
    conv_rows = []
    d_xs = jnp.zeros_like(xs_part)
    for offset in range(width):
        begin = width - 1 - offset
        conv_rows.append(
            jnp.sum(d_pre * masks[offset][:, None] * extended[begin : begin + count], axis=0)
        )
        masked = further * later_masks[offset][:, None]
        d_xs = d_xs + conv_weight[width - 1 - offset][None, :] * masked[offset : offset + count]
    conv_grad = jnp.stack(conv_rows[::-1], axis=0)
    conv_bias_part = jnp.sum(d_pre, axis=0)
    d_mixed = jnp.where(living[:, None], jnp.concatenate([d_xs, d_z], axis=1), 0.0).astype(
        jnp.bfloat16
    )
    mixed_owner = to_owner(d_mixed, route)
    grad_in = contract(normed_owner, mixed_owner, 0, 0)
    d_normed = to_home(contract(mixed_owner, w_in, 1, 1).astype(jnp.bfloat16), route).astype(
        jnp.float32
    )
    gain_part = jnp.sum(d_normed * x_in * scale, axis=0)
    scaled_back = d_normed * norm_gain[None, :]
    x_grad = cotangent + scale * (
        scaled_back - x_in * scale * scale * jnp.mean(scaled_back * x_in, axis=1, keepdims=True)
    )
    sums = lax.psum(
        (gain_part, conv_grad, conv_bias_part, d_aneg * a_neg, skip_grad, bias_table),
        ("dp", "wide"),
    )
    columns = dt_bias.shape[1]
    bias_grad = lax.dynamic_slice_in_dim(sums[5], where_wide * columns, columns, 1)
    returned = (
        lax.all_to_all(grad_in, "wide", split_axis=1, concat_axis=1, tiled=True),
        lax.all_to_all(grad_x, "wide", split_axis=1, concat_axis=1, tiled=True),
        lax.all_to_all(grad_dt, "wide", split_axis=1, concat_axis=1, tiled=True),
        lax.all_to_all(grad_out, "wide", split_axis=1, concat_axis=1, tiled=True),
    )
    tables = (
        collect_groups(returned[0], wide),
        collect_groups(returned[1], wide),
        collect_groups(returned[2], wide),
        collect_groups(returned[3], wide),
    )
    in_grad, xproj_grad, dtproj_grad, out_grad = (
        lax.psum_scatter(tables[0], "dp", scatter_dimension=0, tiled=True),
        lax.psum_scatter(tables[1], "dp", scatter_dimension=0, tiled=True),
        lax.psum_scatter(tables[2], "dp", scatter_dimension=0, tiled=True),
        lax.psum_scatter(tables[3], "dp", scatter_dimension=0, tiled=True),
    )
    return (
        result,
        x_grad,
        sums[0],
        sums[1],
        sums[2],
        sums[3],
        sums[4],
        in_grad,
        xproj_grad,
        dtproj_grad,
        bias_grad,
        out_grad,
    )


def solution(mesh):
    in_specs = (
        P(("dp", "wide"), None),
        P("dp", None),
        P(("dp", "wide")),
        P(),
        P(),
        P(),
        P(),
        P(),
        P("dp", None, "wide"),
        P("dp", None, "wide"),
        P("dp", None, "wide"),
        P(None, "wide"),
        P("dp", None, "wide"),
        P(("dp", "wide"), None),
    )
    out_specs = (
        P(("dp", "wide"), None),
        P(("dp", "wide"), None),
        P(),
        P(),
        P(),
        P(),
        P(),
        P("dp", None, "wide"),
        P("dp", None, "wide"),
        P("dp", None, "wide"),
        P(None, "wide"),
        P("dp", None, "wide"),
    )
    return jax.shard_map(body, mesh=mesh, in_specs=in_specs, out_specs=out_specs, check_vma=False)
```

profile of v0, /device:TPU:0, one launch (start us, length us, event | category | flops | bytes accessed | tf_op | source)
XLA Modules:
  0.0 6019.4 jit_solution(7257909985722321231)
XLA Ops:
  47.1 21.6 all-to-all-done.5
  72.3 27.0 all-gather.9.cloned.1.call-done
  99.3 9.1 slice_bitcast_fusion.2
  133.2 23.1 pad_maximum_fusion
  176.1 711.3 %all-to-all-done.1 = bf16[2048,8,1024]{2,0,1:T(8,128)(2,1)} async-done(((bf16[2048,8,1024]{2,0,1:T(8,128)(2,1)}), bf16[2048,8,1024]{2,0,1:T(8,128)(2,1)}, u32[]{:S(2)}, u32[]{:S(2)}) %all-to-all-start.1) | async-done | bytes 33554464 | tf_op jit(solution)/shard_map/all_to_all | solution.py:342
  891.4 42.2 copy.74
  933.7 16.7 convolution_convert_fusion
  966.9 11.7 pad_maximum_fusion.2
  978.6 71.8 %all-to-all-done.2 = bf16[8,32,8192]{2,1,0:T(8,128)(2,1)} async-done(((bf16[8,32,8192]{2,1,0:T(8,128)(2,1)}), bf16[8,32,8192]{2,1,0:T(8,128)(2,1)}, u32[]{:S(2)}, u32[]{:S(2)}) %all-to-all-start.2) | async-done | bytes 4194336 | tf_op jit(solution)/shard_map/all_to_all | solution.py:102
  1068.9 122.8 %collective-permute-done = bf16[3,4096]{1,0:T(4,128)(2,1)S(1)} collective-permute-done((bf16[3,4096]{1,0:T(4,128)(2,1)S(1)}, bf16[3,4096]{1,0:T(4,128)(2,1)S(1)}, u32[]{:S(2)}, u32[]{:S(2)}) %collective-permute-start) | collective-permute-done | bytes 24608 | tf_op jit(solution)/shard_map/ppermute | solution.py:18
  1198.2 219.5 %all-to-all-done.10 = bf16[2048,8,512]{2,0,1:T(8,128)(2,1)} async-done(((bf16[2048,8,512]{2,0,1:T(8,128)(2,1)}), bf16[2048,8,512]{2,0,1:T(8,128)(2,1)}, u32[]{:S(2)}, u32[]{:S(2)}) %all-to-all-start.10) | async-done | bytes 16777248 | tf_op jit(solution)/shard_map/all_to_all | solution.py:351
  1417.7 9.8 all-to-all-start.3
  1427.5 21.6 copy.79
  1449.1 11.9 convolution_convert_fusion.2
  1461.0 14.0 all-to-all-done.3
  1486.0 42.4 all-to-all-done.13
  1554.2 36.0 all-to-all-done.7
  1602.3 130.0 %while.98 = (s32[]{:T(128)}, f32[16,4096]{1,0:T(8,128)S(1)}, f32[4,32,4096]{2,1,0:T(8,128)S(1)}, f32[16,4096]{1,0:T(8,128)S(1)}, f32[4,32]{1,0:T(4,128)}, /*inde...) while((s32[]{:T(128)}, f32[16,4096]{1,0:T(8,128)S(1)}, ...), condition=%wide.region_14.18_spmd.clone, body=%wide.region_13.17_spmd.clone.sunk | while | flops 10682402 | bytes 5512939 | solution.py:182
  1612.0 22.8 multiply_add_fusion.138
  1644.8 22.8 multiply_add_fusion.138
  1677.1 22.8 multiply_add_fusion.138
  1709.5 22.8 multiply_add_fusion.138
  1733.4 129.0 %while.100 = (s32[]{:T(128)}, f32[16,4096]{1,0:T(8,128)S(1)}, f32[4,32,4096]{2,1,0:T(8,128)S(1)}, f32[16,4096]{1,0:T(8,128)S(1)}, f32[4,32]{1,0:T(4,128)}, /*ind...) while((s32[]{:T(128)}, f32[16,4096]{1,0:T(8,128)S(1)}, ...), condition=%wide.region_52.57_spmd.clone, body=%wide.region_51.56_spmd.clone.sunk | while | flops 10551331 | bytes 3940035 | solution.py:224
  1742.8 22.8 add_multiply_fusion.2
  1775.1 22.7 add_multiply_fusion.2
  1807.4 22.7 add_multiply_fusion.2
  1839.7 22.7 add_multiply_fusion.2
  1863.2 10.2 while.99
  1876.2 221.3 %while.96 = (s32[]{:T(128)}, f32[16,4096]{1,0:T(8,128)S(1)}, f32[4,16,4096]{2,1,0:T(8,128)}, f32[4,32,4096]{2,1,0:T(8,128)}, f32[4,32,4096]{2,1,0:T(8,128)S(1)},...) while((s32[]{:T(128)}, f32[16,4096]{1,0:T(8,128)S(1)}, ...), condition=%wide.region_50.54_spmd, body=%wide.region_17.53_spmd.sunk | while | flops 20185120 | bytes 22100880 | solution.py:205
  1888.3 22.9 multiply_reduce_fusion.159
  1943.8 22.9 multiply_reduce_fusion.159
  1998.9 22.9 multiply_reduce_fusion.159
  2053.9 22.9 multiply_reduce_fusion.159
  2097.5 10.2 while.101
  2113.7 738.0 %while.97 = (s32[]{:T(128)}, f32[16,4096]{1,0:T(8,128)S(1)}, f32[4,32,4096]{2,1,0:T(8,128)}, bf16[4,32,16]{2,1,0:T(8,128)(2,1)}, bf16[4,32,16]{2,1,0:T(8,128)(2,...) while((s32[]{:T(128)}, f32[16,4096]{1,0:T(8,128)S(1)}, ...), condition=%wide.region_184.189_spmd, body=%wide.region_55.188_spmd.sunk | while | flops 80014368 | bytes 59352932 | solution.py:279
  2148.9 28.4 bitcast_dynamic-update-slice_fusion.11
  2331.2 28.5 bitcast_dynamic-update-slice_fusion.11
  2514.1 28.4 bitcast_dynamic-update-slice_fusion.11
  2696.6 28.4 bitcast_dynamic-update-slice_fusion.11
  2870.6 47.0 all-to-all-done.14
  2934.0 40.6 all-to-all-done.16
  3004.9 22.2 all-to-all-done.21
  3045.1 45.3 all-to-all-done.20
  3098.5 89.0 %all-to-all-done.17 = bf16[8,32,8192]{2,1,0:T(8,128)(2,1)} async-done(((bf16[8,32,8192]{2,1,0:T(8,128)(2,1)}), bf16[8,32,8192]{2,1,0:T(8,128)(2,1)}, u32[]{:S(2)}, u32[]{:S(2)}) %all-to-all-start.17) | async-done | bytes 4194336 | tf_op jit(solution)/shard_map/all_to_all | solution.py:102
  3191.1 17.0 convolution_convert_fusion.3
  3208.1 31.4 all-to-all-done.9
  3246.9 14.6 fusion.423
  3283.0 25.5 fusion.422
  3308.5 689.7 %all-to-all-done.22 = f32[2048,8,512]{2,0,1:T(8,128)} async-done(((f32[2048,8,512]{2,0,1:T(8,128)}), f32[2048,8,512]{2,0,1:T(8,128)}, u32[]{:S(2)}, u32[]{:S(2)}) %all-to-all-start.22) | async-done | bytes 33554464 | tf_op jit(solution)/shard_map/all_to_all | solution.py:481
  3998.3 9.8 all-to-all-start.19
  4023.9 11.2 slice_reduce_fusion.5
  4035.1 10.3 slice_reduce_fusion.1
  4045.4 10.7 pad_maximum_fusion.3
  4056.2 1393.0 %all-to-all-done.19 = f32[2048,8,1024]{2,0,1:T(8,128)} async-done(((f32[2048,8,1024]{2,0,1:T(8,128)}), f32[2048,8,1024]{2,0,1:T(8,128)}, u32[]{:S(2)}, u32[]{:S(2)}) %all-to-all-start.19) | async-done | bytes 67108896 | tf_op jit(solution)/shard_map/all_to_all | solution.py:478
  5449.2 18.9 slice_reduce_fusion.3
  5468.2 16.5 slice_reduce_fusion
  5484.6 17.9 pad_maximum_fusion.1
  5502.6 12.0 convolution_convert_fusion.4
  5518.7 26.1 all-to-all-done.11
  5550.6 113.7 %all-reduce.7.cloned.1.call-done = (f32[4,4096]{1,0:T(4,128)}, f32[16,4096]{1,0:T(8,128)}) async-done(((f32[4,4096]{1,0:T(4,128)}, f32[16,4096]{1,0:T(8,128)}), (f32[4,4096]{1,0:T(4,128)}, f32[16,4096]{1,0:T(8,128)})) %all-reduce.7.cloned.1.call-update) | async-done | bytes 327696 | tf_op jit(solution)/shard_map/psum | solution.py:471
  5664.3 27.5 reduce-scatter.9.cloned.1.call-done
  5691.8 27.7 reduce-scatter.7.cloned.1.call-done
  5719.5 102.3 %reduce-scatter.11.cloned.1.call-done = f32[512,3,512]{2,0,1:T(8,128)} async-done(((f32[2048,3,512]{2,0,1:T(8,128)}), f32[512,3,512]{2,0,1:T(8,128)}) %reduce-scatter.11.cloned.1.call-update) | async-done | bytes 3145744 | tf_op jit(solution)/shard_map/reduce_scatter | solution.py:493
  5821.8 183.8 %reduce-scatter.5.cloned.1.call-done = f32[512,3,1024]{2,0,1:T(8,128)} async-done(((f32[2048,3,1024]{2,0,1:T(8,128)}), f32[512,3,1024]{2,0,1:T(8,128)}) %reduce-scatter.5.cloned.1.call-update) | async-done | bytes 6291472 | tf_op jit(solution)/shard_map/reduce_scatter | solution.py:490
  (2799 shorter events, 1178.6 us)
Async XLA Ops:
  7.2 92.1 %all-gather.9.cloned.1.call-start = ((), (), s32[]{:S(2)}) async-start(), calls=%async_computation.27 | async-start | bytes 15728640 | tf_op jit(solution)/shard_map/all_gather | solution.py:332
  14.8 21.5 all-to-all-start.6
  22.3 1033.9 %copy-start.282 = (s32[4,1]{0,1:T(1,128)}, s32[4,1]{0,1:T(1,128)S(1)}, u32[]{:S(2)}) copy-start(s32[4,1]{0,1:T(1,128)S(1)} %reduce-window.4) | copy-start | bytes 52
  23.5 1571.7 %copy-start.229 = (pred[128]{0:T(512)(128)(4,1)}, pred[128]{0:T(512)(128)(4,1)S(1)}, u32[]{:S(2)}) copy-start(pred[128]{0:T(512)(128)(4,1)S(1)} %broadcast_compare_fusion.1) | copy-start | bytes 388
  36.3 32.4 all-to-all-start.5
  42.4 1152.3 %copy-start.255 = (s32[1024]{0:T(1024)}, s32[1024]{0:T(1024)S(1)}, u32[]{:S(2)}) copy-start(s32[1024]{0:T(1024)S(1)} %pad_clamp_fusion.2) | copy-start | bytes 12292
  45.4 1497.8 %copy-start.259 = (pred[256]{0:T(512)(128)(4,1)}, pred[256]{0:T(512)(128)(4,1)S(1)}, u32[]{:S(2)}) copy-start(pred[256]{0:T(512)(128)(4,1)S(1)} %get-tuple-element.1996) | copy-start | bytes 772
  45.5 1498.4 %copy-start.262 = (pred[256]{0:T(512)(128)(4,1)}, pred[256]{0:T(512)(128)(4,1)S(1)}, u32[]{:S(2)}) copy-start(pred[256]{0:T(512)(128)(4,1)S(1)} %get-tuple-element.1997) | copy-start | bytes 772
  68.7 39.7 all-to-all-start
  108.4 825.3 %copy-start.77 = (bf16[8,32,2048]{2,1,0:T(8,128)(2,1)}, bf16[8,32,2048]{2,1,0:T(8,128)(2,1)S(1)}, u32[]{:S(2)}) copy-start(bf16[8,32,2048]{2,1,0:T(8,128)(2,1)S(1)} %all-to-all-done) | copy-start | bytes 3145732
  108.4 48.0 all-to-all-start.12
  157.4 730.0 %all-to-all-start.1 = ((bf16[2048,8,1024]{2,0,1:T(8,128)(2,1)}), bf16[2048,8,1024]{2,0,1:T(8,128)(2,1)}, u32[]{:S(2)}, u32[]{:S(2)}) async-start(bf16[2048,8,1024]{2,0,1:T(8,128)(2,1)} %pad_maximum_fusion), calls=%async_computation.1 | async-start | bytes 67108864 | tf_op jit(solution)/shard_map/all_to_all | solution.py:342
  164.6 792.9 %all-gather.11.cloned.1.call-start = ((), (), s32[]{:S(2)}) async-start(), calls=%async_computation.28 | async-start | bytes 7864320 | tf_op jit(solution)/shard_map/all_gather | solution.py:335
  887.3 63.1 %all-to-all-start.4 = ((bf16[160,8,512]{2,0,1:T(8,128)(2,1)}), bf16[160,8,512]{2,0,1:T(8,128)(2,1)S(1)}, u32[]{:S(2)}, u32[]{:S(2)}) async-start(bf16[160,8,512]{2,0,1:T(8,128)(2,1)} %pad_maximum_fusion.6), calls=%async_computation.4 | async-start | bytes 2621440 | tf_op jit(solution)/shard_map/all_to_all | solution.py:345
  951.5 98.9 %all-to-all-start.2 = ((bf16[8,32,8192]{2,1,0:T(8,128)(2,1)}), bf16[8,32,8192]{2,1,0:T(8,128)(2,1)}, u32[]{:S(2)}, u32[]{:S(2)}) async-start(bf16[8,32,8192]{2,1,0:T(8,128)(2,1)} %bitcast.3516), calls=%async_computation.2 | async-start | bytes 8388608 | tf_op jit(solution)/shard_map/all_to_all | solution.py:102
  978.6 79.1 %copy-start.235 = (f32[4,4096]{1,0:T(4,128)S(1)}, f32[4,4096]{1,0:T(4,128)}, u32[]{:S(2)}) copy-start(f32[4,4096]{1,0:T(4,128)} %param.40) | copy-start | bytes 196612
  1050.4 367.3 %all-to-all-start.10 = ((bf16[2048,8,512]{2,0,1:T(8,128)(2,1)}), bf16[2048,8,512]{2,0,1:T(8,128)(2,1)}, u32[]{:S(2)}, u32[]{:S(2)}) async-start(bf16[2048,8,512]{2,0,1:T(8,128)(2,1)} %pad_maximum_fusion.2), calls=%async_computation.10 | async-start | bytes 33554432 | tf_op jit(solution)/shard_map/all_to_all | solution.py:351
  1056.9 134.8 %copy-start.273 = (f32[128]{0:T(128)}, f32[128]{0:T(128)S(1)}, u32[]{:S(2)}) copy-start(f32[128]{0:T(128)S(1)} %get-tuple-element.1324) | copy-start | bytes 1540
  1057.7 537.6 %copy-start.251 = (pred[128]{0:T(512)(128)(4,1)}, pred[128]{0:T(512)(128)(4,1)S(1)}, u32[]{:S(2)}) copy-start(pred[128]{0:T(512)(128)(4,1)S(1)} %get-tuple-element.1319) | copy-start | bytes 388
  1057.7 134.0 %copy-start.267 = (f32[128]{0:T(128)}, f32[128]{0:T(128)S(1)}, u32[]{:S(2)}) copy-start(f32[128]{0:T(128)S(1)} %get-tuple-element.1998) | copy-start | bytes 1540
  1057.7 134.0 %copy-start.269 = (f32[128]{0:T(128)}, f32[128]{0:T(128)S(1)}, u32[]{:S(2)}) copy-start(f32[128]{0:T(128)S(1)} %get-tuple-element.1999) | copy-start | bytes 1540
  1057.7 134.0 %copy-start.271 = (f32[128]{0:T(128)}, f32[128]{0:T(128)S(1)}, u32[]{:S(2)}) copy-start(f32[128]{0:T(128)S(1)} %get-tuple-element.2000) | copy-start | bytes 1540
  1057.8 134.0 %copy-start.207 = (f32[1,4096]{1,0:T(1,128)}, f32[1,4096]{1,0:T(1,128)S(1)}, u32[]{:S(2)}) copy-start(f32[1,4096]{1,0:T(1,128)S(1)} %get-tuple-element.1984) | copy-start | bytes 49156
  1057.8 134.0 %copy-start.209 = (f32[1,4096]{1,0:T(1,128)}, f32[1,4096]{1,0:T(1,128)S(1)}, u32[]{:S(2)}) copy-start(f32[1,4096]{1,0:T(1,128)S(1)} %get-tuple-element.1985) | copy-start | bytes 49156
  1057.8 134.0 %copy-start.211 = (f32[1,4096]{1,0:T(1,128)}, f32[1,4096]{1,0:T(1,128)S(1)}, u32[]{:S(2)}) copy-start(f32[1,4096]{1,0:T(1,128)S(1)} %get-tuple-element.1986) | copy-start | bytes 49156
  1057.8 134.0 %copy-start.213 = (f32[1,4096]{1,0:T(1,128)}, f32[1,4096]{1,0:T(1,128)S(1)}, u32[]{:S(2)}) copy-start(f32[1,4096]{1,0:T(1,128)S(1)} %get-tuple-element.1987) | copy-start | bytes 49156
  1064.6 130.0 %copy-start.4 = (bf16[128,8192]{1,0:T(8,128)(2,1)}, bf16[128,8192]{1,0:T(8,128)(2,1)S(1)}, u32[]{:S(2)}) copy-start(bf16[128,8192]{1,0:T(8,128)(2,1)S(1)} %select_select_fusion.4) | copy-start | bytes 6291460
  1064.6 127.1 %copy-start.258 = (f32[4096]{0:T(1024)S(1)}, f32[4096]{0:T(1024)}, u32[]{:S(2)}) copy-start(f32[4096]{0:T(1024)} %param.41) | copy-start | bytes 49156
  1064.7 127.0 %collective-permute-start = (bf16[3,4096]{1,0:T(4,128)(2,1)S(1)}, bf16[3,4096]{1,0:T(4,128)(2,1)S(1)}, u32[]{:S(2)}, u32[]{:S(2)}) collective-permute-start(bf16[3,4096]{1,0:T(4,128)(2,1)S(1)} %slice.5223), channel_id=1, source_target_pairs={{0,1},{1,2},{2,3},{3,4},{4,5},{5,6},{6,7},{8,9},{9,10},{10,11},{11... | collective-permute-start | bytes 73736 | tf_op jit(solution)/shard_map/ppermute | solution.py:18
  1068.9 125.8 %copy-start.5 = (f32[128,4096]{1,0:T(8,128)}, f32[128,4096]{1,0:T(8,128)S(1)}, u32[]{:S(2)}) copy-start(f32[128,4096]{1,0:T(8,128)S(1)} %slice_convert_fusion) | copy-start | bytes 6291460
  1417.7 57.3 all-to-all-start.3
  1476.3 52.1 all-to-all-start.13
  1485.1 53.5 copy-start.170
  1528.4 10.2 all-to-all-start.8
  1538.6 51.6 all-to-all-start.7
  1543.0 320.2 %all-gather.13.cloned.1.call-start = ((), (), s32[]{:S(2)}) async-start(), calls=%async_computation.33 | async-start | bytes 2359296 | tf_op jit(solution)/shard_map/all_gather | solution.py:23
  1544.6 45.6 copy-start.265
  1602.3 260.9 %all-gather.15.cloned.1.call-start = ((), (), s32[]{:S(2)}) async-start(), calls=%async_computation.34 | async-start | bytes 2359296 | tf_op jit(solution)/shard_map/all_gather | solution.py:23
  1733.1 364.4 %all-gather.17.cloned.1.call-start = ((), (), s32[]{:S(2)}) async-start(), calls=%async_computation.35 | async-start | bytes 2359296 | tf_op jit(solution)/shard_map/all_gather | solution.py:23
  2331.2 37.2 copy-start.13
  2331.2 37.1 copy-start.32
  2331.2 37.1 copy-start.71
  2331.2 37.1 copy-start.177
  2856.6 10.2 all-to-all-start.15
  2866.8 50.8 all-to-all-start.14
  2870.4 50.0 copy-start.12
  2922.5 52.1 all-to-all-start.16
  2934.0 45.0 copy-start.283
  2974.6 52.5 all-to-all-start.21
  2997.9 6.9 collective-permute-start.1
  3027.1 63.2 %all-to-all-start.20 = ((f32[160,8,512]{2,0,1:T(8,128)}), f32[160,8,512]{2,0,1:T(8,128)}, u32[]{:S(2)}, u32[]{:S(2)}) async-start(f32[160,8,512]{2,0,1:T(8,128)} %fusion.383), calls=%async_computation.21 | async-start | bytes 5242880 | tf_op jit(solution)/shard_map/all_to_all | solution.py:479
  3090.4 97.1 %all-to-all-start.17 = ((bf16[8,32,8192]{2,1,0:T(8,128)(2,1)}), bf16[8,32,8192]{2,1,0:T(8,128)(2,1)}, u32[]{:S(2)}, u32[]{:S(2)}) async-start(bf16[8,32,8192]{2,1,0:T(8,128)(2,1)} %select_select_fusion), calls=%async_computation.17 | async-start | bytes 8388608 | tf_op jit(solution)/shard_map/all_to_all | solution.py:102
  3187.5 52.0 all-to-all-start.9
  3239.5 30.0 all-to-all-start.18
  3269.5 728.8 %all-to-all-start.22 = ((f32[2048,8,512]{2,0,1:T(8,128)}), f32[2048,8,512]{2,0,1:T(8,128)}, u32[]{:S(2)}, u32[]{:S(2)}) async-start(f32[2048,8,512]{2,0,1:T(8,128)} %fusion.423), calls=%async_computation.25 | async-start | bytes 67108864 | tf_op jit(solution)/shard_map/all_to_all | solution.py:481
  3308.5 701.1 %copy-start.195 = (f32[4,4096]{1,0:T(4,128)S(1)}, f32[4,4096]{1,0:T(4,128)}, u32[]{:S(2)}) copy-start(f32[4,4096]{1,0:T(4,128)} %get-tuple-element.825) | copy-start | bytes 196612
  3998.3 1451.0 %all-to-all-start.19 = ((f32[2048,8,1024]{2,0,1:T(8,128)}), f32[2048,8,1024]{2,0,1:T(8,128)}, u32[]{:S(2)}, u32[]{:S(2)}) async-start(f32[2048,8,1024]{2,0,1:T(8,128)} %fusion.422), calls=%async_computation.19 | async-start | bytes 134217728 | tf_op jit(solution)/shard_map/all_to_all | solution.py:478
  4008.1 1541.1 %all-reduce.5.cloned.1.call-start = ((), (), s32[]{:S(2)}) async-start(), calls=%async_computation.36 | async-start | bytes 212992 | tf_op jit(solution)/shard_map/psum | solution.py:471
  4015.3 1648.9 %all-reduce.7.cloned.1.call-start = ((), (), s32[]{:S(2)}) async-start(), calls=%async_computation.37 | async-start | bytes 655360 | tf_op jit(solution)/shard_map/psum | solution.py:471
  4016.1 1675.7 %reduce-scatter.9.cloned.1.call-start = ((), (), s32[]{:S(2)}) async-start(), calls=%async_computation.31 | async-start | bytes 983040 | tf_op jit(solution)/shard_map/reduce_scatter | solution.py:492
  4019.8 1699.7 %reduce-scatter.7.cloned.1.call-start = ((), (), s32[]{:S(2)}) async-start(), calls=%async_computation.30 | async-start | bytes 1228800 | tf_op jit(solution)/shard_map/reduce_scatter | solution.py:491
  4023.8 1797.9 %reduce-scatter.11.cloned.1.call-start = ((), (), s32[]{:S(2)}) async-start(), calls=%async_computation.32 | async-start | bytes 15728640 | tf_op jit(solution)/shard_map/reduce_scatter | solution.py:493
  4056.1 1949.4 %reduce-scatter.5.cloned.1.call-start = ((), (), s32[]{:S(2)}) async-start(), calls=%async_computation.29 | async-start | bytes 31457280 | tf_op jit(solution)/shard_map/reduce_scatter | solution.py:490
  5514.5 30.3 all-to-all-start.11
  (861 other events, 11923.7 us)
Sparse Core Ops, SparseCore 0:
  12.4 86.8 all-gather.8
  168.0 46.6 all-gather.10
  1602.4 47.3 all-gather.12
  1733.2 47.5 all-gather.14
  1863.3 47.3 all-gather.16
  4015.9 1510.4 all-reduce.4
  5532.4 131.8 all-reduce.6
  5667.5 24.2 reduce-scatter.8
  5695.0 24.4 reduce-scatter.6
  5722.7 99.0 reduce-scatter.10
  5825.1 180.4 reduce-scatter.4
where the time goes:
time: 6050 us; the launch traced here: 6020 us
  waiting for transfers between devices  4120 us (68%)
  other arithmetic  1160 us (19%)
  local copies, waits for them, and re-layouts  444 us (7%)
  starting transfers between devices  126 us (2%)
  matrix products  113 us (2%)
    all_to_all x1, waiting for transfers between devices, body(): lax.all_to_all(grad_in, 'wide', split_axis=1, concat_axis=1, tiled=True)  1390 us
    all_to_all x1, waiting for transfers between devices, body(): lax.all_to_all(spread_master(full_rows[0], wide), 'wide', split_axis=1, c...  711 us
    all_to_all x1, waiting for transfers between devices, body(): lax.all_to_all(grad_out, 'wide', split_axis=1, concat_axis=1, tiled=True)  690 us
    all_to_all x10, waiting for transfers between devices, swap_rows(): lax.all_to_all(values, 'wide', split_axis=0, concat_axis=0, tiled=True)  323 us
    all_to_all x1, waiting for transfers between devices, body(): lax.all_to_all(spread_master(full_rows[3], wide), 'wide', split_axis=1, c...  220 us
    reduce_sum x56, other arithmetic, one_block(): jnp.sum(weighted * a_neg + d_state * b_part[position][:, None] * value[po...  215 us
    reduce_scatter x1, waiting for transfers between devices, body(): lax.psum_scatter(tables[0], 'dp', scatter_dimension=0, tiled=True)  184 us
    reduce_sum x44, other arithmetic, one_block(): jnp.sum(c_part[position][:, None] * state, axis=0)  142 us
  transfers between devices with their start and end apart: 36, of which 27 were waited for; matrix products, arithmetic and copies ran while one was open for 16% of the time, Pallas kernels for 0%

commit v1 on v0

v1 whole, which is shorter than its diff:
```python
import jax
import jax.numpy as jnp
from jax import lax
from jax.experimental import pallas as pl
from jax.experimental.pallas import tpu as pltpu
from jax.sharding import PartitionSpec as P

F32 = jnp.float32
BF = jnp.bfloat16
INNER = 4096
STATE = 16
DT_RANK = 128
EPSILON = 1e-05


STEPS=16
HUGE=1e30

def scan_forward_kernel(dtp_ref,u_ref,b_ref,c_ref,keep_ref,alog_ref,skip_ref,z_ref, gated_ref,y_ref,heads_ref, st, dec, inj, ys, a2):
    T,C=u_ref.shape
    @pl.when(pl.program_id(0)==0)
    def _():
        st[...]=jnp.zeros_like(st)
        a2[...]=-jnp.exp(alog_ref[...])*1.4426950408889634
    delta=jax.nn.softplus(dtp_ref[...].astype(F32))
    u=u_ref[...].astype(F32)
    dec[...]=jnp.where(keep_ref[...]>0,delta,HUGE)
    inj[...]=delta*u
    def chunk(k,state):
        heads_ref[k]=state
        b=b_ref[k]; c=c_ref[k]
        an=a2[...]
        base=pl.multiple_of(k*STEPS,STEPS)
        for j in range(STEPS):
            d=dec[pl.ds(base+j,1),:]
            v=inj[pl.ds(base+j,1),:]
            state=jnp.exp2(d*an)*state+b[:,j:j+1]*v
            ys[pl.ds(base+j,1),:]=jnp.sum(c[:,j:j+1]*state,axis=0,keepdims=True)
        return state
    st[...]=lax.fori_loop(0,T//STEPS,chunk,st[...])
    y=ys[...]+skip_ref[...]*u
    y_ref[...]=y
    z=z_ref[...].astype(F32)
    gated_ref[...]=(y*(z*jax.nn.sigmoid(z))).astype(BF)

def scan_forward(dtp,u,b,c,keep,alog,skip,z,T=128):
    N,C=u.shape
    S=alog.shape[0]
    nk=N//STEPS; tk=T//STEPS
    row=pl.BlockSpec((T,C),lambda i:(i,0))
    col=pl.BlockSpec((tk,S,STEPS),lambda i:(i,0,0))
    whole=lambda s: pl.BlockSpec(s,lambda i:(0,0))
    return pl.pallas_call(scan_forward_kernel,grid=(N//T,),
      in_specs=[row,row,col,col,pl.BlockSpec((T,1),lambda i:(i,0)),whole((S,C)),whole((1,C)),row],
      out_specs=[row,row,pl.BlockSpec((tk,S,C),lambda i:(i,0,0))],
      out_shape=[jax.ShapeDtypeStruct((N,C),BF),jax.ShapeDtypeStruct((N,C),F32),jax.ShapeDtypeStruct((nk,S,C),F32)],
      scratch_shapes=[pltpu.VMEM((S,C),F32),pltpu.VMEM((T,C),F32),pltpu.VMEM((T,C),F32),pltpu.VMEM((T,C),F32),pltpu.VMEM((S,C),F32)],
      compiler_params=pltpu.CompilerParams(vmem_limit_bytes=48<<20),
      name="scan_forward")(dtp,u,b,c,keep,alog,skip,z)

def scan_backward_kernel(dtp_ref,u_ref,b_ref,c_ref,keep_ref,alog_ref,skip_ref,z_ref,y_ref,dg_ref,heads_ref,
        ddtp_ref,dus_ref,dz_ref,dm_ref,dalog_ref,dskip_ref, run, dec, inj, dly, dys, sq, wa, sts, dcs, an2, an1, acc):
    T,C=u_ref.shape
    S=alog_ref.shape[0]
    first=pl.program_id(0)==0
    last=pl.program_id(0)==pl.num_programs(0)-1
    @pl.when(first)
    def _():
        run[...]=jnp.zeros_like(run)
        acc[...]=jnp.zeros_like(acc)
        dskip_ref[...]=jnp.zeros_like(dskip_ref)
        an1[...]=-jnp.exp(alog_ref[...])
        an2[...]=an1[...]*1.4426950408889634
    dtp=dtp_ref[...].astype(F32)
    delta=jax.nn.softplus(dtp)
    u=u_ref[...].astype(F32)
    dec[...]=jnp.where(keep_ref[...]>0,delta,HUGE)
    dly[...]=delta
    inj[...]=delta*u
    z=z_ref[...].astype(F32)
    sg=jax.nn.sigmoid(z)
    dg=dg_ref[...].astype(F32)
    dy=dg*(z*sg)
    dys[...]=dy
    dz_ref[...]=(dg*y_ref[...]*(sg*(1.0+z*(1.0-sg)))).astype(BF)
    dskip_ref[...]+=jnp.sum(dy*u,axis=0,keepdims=True)
    def chunk(i,running):
        k=T//STEPS-1-i
        b=b_ref[k]; c=c_ref[k]
        base=pl.multiple_of(k*STEPS,STEPS)
        state=heads_ref[k]
        an=an2[...]
        for j in range(STEPS):
            d=dec[pl.ds(base+j,1),:]
            v=inj[pl.ds(base+j,1),:]
            dc=jnp.exp2(d*an)
            sd=dc*state
            state=sd+b[:,j:j+1]*v
            dcs[j]=dc
            sts[j]=sd
        lane=lax.broadcasted_iota(jnp.int32,(S,STEPS),1)
        db=jnp.zeros((S,STEPS),F32); dcc=jnp.zeros((S,STEPS),F32)
        for j in range(STEPS-1,-1,-1):
            g=dys[pl.ds(base+j,1),:]
            v=inj[pl.ds(base+j,1),:]
            bj=b[:,j:j+1]
            ds=c[:,j:j+1]*g+running
            sd=sts[j]
            w=ds*sd
            sq[pl.ds(base+j,1),:]=jnp.sum(ds*bj,axis=0,keepdims=True)
            wa[pl.ds(base+j,1),:]=jnp.sum(w*an1[...],axis=0,keepdims=True)
            acc[...]+=w*dly[pl.ds(base+j,1),:]
            db=jnp.where(lane==j,jnp.sum(ds*v,axis=1,keepdims=True),db)
            dcc=jnp.where(lane==j,jnp.sum(g*(sd+bj*v),axis=1,keepdims=True),dcc)
            running=dcs[j]*ds
        dm_ref[k,:S]=db
        dm_ref[k,S:]=dcc
        return running
    run[...]=lax.fori_loop(0,T//STEPS,chunk,run[...])
    dd=wa[...]+u*sq[...]
    ddtp_ref[...]=(dd*jax.nn.sigmoid(dtp)).astype(BF)
    dus_ref[...]=delta*sq[...]+dy*skip_ref[...]
    @pl.when(last)
    def _():
        dalog_ref[...]=acc[...]*an1[...]

def scan_backward(dtp,u,b,c,keep,alog,skip,z,y,dg,heads,T=128):
    N,C=u.shape
    S=alog.shape[0]
    nk=N//STEPS; tk=T//STEPS; nb=N//T
    row=pl.BlockSpec((T,C),lambda i:(nb-1-i,0))
    col=pl.BlockSpec((tk,S,STEPS),lambda i:(nb-1-i,0,0))
    whole=lambda s: pl.BlockSpec(s,lambda i:(0,0))
    sc=lambda *s: pltpu.VMEM(s,F32)
    return pl.pallas_call(scan_backward_kernel,grid=(nb,),
      in_specs=[row,row,col,col,pl.BlockSpec((T,1),lambda i:(nb-1-i,0)),whole((S,C)),whole((1,C)),row,row,row,pl.BlockSpec((tk,S,C),lambda i:(nb-1-i,0,0))],
      out_specs=[row,row,row,pl.BlockSpec((tk,2*S,STEPS),lambda i:(nb-1-i,0,0)),whole((S,C)),whole((1,C))],
      out_shape=[jax.ShapeDtypeStruct((N,C),BF),jax.ShapeDtypeStruct((N,C),F32),jax.ShapeDtypeStruct((N,C),BF),jax.ShapeDtypeStruct((nk,2*S,STEPS),F32),jax.ShapeDtypeStruct((S,C),F32),jax.ShapeDtypeStruct((1,C),F32)],
      scratch_shapes=[sc(S,C),sc(T,C),sc(T,C),sc(T,C),sc(T,C),sc(T,C),sc(T,C),sc(STEPS,S,C),sc(STEPS,S,C),sc(S,C),sc(S,C),sc(S,C)],
      compiler_params=pltpu.CompilerParams(vmem_limit_bytes=48<<20),
      name="scan_backward")(dtp,u,b,c,keep,alog,skip,z,y,dg,heads)


def contract(left, right, left_dim, right_dim):
    return lax.dot_general(
        left, right, (((left_dim,), (right_dim,)), ((), ())), preferred_element_type=F32
    )


def segment_of(places, bounds):
    return jnp.sum((places[:, None] >= bounds[None, :]).astype(jnp.int32), axis=1)


def conv_masks(places, bounds, width):
    segment = segment_of(places, bounds)
    return [
        ((places >= offset) & (segment_of(places - offset, bounds) == segment)).astype(F32)
        for offset in range(width)
    ]


def silu_slope(values):
    sigma = jax.nn.sigmoid(values)
    return sigma * (1.0 + values * (1.0 - sigma))


def split_kinds(rows, kinds, parts):
    count, depth = rows.shape
    pieces = rows.reshape(count, parts, 1, depth // parts)
    picked = kinds[:, None, :, None]
    return jnp.where(picked, pieces, jnp.zeros((), rows.dtype)).reshape(count, 3 * depth)


def gather_master(master):
    rows = lax.all_gather(jnp.transpose(master.astype(BF), (1, 0, 2)), "dp", axis=0)
    return rows.reshape(-1, master.shape[2])


def scatter_master(grad, rows):
    parts = lax.axis_size("dp")
    kept = lax.psum_scatter(
        grad.reshape(parts, 3, rows, grad.shape[1]), "dp", scatter_dimension=0, tiled=False
    )
    return jnp.transpose(kept, (1, 0, 2))


def halves_out(block, wide):
    half = wide // 2
    columns = block.shape[1] // 2
    low = lax.axis_index("wide") < half
    first, second = block[:, :columns], block[:, columns:]
    even = [(v, 2 * v) if v < half else (v, 2 * (v - half) + 1) for v in range(wide)]
    odd = [(v, 2 * v + 1) if v < half else (v, 2 * (v - half)) for v in range(wide)]
    got_a = lax.ppermute(jnp.where(low, first, second), "wide", even)
    got_b = lax.ppermute(jnp.where(low, second, first), "wide", odd)
    is_even = lax.axis_index("wide") % 2 == 0
    return jnp.where(is_even, got_a, got_b), jnp.where(is_even, got_b, got_a)


def halves_back(xs, z, wide):
    half = wide // 2
    low = lax.axis_index("wide") < half
    even = [(2 * v, v) if v < half else (2 * (v - half) + 1, v) for v in range(wide)]
    odd = [(2 * v + 1, v) if v < half else (2 * (v - half), v) for v in range(wide)]
    is_even = lax.axis_index("wide") % 2 == 0
    got_a = lax.ppermute(jnp.where(is_even, xs, z), "wide", even)
    got_b = lax.ppermute(jnp.where(is_even, z, xs), "wide", odd)
    return jnp.concatenate([jnp.where(low, got_a, got_b), jnp.where(low, got_b, got_a)], axis=1)


def body(
    x_in,
    lengths,
    modality,
    norm_gain,
    conv_weight,
    conv_bias,
    a_log,
    d_skip,
    in_master,
    xproj_master,
    dtproj_master,
    dt_bias,
    out_master,
    cotangent,
):
    wide, dp = lax.axis_size("wide"), lax.axis_size("dp")
    place = lax.axis_index("wide")
    count = x_in.shape[0]
    span = count * wide
    channels = INNER // wide
    width = conv_weight.shape[0]
    own = lambda table: lax.dynamic_slice_in_dim(table, place * channels, channels, table.ndim - 1)

    bounds = jnp.cumsum(lengths.reshape(-1))
    places = jnp.arange(span, dtype=jnp.int32)
    living = places < bounds[-1]
    masks = conv_masks(places, bounds, width)
    later = conv_masks(jnp.arange(span + width - 1, dtype=jnp.int32), bounds, width)
    alive_here = (place * count + jnp.arange(count, dtype=jnp.int32)) < bounds[-1]

    scale = lax.rsqrt(jnp.mean(x_in * x_in, axis=1, keepdims=True) + EPSILON)
    normed = (x_in * scale * norm_gain[None, :]).astype(BF)
    d_branch = jnp.where(alive_here[:, None], cotangent, 0.0).astype(BF)
    w_in = gather_master(in_master)
    normed_all = lax.all_gather(normed, "wide", axis=0, tiled=True)
    kinds_all = lax.all_gather(modality, "wide", axis=0, tiled=True)
    w_x = gather_master(xproj_master)
    w_dt = gather_master(dtproj_master)
    w_out = gather_master(out_master)
    d_branch_all = lax.all_gather(d_branch, "wide", axis=0, tiled=True)
    kinds = (kinds_all[:, None] == jnp.arange(3, dtype=jnp.int32)[None, :]) & living[:, None]

    normed_kinds = split_kinds(normed_all, kinds, dp)
    mixed = contract(normed_kinds, w_in, 1, 0).astype(BF)
    xs, z = halves_out(mixed, wide)

    taps = own(conv_weight)
    xs_value = xs.astype(F32)
    extended = jnp.concatenate([jnp.zeros((width - 1, channels), F32), xs_value], axis=0)
    pre = own(conv_bias)[None, :]
    for offset in range(width):
        begin = width - 1 - offset
        pre = (
            pre + taps[begin][None, :] * extended[begin : begin + span] * masks[offset][:, None]
        )
    inner = jax.nn.silu(pre).astype(BF)

    rank = xproj_master.shape[0] * dp
    w_x_kinds = w_x.reshape(dp, 3, rank // dp, channels).transpose(1, 0, 2, 3).reshape(3, rank, channels)
    by_kind = contract(inner, w_x_kinds.reshape(3 * rank, channels), 1, 1).reshape(span, 3, rank)
    proj = lax.psum(jnp.sum(jnp.where(kinds[:, :, None], by_kind, 0.0), axis=1), "wide")
    rates = proj[:, :DT_RANK].astype(BF)
    maps = proj[:, DT_RANK:].astype(BF).astype(F32)
    rates_kinds = split_kinds(rates, kinds, dp)
    bias = jnp.where(kinds[:, :, None], dt_bias.astype(BF).astype(F32)[None], 0.0).sum(axis=1)
    dtp = (contract(rates_kinds, w_dt, 1, 0) + bias).astype(BF)

    blocks = span // STEPS
    to_columns = lambda rows: rows.reshape(blocks, STEPS, -1).transpose(0, 2, 1)
    b_columns = to_columns(maps[:, :STATE])
    c_columns = to_columns(maps[:, STATE:])
    keep = masks[1][:, None]
    a_own = own(a_log)
    skip_own = own(d_skip)[None, :]
    gated, y_value, heads = scan_forward(dtp, inner, b_columns, c_columns, keep, a_own, skip_own, z)

    d_branch_kinds = split_kinds(d_branch_all, kinds, dp)
    d_gated = contract(d_branch_kinds, w_out, 1, 0).astype(BF)
    w_out_kinds = w_out.reshape(dp, 3, -1, channels)
    branch = jnp.zeros((span, x_in.shape[1]), F32)
    for kind in range(3):
        picked = jnp.where(kinds[:, kind : kind + 1], gated, jnp.zeros((), BF))
        branch = branch + contract(picked, w_out_kinds[:, kind].reshape(-1, channels), 1, 1)
    branch = lax.psum_scatter(branch.astype(BF), "wide", scatter_dimension=0, tiled=True)
    result = x_in + branch.astype(F32)
    grad_out = contract(d_branch_kinds, gated, 0, 0)
    out_grad = scatter_master(grad_out.astype(BF), out_master.shape[0]).astype(F32)

    d_dtp, d_scan, d_z, d_columns, alog_part, skip_part = scan_backward(
        dtp, inner, b_columns, c_columns, keep, a_own, skip_own, z, y_value, d_gated, heads
    )
    d_dtp = jnp.where(living[:, None], d_dtp, jnp.zeros((), BF))
    d_maps = d_columns.transpose(0, 2, 1).reshape(span, 2 * STATE)
    d_rates = jnp.zeros((span, DT_RANK), F32)
    w_dt_kinds = w_dt.reshape(dp, 3, -1, channels)
    d_dtp_kinds = split_kinds(d_dtp, kinds, 1)
    for kind in range(3):
        picked = jnp.where(kinds[:, kind : kind + 1], d_dtp, jnp.zeros((), BF))
        d_rates = d_rates + contract(picked, w_dt_kinds[:, kind].reshape(-1, channels), 1, 1)
    d_proj = lax.psum(jnp.concatenate([d_rates, d_maps], axis=1), "wide")
    d_proj = jnp.where(living[:, None], d_proj, 0.0).astype(BF)
    grad_dt = contract(rates_kinds, d_dtp, 0, 0)
    bias_part = jnp.stack(
        [jnp.sum(jnp.where(kinds[:, k : k + 1], d_dtp.astype(F32), 0.0), axis=0) for k in range(3)]
    )
    d_proj_kinds = split_kinds(d_proj, kinds, 1)
    d_inner = contract(d_proj_kinds, w_x_kinds.reshape(3 * rank, channels), 1, 0).astype(BF)
    grad_x = contract(d_proj_kinds, inner, 0, 0)
    grad_x = grad_x.reshape(3, dp, rank // dp, channels).transpose(1, 0, 2, 3).reshape(-1, channels)
    xproj_grad = scatter_master(grad_x, rank // dp)
    dtproj_grad = scatter_master(grad_dt, dtproj_master.shape[0])

    d_pre = (d_inner.astype(F32) + d_scan) * silu_slope(pre)
    further = jnp.concatenate([d_pre, jnp.zeros((width - 1, channels), F32)], axis=0)
    conv_rows = []
    d_xs = jnp.zeros_like(xs_value)
    for offset in range(width):
        begin = width - 1 - offset
        conv_rows.append(
            jnp.sum(d_pre * masks[offset][:, None] * extended[begin : begin + span], axis=0)
        )
        masked = further * later[offset][:, None]
        d_xs = d_xs + taps[begin][None, :] * masked[offset : offset + span]
    conv_part = jnp.stack(conv_rows[::-1], axis=0)
    conv_bias_part = jnp.sum(d_pre, axis=0)
    d_xs = jnp.where(living[:, None], d_xs, 0.0).astype(BF)
    d_z = jnp.where(living[:, None], d_z, jnp.zeros((), BF))
    d_mixed = halves_back(d_xs, d_z, wide)
    grad_in = contract(normed_kinds, d_mixed, 0, 0)
    in_grad = scatter_master(grad_in.astype(BF), in_master.shape[0]).astype(F32)

    d_normed = jnp.zeros((span, x_in.shape[1]), F32)
    w_in_kinds = w_in.reshape(dp, 3, -1, w_in.shape[1])
    for kind in range(3):
        picked = jnp.where(kinds[:, kind : kind + 1], d_mixed, jnp.zeros((), BF))
        d_normed = d_normed + contract(
            picked, w_in_kinds[:, kind].reshape(-1, w_in.shape[1]), 1, 1
        )
    d_normed = lax.psum_scatter(d_normed.astype(BF), "wide", scatter_dimension=0, tiled=True)
    d_normed = d_normed.astype(F32)
    gain_part = jnp.sum(d_normed * x_in * scale, axis=0)
    scaled_back = d_normed * norm_gain[None, :]
    x_grad = cotangent + scale * (
        scaled_back - x_in * scale * scale * jnp.mean(scaled_back * x_in, axis=1, keepdims=True)
    )

    shared = jnp.concatenate([conv_part, conv_bias_part[None], alog_part, skip_part, bias_part], axis=0)
    shared = lax.psum(shared, "dp")
    table = lax.all_gather(shared[: width + STATE + 2], "wide", axis=1, tiled=True)
    gain_grad = lax.psum(gain_part, ("dp", "wide"))
    return (
        result,
        x_grad,
        gain_grad,
        table[:width],
        table[width],
        table[width + 1 : width + 1 + STATE],
        table[width + 1 + STATE],
        in_grad,
        xproj_grad,
        dtproj_grad,
        shared[width + STATE + 2 :],
        out_grad,
    )


def solution(mesh):
    in_specs = (
        P(("dp", "wide"), None),
        P("dp", None),
        P(("dp", "wide")),
        P(),
        P(),
        P(),
        P(),
        P(),
        P("dp", None, "wide"),
        P("dp", None, "wide"),
        P("dp", None, "wide"),
        P(None, "wide"),
        P("dp", None, "wide"),
        P(("dp", "wide"), None),
    )
    out_specs = (
        P(("dp", "wide"), None),
        P(("dp", "wide"), None),
        P(),
        P(),
        P(),
        P(),
        P(),
        P("dp", None, "wide"),
        P("dp", None, "wide"),
        P("dp", None, "wide"),
        P(None, "wide"),
        P("dp", None, "wide"),
    )
    return jax.shard_map(body, mesh=mesh, in_specs=in_specs, out_specs=out_specs, check_vma=False)
```

time: 6050 us -> 1000 us (0.17)
  waiting for transfers between devices: 4120 us -> 403 us
  other arithmetic: 1160 us -> 54.2 us
  local copies, waits for them, and re-layouts: 444 us -> 50.8 us
  blocking collectives: 15.7 us -> 222 us
  Pallas kernels: 0 us -> 123 us
  starting transfers between devices: 126 us -> 13.8 us
    all_to_all x23 -> x0, waiting for transfers between devices: 3520 us -> none  [the longest x1 1390 us: body(): lax.all_to_all(grad_in, 'wide', split_axis=1, concat_axis=1, tiled=True)]
    reduce_sum x178 -> x3, other arithmetic: 638 us -> 6.97 us  [the longest x1 3.84 us: body(): jnp.sum(d_pre * masks[offset][:, None] * extended[begin:begin + span], ax...]
    all_gather x5 -> x4, waiting for transfers between devices: 27 us -> 189 us  [the longest x2 103 us: gather_master(): lax.all_gather(jnp.transpose(master.astype(BF), (1, 0, 2)), 'dp', axis=0)]
    mul x390 -> x0, other arithmetic: 157 us -> none  [the longest x4 91 us: one_block(): running = step_decay(step_size[position], kept[position], a_neg) * running]
    psum x0 -> x4, blocking collectives: none -> 144 us  [the longest x1 51 us: body(): lax.psum(jnp.sum(jnp.where(kinds[:, :, None], by_kind, 0.0), axis=1), 'wi...]
    reduce_scatter x4 -> x5, waiting for transfers between devices: 341 us -> 209 us  [the longest x3 178 us: scatter_master(): lax.psum_scatter(grad.reshape(parts, 3, rows, grad.shape[1]), 'dp', scatt...]
    pallas_call x0 -> x2, Pallas kernels: none -> 123 us  [the longest x1 105 us: scan_backward(): pl.pallas_call(scan_backward_kernel, grid=(nb,), in_specs=[row, row, col,...]
    add x47 -> x0, other arithmetic: 122 us -> none  [the longest x4 91.4 us: one_block(): step_decay(step_size[position], kept[position], a_neg) * state]
  transfers between devices with their start and end apart: 36 -> 14, of which waited for: 27 -> 9; matrix products, arithmetic and copies ran while one was open for 16% -> 18% of each run, Pallas kernels for 0% -> 0%
where the time goes in v1:
time: 1000 us; the launch traced here: 993 us
  waiting for transfers between devices  403 us (40%)
  blocking collectives  222 us (22%)
  Pallas kernels  123 us (12%)
  matrix products  111 us (11%)
  other arithmetic  54.2 us (5%)
  local copies, waits for them, and re-layouts  50.8 us (5%)
  between operations  15.2 us (2%)
  starting transfers between devices  13.8 us (1%)
    reduce_scatter x3, waiting for transfers between devices, scatter_master(): lax.psum_scatter(grad.reshape(parts, 3, rows, grad.shape[1]), 'dp', scatt...  178 us
    dot_general x18, matrix products, contract(): lax.dot_general(left, right, (((left_dim,), (right_dim,)), ((), ())), pre...  111 us
    pallas_call x1, Pallas kernels, scan_backward(): pl.pallas_call(scan_backward_kernel, grid=(nb,), in_specs=[row, row, col,...  105 us
    all_gather x2, waiting for transfers between devices, gather_master(): lax.all_gather(jnp.transpose(master.astype(BF), (1, 0, 2)), 'dp', axis=0)  103 us
    all_gather x1, waiting for transfers between devices, body(): d_branch_all = lax.all_gather(d_branch, 'wide', axis=0, tiled=True)  68 us
    psum x1, blocking collectives, body(): lax.psum(jnp.sum(jnp.where(kinds[:, :, None], by_kind, 0.0), axis=1), 'wi...  51 us
    psum x1, blocking collectives, body(): d_proj = lax.psum(jnp.concatenate([d_rates, d_maps], axis=1), 'wide')  43.4 us
    all_gather x1, blocking collectives, body(): lax.all_gather(shared[:width + STATE + 2], 'wide', axis=1, tiled=True)  42.6 us
  transfers between devices with their start and end apart: 14, of which 9 were waited for; matrix products, arithmetic and copies ran while one was open for 18% of the time, Pallas kernels for 0%

profile of v1, /device:TPU:0, one launch (start us, length us, event | category | flops | bytes accessed | tf_op | source)
XLA Modules:
  0.0 993.2 jit_solution(15332025465656163631)
XLA Ops:
  7.3 1.5 multiply_reduce_fusion.4
  9.3 2.2 multiply_convert_fusion.1
  13.9 4.9 convert_bitcast_fusion.2
  19.0 1.8 copy-done.18
  20.8 1.3 convert_bitcast_fusion.3
  23.2 8.6 all-gather.1
  36.3 20.8 %all-gather.4 = s32[8,1,128]{2,1,0:T(1,128)S(1)} all-gather(s32[1,1,128]{2,1,0:T(1,128)S(1)} %bitcast.204), channel_id=1, replica_groups=mesh['dp'=4,'wide'=8] {'wide'}, dimensions={0}, use_global_device_ids=true | all-gather | bytes 4608 | tf_op jit(solution)/shard_map/all_gather | solution.py:247
  59.9 6.1 all-gather.2
  66.0 2.1 select_reduce_fusion
  68.9 18.8 %all-gather.10.cloned.1.call-done = bf16[1024,2048]{1,0:T(8,128)(2,1)} async-done(((bf16[128,2048]{1,0:T(8,128)(2,1)}), bf16[1024,2048]{1,0:T(8,128)(2,1)}) %all-gather.10.cloned.1.call-update) | async-done | bytes 4194320 | tf_op jit(solution)/shard_map/all_gather | solution.py:246
  87.7 6.4 copy.80
  94.1 68.0 %all-gather.12.cloned.1.call-done = bf16[1024,2048]{1,0:T(8,128)(2,1)} async-done(((bf16[128,2048]{1,0:T(8,128)(2,1)}), bf16[1024,2048]{1,0:T(8,128)(2,1)}) %all-gather.12.cloned.1.call-update) | async-done | bytes 4194320 | tf_op jit(solution)/shard_map/all_gather | solution.py:251
  162.1 6.4 copy.81
  168.5 76.1 %all-gather.14.cloned.1.call-done = bf16[12,512,1024]{2,1,0:T(8,128)(2,1)} async-done(((bf16[3,512,1024]{2,1,0:T(8,128)(2,1)}), bf16[12,512,1024]{2,1,0:T(8,128)(2,1)}) %all-gather.14.cloned.1.call-update) | async-done | bytes 12582928 | tf_op jit(solution)/shard_map/all_gather | solution.py:175
  244.7 17.9 %bitcast_convert_fusion = bf16[1024,1024]{1,0:T(8,128)(2,1)S(1)} fusion(bf16[4,3,512,1024]{3,2,1,0:T(8,128)(2,1)} %bitcast.156, pred[1024,3]{0,1:T(4,128)(4,1)S(1)} %fusion.64, bf16[1024,4,512]{0,2,1:T(8,128)(2,1)} %bitcast.152), kind=kOutput, calls=%fused_computation.8 | convolution fusion | flops 12892241920 | bytes 18877440 | tf_op jit(solution)/shard_map/dot_general | solution.py:145
  262.8 1.5 collective-permute-start.1
  264.3 1.8 collective-permute-start
  266.1 26.4 %all-gather.16.cloned.1.call-done = bf16[12,512,512]{2,1,0:T(8,128)(2,1)} async-done(((bf16[3,512,512]{2,1,0:T(8,128)(2,1)}), bf16[12,512,512]{2,1,0:T(8,128)(2,1)}) %all-gather.16.cloned.1.call-update) | async-done | bytes 6291472 | tf_op jit(solution)/shard_map/all_gather | solution.py:175
  292.5 11.4 %bitcast_convert_fusion.1.dg_ref = bf16[1024,512]{1,0:T(8,128)(2,1)} fusion(bf16[4,3,512,512]{3,2,1,0:T(8,128)(2,1)} %bitcast.162, pred[1024,3]{0,1:T(4,128)(4,1)S(1)} %fusion.64, bf16[1024,4,512]{0,2,1:T(8,128)(2,1)} %bitcast.154), kind=kOutput, calls=%fused_computation.29 | convolution fusion | flops 6449266688 | bytes 11537408 | tf_op jit(solution)/shard_map/dot_general | solution.py:145
  303.9 1.8 broadcast_select_fusion.10
  305.7 2.8 multiply_convert_fusion
  308.5 1.6 select_reduce_fusion.1
  310.1 51.0 %all-reduce.8 = bf16[1024,160]{0,1:T(8,128)(2,1)S(1)} all-reduce(f32[1024,160]{0,1:T(8,128)} %select_reduce_fusion.1), channel_id=1, replica_groups=mesh['dp'=4,'wide'=8] {'wide'}, use_global_device_ids=true, to_apply=%region_7.8 | all-reduce | flops 163840 | bytes 983040 | tf_op jit(solution)/shard_map/psum | solution.py:272
  362.2 1.3 copy.88
  364.5 1.3 copy.87
  365.9 2.5 fusion.11.dtp_ref
  368.4 18.6 %scan_forward.1 = (bf16[1024,512]{1,0:T(8,128)(2,1)S(1)}, f32[1024,512]{1,0:T(8,128)}, f32[64,16,512]{2,1,0:T(8,128)}) custom-call(bf16[1024,512]{1,0:T(8,128)(2,1)S(1)} %fusion.11.dtp_ref, bf16[1024,512]{1,0:T(8,128)(2,1)S(1)} %get-tuple-element.54.u_ref, f32[64,16,16]{2,1,0:T(8,128)S(1)} %bitcast.145, f32[64,16,16]{2,1,0:T(8,128)S(1)} %bitcast.147, ...), custom_call_target="tpu_custom_call" | custom-call | tf_op jit(solution)/shard_map/scan_forward/pallas_call | solution.py:53
  387.0 104.8 %scan_backward.1 = (bf16[1024,512]{1,0:T(8,128)(2,1)S(1)}, f32[1024,512]{1,0:T(8,128)}, bf16[1024,512]{1,0:T(8,128)(2,1)S(1)}, f32[64,32,16]{2,1,0:T(8,128)S(1)}...) custom-call(bf16[1024,512]{1,0:T(8,128)(2,1)S(1)} %fusion.11.dtp_ref, bf16[1024,512]{1,0:T(8,128)(2,1)} %copy-done.2, ...), custom_call_target="tpu_custom_call" | custom-call | tf_op jit(solution)/shard_map/scan_backward/pallas_call | solution.py:135
  493.9 1.2 copy.72
  495.2 1.6 fusion.37
  496.8 1.6 convolution_add_fusion.1
  498.4 1.6 convolution_add_fusion
  500.1 43.4 %all-reduce.9 = bf16[1024,160]{0,1:T(8,128)(2,1)S(1)} all-reduce(f32[1024,160]{0,1:T(8,128)S(1)} %pad_maximum_fusion.1), channel_id=1, replica_groups=mesh['dp'=4,'wide'=8] {'wide'}, use_global_device_ids=true, to_apply=%region_10.11 | all-reduce | flops 163840 | bytes 983040 | tf_op jit(solution)/shard_map/psum | solution.py:311
  543.7 1.9 convolution_convert_fusion.2
  546.0 3.8 multiply_reduce_fusion
  549.9 2.9 broadcast_select_fusion.9
  552.8 9.5 collective-permute-start.2
  563.5 9.2 fusion.89
  572.7 1.7 convolution_bitcast_fusion
  574.5 4.1 collective-permute-done.3
  578.6 1.7 broadcast_select_fusion.5
  580.3 6.9 fusion.15
  587.2 6.8 fusion.13
  594.1 10.1 %add_convert_fusion = bf16[1024,2048]{1,0:T(8,128)(2,1)} fusion(f32[1024,2048]{1,0:T(8,128)} %fusion.15, f32[1024,2048]{1,0:T(8,128)} %fusion.13, bf16[2048,1024]{1,0:T(8,128)(2,1)S(1)} %bitcast.165, pred[1024]{0:T(1024)(128)(4,1)S(1)} %copy-done.45, bf16[1024,512]{1,0:T(8,128)(2,1)S(1)} %get-tuple-element.65, bf16[1024,512]{1,0:T(8,128)(2,1)S(1)} %get-tuple-element.64), kind=kOutput, calls=%fused_computation.4 | convolution fusion | flops 4306501632 | bytes 27264000 | tf_op jit(solution)/shard_map/dot_general | solution.py:145
  604.7 3.3 fusion.90
  608.0 2.4 fusion.42
  610.4 5.7 fusion.40
  616.0 6.7 add_convert_fusion.1
  622.8 9.5 broadcast_select_fusion
  632.4 8.8 convolution_convert_fusion.1
  642.4 20.6 %convolution_convert_fusion = bf16[6144,1024]{1,0:T(8,128)(2,1)} fusion(bf16[1024,6144]{0,1:T(8,128)(2,1)} %bitcast.159, bf16[1024,512]{1,0:T(8,128)(2,1)S(1)} %copy-done.21, bf16[1024,512]{1,0:T(8,128)(2,1)S(1)} %get-tuple-element.64), kind=kOutput, calls=%fused_computation.2 | convolution fusion | flops 12895387648 | bytes 27262976 | tf_op jit(solution)/shard_map/dot_general | solution.py:145
  665.5 11.1 %psum.31 = f32[25,512]{1,0:T(8,128)S(1)} all-reduce(f32[25,512]{1,0:T(8,128)S(1)} %concatenate.19), channel_id=1, replica_groups=mesh['dp'=4,'wide'=8] {'dp'}, use_global_device_ids=true, to_apply=%region_27.28 | all-reduce | flops 12800 | bytes 102400 | tf_op jit(solution)/shard_map/psum | solution.py:359
  676.5 42.6 %all_gather.47 = f32[22,4096]{1,0:T(8,128)S(1)} all-gather(f32[22,512]{1,0:T(8,128)S(1)} %slice.182), channel_id=1, replica_groups=mesh['dp'=4,'wide'=8] {'wide'}, dimensions={1}, use_global_device_ids=true | all-gather | bytes 405504 | tf_op jit(solution)/shard_map/all_gather | solution.py:360
  721.1 1.5 fusion.28
  723.4 2.3 dynamic-slice_bitcast_fusion
  725.7 1.4 fusion.27
  727.1 38.4 %psum.30 = f32[2048]{0:T(1024)} all-reduce(f32[2048]{0:T(1024)S(1)} %get-tuple-element.35), channel_id=1, replica_groups=mesh['dp'=4,'wide'=8] {'dp','wide'}, use_global_device_ids=true, to_apply=%region_18.19 | all-reduce | flops 2048 | bytes 16384 | tf_op jit(solution)/shard_map/psum | solution.py:361
  765.5 31.3 %reduce-scatter.7.cloned.1.call-done = bf16[128,2048]{1,0:T(8,128)(2,1)} async-done(((bf16[1024,2048]{1,0:T(8,128)(2,1)}), bf16[128,2048]{1,0:T(8,128)(2,1)}) %reduce-scatter.7.cloned.1.call-update) | async-done | bytes 524304 | tf_op jit(solution)/shard_map/reduce_scatter | solution.py:295
  796.8 2.9 fusion.25
  799.7 58.5 %reduce-scatter.15.cloned.1.call-done = bf16[1,3,512,512]{3,2,1,0:T(8,128)(2,1)} async-done(((bf16[4,3,512,512]{3,2,1,0:T(8,128)(2,1)}), bf16[1,3,512,512]{3,2,1,0:T(8,128)(2,1)}) %reduce-scatter.15.cloned.1.call-update) | async-done | bytes 1572880 | tf_op jit(solution)/shard_map/reduce_scatter | solution.py:181
  858.2 3.5 convert_bitcast_fusion.1
  861.8 98.2 %reduce-scatter.11.cloned.1.call-done = bf16[1,3,512,1024]{3,2,1,0:T(8,128)(2,1)} async-done(((bf16[4,3,512,1024]{3,2,1,0:T(8,128)(2,1)}), bf16[1,3,512,1024]{3,2,1,0:T(8,128)(2,1)}) %reduce-scatter.11.cloned.1.call-update) | async-done | bytes 3145744 | tf_op jit(solution)/shard_map/reduce_scatter | solution.py:181
  960.0 5.4 convert_bitcast_fusion
  965.3 20.9 %reduce-scatter.13.cloned.1.call-done = f32[1,3,32,512]{3,2,1,0:T(8,128)} async-done(((f32[4,3,32,512]{3,2,1,0:T(8,128)}), f32[1,3,32,512]{3,2,1,0:T(8,128)}) %reduce-scatter.13.cloned.1.call-update) | async-done | bytes 196624 | tf_op jit(solution)/shard_map/reduce_scatter | solution.py:181
  (182 shorter events, 25.1 us)
Async XLA Ops:
  7.2 51.6 %copy-start = (f32[16,4096]{1,0:T(8,128)S(1)}, f32[16,4096]{1,0:T(8,128)}, u32[]{:S(2)}) copy-start(f32[16,4096]{1,0:T(8,128)} %param.20) | copy-start | bytes 786436
  7.2 4.3 copy-start.52
  7.2 5.7 copy-start.13
  7.2 80.5 %all-gather.10.cloned.1.call-start = ((), (), s32[]{:S(2)}) async-start(), calls=%async_computation.5 | async-start | bytes 4718592 | tf_op jit(solution)/shard_map/all_gather | solution.py:246
  11.5 150.7 %all-gather.12.cloned.1.call-start = ((), (), s32[]{:S(2)}) async-start(), calls=%async_computation.7 | async-start | bytes 4718592 | tf_op jit(solution)/shard_map/all_gather | solution.py:251
  13.9 230.8 %all-gather.14.cloned.1.call-start = ((), (), s32[]{:S(2)}) async-start(), calls=%async_computation.12 | async-start | bytes 15728640 | tf_op jit(solution)/shard_map/all_gather | solution.py:175
  18.9 1.9 copy-start.18
  18.9 273.6 %all-gather.16.cloned.1.call-start = ((), (), s32[]{:S(2)}) async-start(), calls=%async_computation.13 | async-start | bytes 7864320 | tf_op jit(solution)/shard_map/all_gather | solution.py:175
  22.1 14.2 %copy-start.51 = (s32[128]{0:T(128)S(1)}, s32[128]{0:T(128)}, u32[]{:S(2)}) copy-start(s32[128]{0:T(128)} %param.16) | copy-start | bytes 1540
  22.1 37.7 %copy-start.25 = (f32[32,3,512]{2,0,1:T(8,128)S(1)}, f32[32,3,512]{2,0,1:T(8,128)}, u32[]{:S(2)}) copy-start(f32[32,3,512]{2,0,1:T(8,128)} %param.24) | copy-start | bytes 589828
  22.1 43.9 %copy-start.46 = (f32[3,512]{1,0:T(4,128)S(1)}, f32[3,512]{1,0:T(4,128)}, u32[]{:S(2)}) copy-start(f32[3,512]{1,0:T(4,128)} %param.25) | copy-start | bytes 18436
  22.2 701.2 %all-reduce.7.cloned.1.call-start = ((), (), s32[]{:S(2)}) async-start(), calls=%async_computation.14 | async-start | bytes 1966080
  57.8 11.1 %copy-start.32 = (pred[1024]{0:T(1024)(128)(4,1)}, pred[1024]{0:T(1024)(128)(4,1)S(1)}, u32[]{:S(2)}) copy-start(pred[1024]{0:T(1024)(128)(4,1)S(1)} %iota_compare_fusion.10) | copy-start | bytes 3076
  58.8 246.9 %copy-start.34 = (f32[1,512]{1,0:T(1,128)}, f32[1,512]{1,0:T(1,128)S(1)}, u32[]{:S(2)}) copy-start(f32[1,512]{1,0:T(1,128)S(1)} %get-tuple-element.79) | copy-start | bytes 6148
  58.8 246.9 %copy-start.36 = (f32[1,512]{1,0:T(1,128)}, f32[1,512]{1,0:T(1,128)S(1)}, u32[]{:S(2)}) copy-start(f32[1,512]{1,0:T(1,128)S(1)} %get-tuple-element.80) | copy-start | bytes 6148
  58.8 246.9 %copy-start.38 = (f32[1,512]{1,0:T(1,128)}, f32[1,512]{1,0:T(1,128)S(1)}, u32[]{:S(2)}) copy-start(f32[1,512]{1,0:T(1,128)S(1)} %get-tuple-element.81) | copy-start | bytes 6148
  58.8 246.9 %copy-start.40 = (f32[1,512]{1,0:T(1,128)}, f32[1,512]{1,0:T(1,128)S(1)}, u32[]{:S(2)}) copy-start(f32[1,512]{1,0:T(1,128)S(1)} %get-tuple-element.82) | copy-start | bytes 6148
  59.6 246.0 %copy-start.30 = (f32[1024]{0:T(1024)}, f32[1024]{0:T(1024)S(1)}, u32[]{:S(2)}) copy-start(f32[1024]{0:T(1024)S(1)} %get-tuple-element.89) | copy-start | bytes 12292
  66.0 28.1 %copy-start.19 = (bf16[12,32,512]{2,1,0:T(8,128)(2,1)}, bf16[12,32,512]{2,1,0:T(8,128)(2,1)S(1)}, u32[]{:S(2)}) copy-start(bf16[12,32,512]{2,1,0:T(8,128)(2,1)S(1)} %all-gather.2) | copy-start | bytes 1179652
  262.8 41.1 %collective-permute-start.1 = (bf16[1024,512]{1,0:T(8,128)(2,1)S(1)}, bf16[1024,512]{1,0:T(8,128)(2,1)}, u32[]{:S(2)}, u32[]{:S(2)}) collective-permute-start(bf16[1024,512]{1,0:T(8,128)(2,1)S(1)} %get-tuple-element.68), channel_id=1, source_target_pairs={{0,1},{1,3},{2,5},{3,7},{4,0},{5,2},{6,4},{7,6},{8,9},{9,11},{10,1... | collective-permute-start | bytes 3145736 | tf_op jit(solution)/shard_map/ppermute | solution.py:195
  264.3 39.6 %collective-permute-start = (bf16[1024,512]{1,0:T(8,128)(2,1)S(1)}, bf16[1024,512]{1,0:T(8,128)(2,1)}, u32[]{:S(2)}, u32[]{:S(2)}) collective-permute-start(bf16[1024,512]{1,0:T(8,128)(2,1)S(1)} %get-tuple-element.69), channel_id=1, source_target_pairs={{0,0},{1,2},{2,4},{3,6},{4,1},{5,3},{6,5},{7,7},{8,8},{9,10},{10,1... | collective-permute-start | bytes 3145736 | tf_op jit(solution)/shard_map/ppermute | solution.py:194
  305.6 2.9 copy-start.9
  305.6 62.8 %copy-start.4 = (bf16[1024,512]{1,0:T(8,128)(2,1)}, bf16[1024,512]{1,0:T(8,128)(2,1)S(1)}, u32[]{:S(2)}) copy-start(bf16[1024,512]{1,0:T(8,128)(2,1)S(1)} %get-tuple-element.66.z_ref) | copy-start | bytes 3145732
  305.7 2.8 copy-start.22
  308.5 59.9 %copy-start.2 = (bf16[1024,512]{1,0:T(8,128)(2,1)}, bf16[1024,512]{1,0:T(8,128)(2,1)S(1)}, u32[]{:S(2)}) copy-start(bf16[1024,512]{1,0:T(8,128)(2,1)S(1)} %get-tuple-element.54.u_ref) | copy-start | bytes 3145732
  361.1 7.3 copy-start.23
  387.0 104.8 %copy-start.5 = (bf16[1024,512]{1,0:T(8,128)(2,1)}, bf16[1024,512]{1,0:T(8,128)(2,1)S(1)}, u32[]{:S(2)}) copy-start(bf16[1024,512]{1,0:T(8,128)(2,1)S(1)} %get-tuple-element.21) | copy-start | bytes 3145732
  492.8 2.4 copy-start.28
  492.8 2.4 copy-start.33
  492.8 2.4 copy-start.50
  492.8 2.4 copy-start.8
  493.9 2.9 copy-start.27
  493.9 2.9 copy-start.49
  496.8 1.6 copy-start.26
  496.8 1.6 copy-start.45
  543.5 2.0 copy-start.10
  543.5 2.4 copy-start.12
  543.6 2.4 copy-start.31
  545.9 3.9 copy-start.35
  545.9 3.9 copy-start.37
  545.9 3.9 copy-start.39
  545.9 3.9 copy-start.41
  545.9 3.9 copy-start.42
  545.9 3.9 copy-start.43
  546.0 3.9 copy-start.44
  552.8 21.7 %collective-permute-start.2 = (bf16[1024,512]{1,0:T(8,128)(2,1)}, bf16[1024,512]{1,0:T(8,128)(2,1)}, u32[]{:S(2)}, u32[]{:S(2)}) collective-permute-start(bf16[1024,512]{1,0:T(8,128)(2,1)} %get-tuple-element.52), channel_id=1, source_target_pairs={{0,0},{2,1},{4,2},{6,3},{1,4},{3,5},{5,6},{7,7},{8,8},{10,9},{12,1... | collective-permute-start | bytes 3145736 | tf_op jit(solution)/shard_map/ppermute | solution.py:206
  563.5 9.2 copy-start.3
  563.5 15.1 %collective-permute-start.3 = (bf16[1024,512]{1,0:T(8,128)(2,1)}, bf16[1024,512]{1,0:T(8,128)(2,1)}, u32[]{:S(2)}, u32[]{:S(2)}) collective-permute-start(bf16[1024,512]{1,0:T(8,128)(2,1)} %broadcast_select_fusion.8), channel_id=1, source_target_pairs={{1,0},{3,1},{5,2},{7,3},{0,4},{2,5},{4,6},{6,7},{9,8},{11,9},{13,1... | collective-permute-start | bytes 3145736 | tf_op jit(solution)/shard_map/ppermute | solution.py:207
  574.4 151.3 %reduce-scatter.9.cloned.1.call-start = ((), (), s32[]{:S(2)}) async-start(), calls=%async_computation.8 | async-start | bytes 4718592 | tf_op jit(solution)/shard_map/reduce_scatter | solution.py:350
  574.5 5.8 copy-start.17
  580.3 13.8 %copy-start.20 = (bf16[1024,512]{1,0:T(8,128)(2,1)}, bf16[1024,512]{1,0:T(8,128)(2,1)S(1)}, u32[]{:S(2)}) copy-start(bf16[1024,512]{1,0:T(8,128)(2,1)S(1)} %get-tuple-element.65) | copy-start | bytes 3145732
  580.3 6.9 copy-start.16
  587.2 6.9 copy-start.15
  604.2 3.8 copy-start.6
  604.2 192.6 %reduce-scatter.7.cloned.1.call-start = ((), (), s32[]{:S(2)}) async-start(), calls=%async_computation.6 | async-start | bytes 4718592 | tf_op jit(solution)/shard_map/reduce_scatter | solution.py:295
  622.8 235.5 %reduce-scatter.15.cloned.1.call-start = ((), (), s32[]{:S(2)}) async-start(), calls=%async_computation.11 | async-start | bytes 7864320 | tf_op jit(solution)/shard_map/reduce_scatter | solution.py:181
  641.2 318.7 %reduce-scatter.11.cloned.1.call-start = ((), (), s32[]{:S(2)}) async-start(), calls=%async_computation.9 | async-start | bytes 15728640 | tf_op jit(solution)/shard_map/reduce_scatter | solution.py:181
  663.0 58.1 %copy-start.24 = (bf16[1024,128]{0,1:T(8,128)(2,1)S(1)}, bf16[1024,128]{0,1:T(8,128)(2,1)}, u32[]{:S(2)}) copy-start(bf16[1024,128]{0,1:T(8,128)(2,1)} %copy-done.23) | copy-start | bytes 786436
  663.0 323.2 %reduce-scatter.13.cloned.1.call-start = ((), (), s32[]{:S(2)}) async-start(), calls=%async_computation.10 | async-start | bytes 983040 | tf_op jit(solution)/shard_map/reduce_scatter | solution.py:181
  721.1 4.6 copy-start.11
  721.1 4.6 copy-start.29
  722.7 74.1 %copy-start.14 = (f32[128,2048]{1,0:T(8,128)S(1)}, f32[128,2048]{1,0:T(8,128)}, u32[]{:S(2)}) copy-start(f32[128,2048]{1,0:T(8,128)} %param.27) | copy-start | bytes 3145732
  722.7 74.1 %copy-start.48 = (f32[128]{0:T(128)S(1)}, f32[128]{0:T(128)}, u32[]{:S(2)}) copy-start(f32[128]{0:T(128)} %copy-done.47) | copy-start | bytes 1540
  960.0 26.3 %copy-start.1 = (f32[16,4096]{1,0:T(8,128)S(1)}, f32[16,4096]{1,0:T(8,128)}, u32[]{:S(2)}) copy-start(f32[16,4096]{1,0:T(8,128)} %param.20) | copy-start | bytes 786436
  (4 other events, 3.4 us)
Sparse Core Ops, SparseCore 0:
  11.6 76.1 all-gather.9
  90.4 71.6 all-gather.11
  164.3 80.3 all-gather.13
  246.1 46.3 all-gather.15
  574.6 33.9 all-reduce.6
  612.5 91.1 reduce-scatter.8
  707.3 89.4 reduce-scatter.6
  800.1 58.1 reduce-scatter.14
  860.8 99.0 reduce-scatter.10
  962.9 23.2 reduce-scatter.12

commit v2 on v1

--- a/solution.py
+++ b/solution.py
@@ -1,3 +1,5 @@
+import functools
+
 import jax
 import jax.numpy as jnp
 from jax import lax
@@ -141,6 +143,271 @@
       name="scan_backward")(dtp,u,b,c,keep,alog,skip,z,y,dg,heads)
 
 
+MESH = pl.DeviceIdType.MESH
+FLIGHT = 3
+
+
+def ring_index(position, wide):
+    if wide != 8:
+        return position
+    turn = position // 4
+    return (1 - turn) * 2 * position + turn * (2 * (7 - position) + 1)
+
+
+def ring_position(index, wide):
+    if wide != 8:
+        return index
+    return index // 2 + index % 2 * (7 - 2 * (index // 2))
+
+
+def gather_kernel(dp, wide, dp_pieces, wide_chunks, *refs):
+    dp_count, wide_count = len(dp_pieces), len(wide_chunks)
+    inputs, refs = refs[: dp_count + wide_count], refs[dp_count + wide_count :]
+    outputs, refs = refs[: dp_count + wide_count], refs[dp_count + wide_count :]
+    wides, narrows, refs = refs[:dp_count], refs[dp_count : 2 * dp_count], refs[2 * dp_count :]
+    x_send, x_recv, core_send, core_recv, on_send, on_recv = refs[:6]
+    up_send, up_recv, down_send, down_recv, local, load = refs[6:]
+    me, place = lax.axis_index("dp"), lax.axis_index("wide")
+    lines = dp // 2
+    line, core = me // 2, me % 2
+    partner = (me + 1 - 2 * core, place)
+    across = [(lax.rem(line + k, lines) * 2 + core, place) for k in range(1, lines)]
+    position = ring_position(place, wide)
+    after = (me, ring_index(lax.rem(position + 1, wide), wide))
+    before = (me, ring_index(lax.rem(position + wide - 1, wide), wide))
+    barrier = pltpu.get_barrier_semaphore()
+    peers = [partner, after, before] + across
+    for peer in peers:
+        pl.semaphore_signal(barrier, inc=1, device_id=peer, device_id_type=MESH)
+    pl.semaphore_wait(barrier, len(peers))
+
+    def remote(source, target, send, recv, device):
+        return pltpu.make_async_remote_copy(
+            src_ref=source, dst_ref=target, send_sem=send, recv_sem=recv, device_id=device, device_id_type=MESH
+        )
+
+    pieces, loads, casts = [], [], []
+    for a, cuts in enumerate(dp_pieces):
+        rows = inputs[a].shape[1] // cuts
+        for kind in range(3):
+            for cut in range(cuts):
+                part = pl.ds(cut * rows, rows)
+                loads.append(
+                    pltpu.make_async_copy(
+                        inputs[a].at[kind, part], wides[a].at[kind, part], load.at[len(loads)]
+                    )
+                )
+                casts.append((wides[a], narrows[a], kind, part))
+                pieces.append(
+                    (
+                        narrows[a].at[kind, part],
+                        lambda owner, a=a, kind=kind, part=part: outputs[a].at[owner, kind, part],
+                    )
+                )
+    chunks = []
+    for a, cuts in enumerate(wide_chunks):
+        rows = inputs[dp_count + a].shape[0] // cuts
+        for cut in range(cuts):
+            part = pl.ds(cut * rows, rows)
+            chunks.append(
+                (
+                    inputs[dp_count + a].at[part],
+                    lambda owner, a=a, part=part: outputs[dp_count + a].at[owner, part],
+                )
+            )
+
+    ups, downs = wide // 2, wide - 1 - wide // 2
+
+    def up(hop, i):
+        owner = ring_index(lax.rem(position + wide - hop, wide), wide)
+        source = chunks[i][0] if hop == 0 else chunks[i][1](owner)
+        return remote(source, chunks[i][1](owner), up_send.at[hop, i], up_recv.at[hop, i], after)
+
+    def down(hop, i):
+        owner = ring_index(lax.rem(position + hop, wide), wide)
+        source = chunks[i][0] if hop == 0 else chunks[i][1](owner)
+        return remote(source, chunks[i][1](owner), down_send.at[hop, i], down_recv.at[hop, i], before)
+
+    def cross(k, j):
+        return remote(pieces[j][0], pieces[j][1](me), x_send.at[k, j], x_recv.at[k, j], across[k])
+
+    def pair(j):
+        return remote(pieces[j][0], pieces[j][1](me), core_send.at[j], core_recv.at[j], partner)
+
+    def onward(k, j):
+        owner = lax.rem(line + lines - 1 - k, lines) * 2 + core
+        return remote(pieces[j][1](owner), pieces[j][1](owner), on_send.at[k, j], on_recv.at[k, j], partner)
+
+    for copy in loads:
+        copy.start()
+    for i in range(len(chunks)):
+        up(0, i).start()
+        if downs:
+            down(0, i).start()
+    copies = []
+    for i, (source, target) in enumerate(chunks):
+        copies.append(pltpu.make_async_copy(source, target(place), local.at[len(pieces) + i]))
+        copies[-1].start()
+    for j, (source, target) in enumerate(pieces):
+        wide_ref, narrow_ref, kind, part = casts[j]
+        loads[j].wait()
+        narrow_ref[kind, part] = wide_ref[kind, part].astype(BF)
+        if j < FLIGHT:
+            for k in range(lines - 1):
+                cross(k, j).start()
+        pair(j).start()
+        copies.append(pltpu.make_async_copy(source, target(me), local.at[j]))
+        copies[-1].start()
+
+    def pass_on(j):
+        for k in range(lines - 1):
+            cross(k, j).wait_recv()
+            onward(k, j).start()
+            if j + FLIGHT < len(pieces):
+                cross(k, j + FLIGHT).start()
+
+    passed = 0
+    for hop in range(1, ups + 1):
+        for i in range(len(chunks)):
+            up(hop - 1, i).wait_recv()
+            if hop < ups:
+                up(hop, i).start()
+            if hop <= downs:
+                down(hop - 1, i).wait_recv()
+                if hop < downs:
+                    down(hop, i).start()
+        if passed < len(pieces):
+            pass_on(passed)
+            passed += 1
+    for j in range(passed, len(pieces)):
+        pass_on(j)
+    for j in range(len(pieces)):
+        pair(j).wait()
+        for k in range(lines - 1):
+            cross(k, j).wait_send()
+            onward(k, j).wait()
+    for i in range(len(chunks)):
+        for hop in range(ups):
+            up(hop, i).wait_send()
+        for hop in range(downs):
+            down(hop, i).wait_send()
+    for copy in copies:
+        copy.wait()
+
+
+def gather_all(dp_arrays, dp_pieces, wide_arrays, wide_chunks):
+    dp, wide = lax.axis_size("dp"), lax.axis_size("wide")
+    pieces = 3 * sum(dp_pieces)
+    chunks = sum(wide_chunks)
+    anywhere = pl.BlockSpec(memory_space=pl.ANY)
+    dma = pltpu.SemaphoreType.DMA
+    lines = dp // 2
+    arrays = list(dp_arrays) + list(wide_arrays)
+    shapes = [(dp,) + a.shape for a in dp_arrays] + [(wide,) + a.shape for a in wide_arrays]
+    return pl.pallas_call(
+        functools.partial(gather_kernel, dp, wide, tuple(dp_pieces), tuple(wide_chunks)),
+        out_shape=[
+            jax.ShapeDtypeStruct(s, BF if i < len(dp_arrays) else a.dtype)
+            for i, (s, a) in enumerate(zip(shapes, arrays))
+        ],
+        in_specs=[anywhere] * len(dp_arrays) + [pl.BlockSpec(memory_space=pltpu.VMEM)] * len(wide_arrays),
+        out_specs=[anywhere] * len(arrays),
+        scratch_shapes=[pltpu.VMEM(a.shape, a.dtype) for a in dp_arrays]
+        + [pltpu.VMEM(a.shape, BF) for a in dp_arrays]
+        + [
+            dma((lines - 1, pieces)),
+            dma((lines - 1, pieces)),
+            dma((pieces,)),
+            dma((pieces,)),
+            dma((lines - 1, pieces)),
+            dma((lines - 1, pieces)),
+            dma((wide // 2, chunks)),
+            dma((wide // 2, chunks)),
+            dma((wide - 1 - wide // 2, chunks)),
+            dma((wide - 1 - wide // 2, chunks)),
+            dma((pieces + chunks,)),
+            dma((pieces,)),
+        ],
+        compiler_params=pltpu.CompilerParams(
+            collective_id=0, has_side_effects=True, vmem_limit_bytes=40 << 20
+        ),
+        name="gather_all",
+    )(*arrays)
+
+
+def sum_wide_kernel(wide, x_ref, out_ref, got, whole, s1, r1, s2, r2):
+    me, place = lax.axis_index("dp"), lax.axis_index("wide")
+    step = out_ref.shape[1] // wide
+    barrier = pltpu.get_barrier_semaphore()
+    peers = [lax.rem(place + k, wide) for k in range(1, wide)]
+    for peer in peers:
+        pl.semaphore_signal(barrier, inc=1, device_id=(me, peer), device_id_type=MESH)
+    pl.semaphore_wait(barrier, wide - 1)
+
+    def columns(index):
+        return pl.ds(pl.multiple_of(index * step, step), step)
+
+    def give(k):
+        return pltpu.make_async_remote_copy(
+            src_ref=x_ref.at[:, columns(peers[k - 1])],
+            dst_ref=got.at[k],
+            send_sem=s1.at[k],
+            recv_sem=r1.at[k],
+            device_id=(me, peers[k - 1]),
+            device_id_type=MESH,
+        )
+
+    def spread(k):
+        return pltpu.make_async_remote_copy(
+            src_ref=whole,
+            dst_ref=out_ref.at[:, columns(place)],
+            send_sem=s2.at[k],
+            recv_sem=r2.at[k],
+            device_id=(me, peers[k - 1]),
+            device_id_type=MESH,
+        )
+
+    order = sorted(range(1, wide), key=lambda k: -min(k, wide - k))
+    for k in order:
+        give(k).start()
+    total = x_ref[:, columns(place)].astype(F32)
+    for k in reversed(order):
+        give(k).wait_recv()
+        total = total + got[k].astype(F32)
+    whole[...] = total.astype(BF)
+    for k in order:
+        spread(k).start()
+    out_ref[:, columns(place)] = whole[...]
+    for k in range(1, wide):
+        spread(k).wait()
+        give(k).wait_send()
+
+
+def sum_wide(x, collective_id):
+    wide = lax.axis_size("wide")
+    rows, span = x.shape
+    vmem = pl.BlockSpec(memory_space=pltpu.VMEM)
+    dma = pltpu.SemaphoreType.DMA
+    return pl.pallas_call(
+        functools.partial(sum_wide_kernel, wide),
+        out_shape=jax.ShapeDtypeStruct((rows, span), BF),
+        in_specs=[vmem],
+        out_specs=vmem,
+        scratch_shapes=[
+            pltpu.VMEM((wide, rows, span // wide), x.dtype),
+            pltpu.VMEM((rows, span // wide), BF),
+            dma((wide,)),
+            dma((wide,)),
+            dma((wide,)),
+            dma((wide,)),
+        ],
+        compiler_params=pltpu.CompilerParams(
+            collective_id=collective_id, has_side_effects=True, vmem_limit_bytes=32 << 20
+        ),
+        name="sum_wide",
+    )(x)
+
+
 def contract(left, right, left_dim, right_dim):
     return lax.dot_general(
         left, right, (((left_dim,), (right_dim,)), ((), ())), preferred_element_type=F32
@@ -182,6 +449,40 @@
         grad.reshape(parts, 3, rows, grad.shape[1]), "dp", scatter_dimension=0, tiled=False
     )
     return jnp.transpose(kept, (1, 0, 2))
+
+
+def hop(block, flip):
+    devices = lax.axis_size("dp")
+    return lax.ppermute(block, "dp", [(d, flip(d)) for d in range(devices)])
+
+
+def from_partners(block):
+    lines = lax.axis_size("dp") // 2
+    blocks = [block, hop(block, lambda d: d ^ 1)]
+    for k in range(1, lines):
+        far = hop(block, lambda d: (d // 2 + k) % lines * 2 + d % 2)
+        blocks += [far, hop(far, lambda d: d ^ 1)]
+    return blocks
+
+
+def swap_features(rows):
+    devices = lax.axis_size("dp")
+    lines = devices // 2
+    depth = rows.shape[1] // devices
+    me = lax.axis_index("dp")
+
+    def part(owner):
+        return lax.dynamic_slice_in_dim(rows, owner * depth, depth, 1)
+
+    core = me % 2
+    blocks = [part(me), hop(part(me + 1 - 2 * core), lambda d: d ^ 1)]
+    for k in range(1, lines):
+        line = (me // 2 + k) % lines
+        blocks.append(hop(part(line * 2 + core), lambda d: (d // 2 + k) % lines * 2 + d % 2))
+        blocks.append(
+            hop(part(line * 2 + 1 - core), lambda d: (d // 2 + k) % lines * 2 + 1 - d % 2)
+        )
+    return blocks
 
 
 def halves_out(block, wide):
@@ -242,16 +543,31 @@
     scale = lax.rsqrt(jnp.mean(x_in * x_in, axis=1, keepdims=True) + EPSILON)
     normed = (x_in * scale * norm_gain[None, :]).astype(BF)
     d_branch = jnp.where(alive_here[:, None], cotangent, 0.0).astype(BF)
-    w_in = gather_master(in_master)
-    normed_all = lax.all_gather(normed, "wide", axis=0, tiled=True)
-    kinds_all = lax.all_gather(modality, "wide", axis=0, tiled=True)
-    w_x = gather_master(xproj_master)
-    w_dt = gather_master(dtproj_master)
+    rank_rows, step_rows = xproj_master.shape[0], dtproj_master.shape[0]
+    small = jnp.concatenate([xproj_master, dtproj_master], axis=0)
+    small = jnp.pad(small, ((0, -small.shape[0] % 16), (0, 0), (0, 0)))
+    w_in, w_small, normed_all, kinds_all = gather_all(
+        [jnp.transpose(in_master, (1, 0, 2)), jnp.transpose(small, (1, 0, 2))],
+        [2, 1],
+        [normed, jnp.broadcast_to(modality[None], (8, count))],
+        [2, 1],
+    )
+    w_in = w_in.reshape(-1, in_master.shape[2])
+    normed_all = normed_all.reshape(span, -1)
+    kinds_all = kinds_all[:, 0].reshape(span)
+    w_x_kinds = w_small[:, :, :rank_rows].transpose(1, 0, 2, 3).reshape(3, -1, channels)
+    w_dt_kinds = w_small[:, :, rank_rows : rank_rows + step_rows].transpose(1, 0, 2, 3)
+    w_dt_kinds = w_dt_kinds.reshape(3, DT_RANK, channels)
     w_out = gather_master(out_master)
     d_branch_all = lax.all_gather(d_branch, "wide", axis=0, tiled=True)
     kinds = (kinds_all[:, None] == jnp.arange(3, dtype=jnp.int32)[None, :]) & living[:, None]
 
     normed_kinds = split_kinds(normed_all, kinds, dp)
+    kinds_parts = from_partners(kinds.astype(BF))
+    feature_kinds = [
+        split_kinds(rows, tags > 0, 1)
+        for rows, tags in zip(swap_features(normed_all), kinds_parts)
+    ]
     mixed = contract(normed_kinds, w_in, 1, 0).astype(BF)
     xs, z = halves_out(mixed, wide)
 
@@ -266,20 +582,20 @@
         )
     inner = jax.nn.silu(pre).astype(BF)
 
-    rank = xproj_master.shape[0] * dp
-    w_x_kinds = w_x.reshape(dp, 3, rank // dp, channels).transpose(1, 0, 2, 3).reshape(3, rank, channels)
-    by_kind = contract(inner, w_x_kinds.reshape(3 * rank, channels), 1, 1).reshape(span, 3, rank)
-    proj = lax.psum(jnp.sum(jnp.where(kinds[:, :, None], by_kind, 0.0), axis=1), "wide")
-    rates = proj[:, :DT_RANK].astype(BF)
-    maps = proj[:, DT_RANK:].astype(BF).astype(F32)
-    rates_kinds = split_kinds(rates, kinds, dp)
+    rank = w_x_kinds.shape[1]
+    across = kinds.T[:, None, :]
+    by_kind = contract(w_x_kinds.reshape(3 * rank, channels), inner, 1, 1).reshape(3, rank, span)
+    proj = sum_wide(jnp.sum(jnp.where(across, by_kind, 0.0), axis=0), 1)
+    rates = proj[:DT_RANK].T
+    maps = proj[DT_RANK:].astype(F32)
+    rates_kinds = split_kinds(rates, kinds, 1)
     bias = jnp.where(kinds[:, :, None], dt_bias.astype(BF).astype(F32)[None], 0.0).sum(axis=1)
-    dtp = (contract(rates_kinds, w_dt, 1, 0) + bias).astype(BF)
+    dtp = (contract(rates_kinds, w_dt_kinds.reshape(3 * DT_RANK, channels), 1, 0) + bias).astype(BF)
 
     blocks = span // STEPS
-    to_columns = lambda rows: rows.reshape(blocks, STEPS, -1).transpose(0, 2, 1)
-    b_columns = to_columns(maps[:, :STATE])
-    c_columns = to_columns(maps[:, STATE:])
+    to_columns = lambda rows: rows.reshape(-1, blocks, STEPS).transpose(1, 0, 2)
+    b_columns = to_columns(maps[:STATE])
+    c_columns = to_columns(maps[STATE:])
     keep = masks[1][:, None]
     a_own = own(a_log)
     skip_own = own(d_skip)[None, :]
@@ -301,25 +617,22 @@
         dtp, inner, b_columns, c_columns, keep, a_own, skip_own, z, y_value, d_gated, heads
     )
     d_dtp = jnp.where(living[:, None], d_dtp, jnp.zeros((), BF))
-    d_maps = d_columns.transpose(0, 2, 1).reshape(span, 2 * STATE)
-    d_rates = jnp.zeros((span, DT_RANK), F32)
-    w_dt_kinds = w_dt.reshape(dp, 3, -1, channels)
-    d_dtp_kinds = split_kinds(d_dtp, kinds, 1)
-    for kind in range(3):
-        picked = jnp.where(kinds[:, kind : kind + 1], d_dtp, jnp.zeros((), BF))
-        d_rates = d_rates + contract(picked, w_dt_kinds[:, kind].reshape(-1, channels), 1, 1)
-    d_proj = lax.psum(jnp.concatenate([d_rates, d_maps], axis=1), "wide")
-    d_proj = jnp.where(living[:, None], d_proj, 0.0).astype(BF)
-    grad_dt = contract(rates_kinds, d_dtp, 0, 0)
+    d_maps = d_columns.transpose(1, 0, 2).reshape(2 * STATE, span)
+    by_kind = contract(w_dt_kinds.reshape(3 * DT_RANK, channels), d_dtp, 1, 1)
+    d_rates = jnp.sum(jnp.where(across, by_kind.reshape(3, DT_RANK, span), 0.0), axis=0)
+    d_proj = sum_wide(jnp.concatenate([d_rates, d_maps], axis=0), 2)
+    d_proj = jnp.where(living[None], d_proj, jnp.zeros((), BF)).T
+    grad_dt = contract(rates_kinds, d_dtp, 0, 0).reshape(3, dp, step_rows, channels)
+    grad_dt = grad_dt.transpose(1, 0, 2, 3).reshape(-1, channels)
     bias_part = jnp.stack(
         [jnp.sum(jnp.where(kinds[:, k : k + 1], d_dtp.astype(F32), 0.0), axis=0) for k in range(3)]
     )
     d_proj_kinds = split_kinds(d_proj, kinds, 1)
     d_inner = contract(d_proj_kinds, w_x_kinds.reshape(3 * rank, channels), 1, 0).astype(BF)
     grad_x = contract(d_proj_kinds, inner, 0, 0)
-    grad_x = grad_x.reshape(3, dp, rank // dp, channels).transpose(1, 0, 2, 3).reshape(-1, channels)
-    xproj_grad = scatter_master(grad_x, rank // dp)
-    dtproj_grad = scatter_master(grad_dt, dtproj_master.shape[0])
+    grad_x = grad_x.reshape(3, dp, rank_rows, channels).transpose(1, 0, 2, 3).reshape(-1, channels)
+    xproj_grad = scatter_master(grad_x, rank_rows)
+    dtproj_grad = scatter_master(grad_dt, step_rows)
 
     d_pre = (d_inner.astype(F32) + d_scan) * silu_slope(pre)
     further = jnp.concatenate([d_pre, jnp.zeros((width - 1, channels), F32)], axis=0)
@@ -337,8 +650,12 @@
     d_xs = jnp.where(living[:, None], d_xs, 0.0).astype(BF)
     d_z = jnp.where(living[:, None], d_z, jnp.zeros((), BF))
     d_mixed = halves_back(d_xs, d_z, wide)
-    grad_in = contract(normed_kinds, d_mixed, 0, 0)
-    in_grad = scatter_master(grad_in.astype(BF), in_master.shape[0]).astype(F32)
+    mixed_parts = from_partners(d_mixed)
+    grad_in = 0.0
+    for pair in range(0, dp, 2):
+        left = jnp.concatenate(feature_kinds[pair : pair + 2], axis=0)
+        grad_in = grad_in + contract(left, jnp.concatenate(mixed_parts[pair : pair + 2], axis=0), 0, 0)
+    in_grad = jnp.transpose(grad_in.reshape(3, -1, d_mixed.shape[1]), (1, 0, 2))
 
     d_normed = jnp.zeros((span, x_in.shape[1]), F32)
     w_in_kinds = w_in.reshape(dp, 3, -1, w_in.shape[1])

time: 1000 us -> 769 us (0.77)
  waiting for transfers between devices: 403 us -> 87.3 us
  Pallas kernels: 123 us -> 273 us
  blocking collectives: 222 us -> 132 us
  starting transfers between devices: 13.8 us -> 34 us
  local copies, waits for them, and re-layouts: 50.8 us -> 66.4 us
    reduce_scatter x3 -> x1, waiting for transfers between devices: 178 us -> 3.94 us  [scatter_master(): lax.psum_scatter(grad.reshape(parts, 3, rows, grad.shape[1]), 'dp', scatt...]
    pallas_call x0 -> x3, Pallas kernels: none -> 149 us  [the longest x1 96.3 us: gather_all(): pl.pallas_call(functools.partial(gather_kernel, dp, wide, tuple(dp_pieces...]
    all_gather x2 -> x1, waiting for transfers between devices: 103 us -> 0.01 us  [gather_master(): lax.all_gather(jnp.transpose(master.astype(BF), (1, 0, 2)), 'dp', axis=0)]
    psum x2 -> x0, blocking collectives: 94.3 us -> none  [the longest x1 51 us: body(): lax.psum(jnp.sum(jnp.where(kinds[:, :, None], by_kind, 0.0), axis=1), 'wi...]
    all_gather x1, waiting for transfers between devices: 68 us -> 0.01 us  [body(): d_branch_all = lax.all_gather(d_branch, 'wide', axis=0, tiled=True)]
    ppermute x1, waiting for transfers between devices: 0.01 us -> 36.6 us  [halves_out(): got_b = lax.ppermute(jnp.where(low, second, first), 'wide', odd)]
    psum x1, blocking collectives: 11.1 us -> 47.4 us  [body(): shared = lax.psum(shared, 'dp')]
    all_gather x3 -> x0, blocking collectives: 35.5 us -> none  [the longest x1 20.8 us: body(): kinds_all = lax.all_gather(modality, 'wide', axis=0, tiled=True)]
  transfers between devices with their start and end apart: 14 -> 19, of which waited for: 9 -> 6; matrix products, arithmetic and copies ran while one was open for 18% -> 24% of each run, Pallas kernels for 0% -> 19%
where the time goes in v2:
time: 769 us; the launch traced here: 762 us
  Pallas kernels  273 us (36%)
  blocking collectives  132 us (17%)
  matrix products  106 us (14%)
  waiting for transfers between devices  87.3 us (11%)
  local copies, waits for them, and re-layouts  66.4 us (9%)
  other arithmetic  48 us (6%)
  starting transfers between devices  34 us (4%)
  between operations  15.6 us (2%)
    dot_general x17, matrix products, contract(): lax.dot_general(left, right, (((left_dim,), (right_dim,)), ((), ())), pre...  106 us
    pallas_call x1, Pallas kernels, scan_backward(): pl.pallas_call(scan_backward_kernel, grid=(nb,), in_specs=[row, row, col,...  105 us
    pallas_call x1, Pallas kernels, gather_all(): pl.pallas_call(functools.partial(gather_kernel, dp, wide, tuple(dp_pieces...  96.3 us
    pallas_call x2, Pallas kernels, sum_wide(): pl.pallas_call(functools.partial(sum_wide_kernel, wide), out_shape=jax.Sh...  53.1 us
    psum x1, blocking collectives, body(): shared = lax.psum(shared, 'dp')  47.4 us
    all_gather x1, blocking collectives, body(): lax.all_gather(shared[:width + STATE + 2], 'wide', axis=1, tiled=True)  47.3 us
    psum x1, blocking collectives, body(): gain_grad = lax.psum(gain_part, ('dp', 'wide'))  37.5 us
    ppermute x1, waiting for transfers between devices, halves_out(): got_b = lax.ppermute(jnp.where(low, second, first), 'wide', odd)  36.6 us
  transfers between devices with their start and end apart: 19, of which 6 were waited for; matrix products, arithmetic and copies ran while one was open for 24% of the time, Pallas kernels for 19%

profile of v2, /device:TPU:0, one launch (start us, length us, event | category | flops | bytes accessed | tf_op | source)
XLA Modules:
  0.0 762.2 jit_solution(6554014270125731785)
XLA Ops:
  9.3 2.2 select_convert_fusion
  11.6 3.4 convert_bitcast_fusion.1
  16.6 2.8 copy-done.6
  19.3 96.3 %gather_all.1 = (bf16[4,3,512,1024]{3,2,1,0:T(8,128)(2,1)}, bf16[4,3,80,512]{3,2,1,0:T(8,128)(2,1)S(1)}, bf16[8,128,2048]{2,1,0:T(8,128)(2,1)S(1)}, s32[8,8,128]{2,1,0:T(8,128)S(1)}) custom-call(f32[3,512,1024]{2,1,0:T(8,128)S(1)} %bitcast.141, f32[3,80,512]{2,1,0:T(8,128)S(1)} %fusion.72.refs_1_, bf16[128,2048]{1,0:T(8,128)(2,1)S(1)} %multiply_convert_fusion.1.refs_2_, ...), custom_call_target="tpu_custom_call" | custom-call | tf_op jit(solution)/shard_map/gather_all/pallas_call | solution.py:307
  115.7 2.0 copy-done.2
  117.7 7.8 %broadcast_in_dim.354 = bf16[1024,4,512]{2,1,0:T(4,128)(2,1)} reshape(bf16[8,128,2048]{2,1,0:T(8,128)(2,1)} %copy-done.2) | data formatting | bytes 8388608 | tf_op jit(solution)/shard_map/jit(_where)/broadcast_in_dim | solution.py:438
  125.6 7.7 %copy.88 = bf16[1024,4,512]{0,2,1:T(8,128)(2,1)} copy(bf16[1024,4,512]{2,1,0:T(4,128)(2,1)} %broadcast_in_dim.354) | data formatting | bytes 8388608 | tf_op jit(solution)/shard_map/jit(_where)/broadcast_in_dim | solution.py:438
  133.9 18.0 %bitcast_convert_fusion = bf16[1024,1024]{1,0:T(8,128)(2,1)S(1)} fusion(bf16[4,3,512,1024]{3,2,1,0:T(8,128)(2,1)} %get-tuple-element.28, pred[1024,3]{0,1:T(4,128)(4,1)S(1)} %get-tuple-element.62, bf16[1024,4,512]{0,2,1:T(8,128)(2,1)} %copy.88), kind=kOutput, calls=%fused_computation.27 | convolution fusion | flops 12892241920 | bytes 18877440 | tf_op jit(solution)/shard_map/dot_general | solution.py:412
  153.0 16.5 %collective-permute-start.1 = (bf16[1024,512]{1,0:T(8,128)(2,1)}, bf16[1024,512]{1,0:T(8,128)(2,1)}, u32[]{:S(2)}, u32[]{:S(2)}) collective-permute-start(bf16[1024,512]{1,0:T(8,128)(2,1)} %get-tuple-element.84), channel_id=1, source_target_pairs={{0,1},{1,3},{2,5},{3,7},{4,0},{5,2},{6,4},{7,6},{8,9},{9,11},{10,1... | collective-permute-start | bytes 3145736 | tf_op jit(solution)/shard_map/ppermute | solution.py:496
  169.6 2.1 collective-permute-start
  176.8 2.1 select_reduce_fusion
  178.9 36.6 %collective-permute-done.1 = bf16[1024,512]{1,0:T(8,128)(2,1)} collective-permute-done((bf16[1024,512]{1,0:T(8,128)(2,1)}, bf16[1024,512]{1,0:T(8,128)(2,1)}, u32[]{:S(2)}, u32[]{:S(2)}) %collective-permute-start.1) | collective-permute-done | bytes 1048608 | tf_op jit(solution)/shard_map/ppermute | solution.py:496
  215.4 1.7 broadcast_select_fusion.13
  217.2 2.8 multiply_convert_fusion
  220.7 28.5 %sum_wide.2 = bf16[160,1024]{1,0:T(8,128)(2,1)S(1)} custom-call(f32[160,1024]{1,0:T(8,128)S(1)} %select_reduce_fusion.1.x_ref), custom_call_target="tpu_custom_call" | custom-call | tf_op jit(solution)/shard_map/sum_wide/pallas_call | solution.py:391
  251.3 1.6 copy-done.22
  252.9 1.8 add_convert_fusion.2.dtp_ref
  254.8 18.6 %scan_forward.1 = (bf16[1024,512]{1,0:T(8,128)(2,1)S(1)}, f32[1024,512]{1,0:T(8,128)}, f32[64,16,512]{2,1,0:T(8,128)}) custom-call(bf16[1024,512]{1,0:T(8,128)(2,1)S(1)} %add_convert_fusion.2.dtp_ref, bf16[1024,512]{1,0:T(8,128)(2,1)S(1)} %get-tuple-element.66.u_ref, f32[64,16,16]{2,1,0:T(8,128)S(1)} %bitcast.142, f32[64,16,16]{2,1,0:T(8,128)S(1)} %bitcast.144, ...), custom_call_target="tpu_custom_call" | custom-call | tf_op jit(solution)/shard_map/scan_forward/pallas_call | solution.py:55
  274.3 6.4 copy.111
  280.7 11.5 %bitcast_convert_fusion.1.dg_ref = bf16[1024,512]{1,0:T(8,128)(2,1)} fusion(bf16[4,3,512,512]{3,2,1,0:T(8,128)(2,1)} %bitcast.155, pred[1024,3]{0,1:T(4,128)(4,1)S(1)} %get-tuple-element.62, bf16[1024,4,512]{0,2,1:T(8,128)(2,1)} %bitcast.149), kind=kOutput, calls=%fused_computation.51 | convolution fusion | flops 6449266688 | bytes 11537408 | tf_op jit(solution)/shard_map/dot_general | solution.py:412
  292.2 104.6 %scan_backward.1 = (bf16[1024,512]{1,0:T(8,128)(2,1)S(1)}, f32[1024,512]{1,0:T(8,128)}, bf16[1024,512]{1,0:T(8,128)(2,1)S(1)}, f32[64,32,16]{2,1,0:T(8,128)S(1)}...) custom-call(bf16[1024,512]{1,0:T(8,128)(2,1)S(1)} %add_convert_fusion.2.dtp_ref, bf16[1024,512]{1,0:T(8,128)(2,1)} %copy-done.3, ...), custom_call_target="tpu_custom_call" | custom-call | tf_op jit(solution)/shard_map/scan_backward/pallas_call | solution.py:137
  399.0 1.2 copy.99
  400.2 1.9 select_reduce_fusion.2
  402.1 24.6 %sum_wide.3 = bf16[160,1024]{1,0:T(8,128)(2,1)S(1)} custom-call(f32[160,1024]{1,0:T(8,128)S(1)} %pad_maximum_fusion.1.x_ref), custom_call_target="tpu_custom_call" | custom-call | tf_op jit(solution)/shard_map/sum_wide/pallas_call | solution.py:391
  429.0 2.5 multiply_reduce_fusion
  431.4 2.9 broadcast_select_fusion.12
  434.4 9.5 %collective-permute-start.2 = (bf16[1024,512]{1,0:T(8,128)(2,1)}, bf16[1024,512]{1,0:T(8,128)(2,1)}, u32[]{:S(2)}, u32[]{:S(2)}) collective-permute-start(bf16[1024,512]{1,0:T(8,128)(2,1)} %get-tuple-element.64), channel_id=1, source_target_pairs={{0,0},{2,1},{4,2},{6,3},{1,4},{3,5},{5,6},{7,7},{8,8},{10,9},{12,1... | collective-permute-start | bytes 3145736 | tf_op jit(solution)/shard_map/ppermute | solution.py:507
  443.9 1.2 broadcast_select_fusion.11
  445.1 4.8 fusion.98
  449.9 1.6 convolution_bitcast_fusion.1
  451.4 1.6 convolution_bitcast_fusion
  453.1 13.7 %collective-permute-done.3 = bf16[1024,512]{1,0:T(8,128)(2,1)} collective-permute-done((bf16[1024,512]{1,0:T(8,128)(2,1)}, bf16[1024,512]{1,0:T(8,128)(2,1)}, u32[]{:S(2)}, u32[]{:S(2)}) %collective-permute-start.3) | collective-permute-done | bytes 1048608 | tf_op jit(solution)/shard_map/ppermute | solution.py:508
  466.8 1.7 broadcast_select_fusion.8
  468.6 6.9 fusion.40
  475.5 6.9 fusion.38
  482.3 10.0 %add_convert_fusion = bf16[1024,2048]{1,0:T(8,128)(2,1)} fusion(f32[1024,2048]{1,0:T(8,128)} %fusion.40, f32[1024,2048]{1,0:T(8,128)} %fusion.38, bf16[2048,1024]{1,0:T(8,128)(2,1)S(1)} %bitcast.158, pred[1024]{0:T(1024)(128)(4,1)S(1)} %get-tuple-element.48, bf16[1024,512]{1,0:T(8,128)(2,1)S(1)} %get-tuple-element.81, ...), kind=kOutput, calls=%fused_computation.5 | convolution fusion | flops 4306501632 | bytes 27264000 | tf_op jit(solution)/shard_map/dot_general | solution.py:412
  492.6 3.3 fusion.99
  495.9 2.4 fusion.62
  498.3 5.7 fusion.60
  504.0 6.7 add_convert_fusion.1
  510.8 4.2 broadcast_select_fusion
  515.0 8.8 %convolution_convert_fusion = bf16[6144,512]{1,0:T(8,128)(2,1)} fusion(bf16[1024,6144]{0,1:T(8,128)(2,1)S(1)} %bitcast.153, bf16[1024,512]{1,0:T(8,128)(2,1)S(1)} %copy-done.14), kind=kOutput, calls=%fused_computation.4 | convolution fusion | flops 6445596672 | bytes 19922944 | tf_op jit(solution)/shard_map/dot_general | solution.py:412
  525.0 4.0 constant_dynamic-slice_fusion.1
  532.3 1.9 broadcast_select_fusion.4
  534.2 1.6 pad_maximum_fusion
  538.2 1.5 copy.102
  539.7 14.7 %collective-permute-done.10 = bf16[1024,512]{1,0:T(8,128)(2,1)} collective-permute-done((bf16[1024,512]{1,0:T(8,128)(2,1)}, bf16[1024,512]{1,0:T(8,128)(2,1)}, u32[]{:S(2)}, u32[]{:S(2)}) %collective-permute-start.10) | collective-permute-done | bytes 1048608 | tf_op jit(solution)/shard_map/ppermute | solution.py:456
  554.5 1.5 copy.104
  556.0 1.9 broadcast_select_fusion.3
  558.9 1.9 broadcast_select_fusion.1
  560.7 17.1 %collective-permute-done.8 = bf16[1024,512]{1,0:T(8,128)(2,1)} collective-permute-done((bf16[1024,512]{1,0:T(8,128)(2,1)}, bf16[1024,512]{1,0:T(8,128)(2,1)}, u32[]{:S(2)}, u32[]{:S(2)}) %collective-permute-start.8) | collective-permute-done | bytes 1048608 | tf_op jit(solution)/shard_map/ppermute | solution.py:456
  577.9 1.5 copy.103
  579.4 1.9 broadcast_select_fusion.2
  582.5 47.4 %psum.15 = f32[25,512]{1,0:T(8,128)S(1)} all-reduce(f32[25,512]{1,0:T(8,128)S(1)} %concatenate.35), channel_id=1, replica_groups=mesh['dp'=4,'wide'=8] {'dp'}, use_global_device_ids=true, to_apply=%region_26.27 | all-reduce | flops 12800 | bytes 102400 | tf_op jit(solution)/shard_map/psum | solution.py:676
  629.9 47.3 %all_gather.15 = f32[22,4096]{1,0:T(8,128)S(1)} all-gather(f32[22,512]{1,0:T(8,128)S(1)} %slice.169), channel_id=1, replica_groups=mesh['dp'=4,'wide'=8] {'wide'}, dimensions={1}, use_global_device_ids=true | all-gather | bytes 405504 | tf_op jit(solution)/shard_map/all_gather | solution.py:677
  679.8 2.3 dynamic-slice_bitcast_fusion.1
  682.0 2.3 dynamic-slice_bitcast_fusion
  684.4 10.5 %fusion.3 = f32[1536,1024]{1,0:T(8,128)S(1)} fusion(bf16[1024,1536]{0,1:T(8,128)(2,1)} %bitcast.162, bf16[1024,1536]{0,1:T(8,128)(2,1)} %bitcast.161, bf16[1024,1024]{1,0:T(8,128)(2,1)} %collective-permute-done.6, bf16[1024,512]{1,0:T(8,128)(2,1)S(1)} %copy-done.28, bf16[1024,512]{1,0:T(8,128)(2,1)S(1)} %copy-done.25), kind=kOutput, calls=%fused_computation.7 | convolution fusion | flops 6467616768 | bytes 16777216 | tf_op jit(solution)/shard_map/dot_general | solution.py:412
  694.9 10.6 %fusion.13 = f32[1536,1024]{1,0:T(8,128)} fusion(f32[1536,1024]{1,0:T(8,128)S(1)} %fusion.3, bf16[1024,1536]{0,1:T(8,128)(2,1)S(1)} %bitcast.163, bf16[1024,1536]{0,1:T(8,128)(2,1)S(1)} %bitcast.164, bf16[1024,1024]{1,0:T(8,128)(2,1)} %collective-permute-done.12, bf16[1024,1024]{1,0:T(8,128)(2,1)} %collective-permute-done.11), kind=kOutput, calls=%fused_computation.18 | convolution fusion | flops 6464995328 | bytes 23068672 | tf_op jit(solution)/shard_map/dot_general | solution.py:412
  705.5 1.5 fusion.51
  707.0 37.5 %psum.14 = f32[2048]{0:T(1024)} all-reduce(f32[2048]{0:T(1024)S(1)} %get-tuple-element.43), channel_id=1, replica_groups=mesh['dp'=4,'wide'=8] {'dp','wide'}, use_global_device_ids=true, to_apply=%region_17.18 | all-reduce | flops 2048 | bytes 16384 | tf_op jit(solution)/shard_map/psum | solution.py:678
  744.5 2.9 fusion.49
  747.4 3.9 reduce-scatter.12.cloned.1.call-done
  751.4 3.5 convert_bitcast_fusion
  (201 shorter events, 30.7 us)
Async XLA Ops:
  7.2 164.5 %copy-start = (f32[16,4096]{1,0:T(8,128)S(1)}, f32[16,4096]{1,0:T(8,128)}, u32[]{:S(2)}) copy-start(f32[16,4096]{1,0:T(8,128)} %param.20) | copy-start | bytes 786436
  7.2 267.1 %all-gather.4.cloned.1.call-start = ((), (), s32[]{:S(2)}) async-start(), calls=%async_computation.4 | async-start | bytes 4718592 | tf_op jit(solution)/shard_map/all_gather | solution.py:562
  11.5 3.5 copy-start.40
  11.5 3.5 copy-start.41
  11.5 269.2 %all-gather.6.cloned.1.call-start = ((), (), s32[]{:S(2)}) async-start(), calls=%async_computation.7 | async-start | bytes 7864320 | tf_op jit(solution)/shard_map/all_gather | solution.py:442
  15.0 664.8 %all-reduce.8.cloned.1.call-start = ((), (), s32[]{:S(2)}) async-start(), calls=%async_computation.8 | async-start | bytes 3538944
  16.4 99.3 %copy-start.45 = (f32[128]{0:T(128)}, f32[128]{0:T(128)S(1)}, u32[]{:S(2)}) copy-start(f32[128]{0:T(128)S(1)} %add_rsqrt_fusion) | copy-start | bytes 1540
  16.6 2.8 copy-start.6
  115.7 2.1 copy-start.2
  153.0 62.4 %collective-permute-start.1 = (bf16[1024,512]{1,0:T(8,128)(2,1)}, bf16[1024,512]{1,0:T(8,128)(2,1)}, u32[]{:S(2)}, u32[]{:S(2)}) collective-permute-start(bf16[1024,512]{1,0:T(8,128)(2,1)} %get-tuple-element.84), channel_id=1, source_target_pairs={{0,1},{1,3},{2,5},{3,7},{4,0},{5,2},{6,4},{7,6},{8,9},{9,11},{10,1... | collective-permute-start | bytes 3145736 | tf_op jit(solution)/shard_map/ppermute | solution.py:496
  169.6 45.9 %collective-permute-start = (bf16[1024,512]{1,0:T(8,128)(2,1)S(1)}, bf16[1024,512]{1,0:T(8,128)(2,1)}, u32[]{:S(2)}, u32[]{:S(2)}) collective-permute-start(bf16[1024,512]{1,0:T(8,128)(2,1)S(1)} %get-tuple-element.85), channel_id=1, source_target_pairs={{0,0},{1,2},{2,4},{3,6},{4,1},{5,3},{6,5},{7,7},{8,8},{9,10},{10,1... | collective-permute-start | bytes 3145736 | tf_op jit(solution)/shard_map/ppermute | solution.py:495
  172.0 4.7 copy-start.44
  173.1 46.9 %copy-start.38 = (bf16[3,4,40,512]{3,2,1,0:T(8,128)(2,1)}, bf16[3,4,40,512]{3,2,1,0:T(8,128)(2,1)S(1)}, u32[]{:S(2)}) copy-start(bf16[3,4,40,512]{3,2,1,0:T(8,128)(2,1)S(1)} %copy.87) | copy-start | bytes 1474564
  217.2 2.8 copy-start.17
  217.2 37.5 %copy-start.5 = (bf16[1024,512]{1,0:T(8,128)(2,1)}, bf16[1024,512]{1,0:T(8,128)(2,1)S(1)}, u32[]{:S(2)}) copy-start(bf16[1024,512]{1,0:T(8,128)(2,1)S(1)} %get-tuple-element.82.z_ref) | copy-start | bytes 3145732
  220.0 34.7 %copy-start.3 = (bf16[1024,512]{1,0:T(8,128)(2,1)}, bf16[1024,512]{1,0:T(8,128)(2,1)S(1)}, u32[]{:S(2)}) copy-start(bf16[1024,512]{1,0:T(8,128)(2,1)S(1)} %get-tuple-element.66.u_ref) | copy-start | bytes 3145732
  250.8 2.1 copy-start.22
  251.1 3.6 copy-start.11
  251.3 3.5 copy-start.35
  252.9 1.9 copy-start.7
  252.9 1.9 copy-start.9
  280.7 11.5 %copy-start.8 = (f32[1024,1]{1,0:T(8,128)S(1)}, f32[1024,1]{1,0:T(8,128)}, u32[]{:S(2)}) copy-start(f32[1024,1]{1,0:T(8,128)} %fusion.71.keep_ref) | copy-start | bytes 12292
  280.7 11.5 %copy-start.10 = (f32[16,64,16]{2,0,1:T(8,128)S(1)}, f32[16,64,16]{2,0,1:T(8,128)}, u32[]{:S(2)}) copy-start(f32[16,64,16]{2,0,1:T(8,128)} %copy.127) | copy-start | bytes 196612
  280.7 11.5 %copy-start.12 = (f32[16,64,16]{2,0,1:T(8,128)S(1)}, f32[16,64,16]{2,0,1:T(8,128)}, u32[]{:S(2)}) copy-start(f32[16,64,16]{2,0,1:T(8,128)} %copy-done.11) | copy-start | bytes 196612
  397.8 2.3 copy-start.16
  400.2 44.9 %slice-start = ((s8[12582912]{0:T(1024)(128)(4,1)}), s8[4194304]{0:T(1024)(128)(4,1)S(1)}, s32[]{:S(2)}) async-start(s8[12582912]{0:T(1024)(128)(4,1)} %bitcast.151), calls=%async_computation.9 | async-start | bytes 8388608
  402.1 24.8 %copy-start.39 = (bf16[3,4,40,512]{3,2,1,0:T(8,128)(2,1)S(1)}, bf16[3,4,40,512]{3,2,1,0:T(8,128)(2,1)}, u32[]{:S(2)}) copy-start(bf16[3,4,40,512]{3,2,1,0:T(8,128)(2,1)} %copy-done.38) | copy-start | bytes 1474564
  402.1 25.6 %copy-start.37 = (f32[1024,512]{1,0:T(8,128)S(1)}, f32[1024,512]{1,0:T(8,128)}, u32[]{:S(2)}) copy-start(f32[1024,512]{1,0:T(8,128)} %get-tuple-element.34) | copy-start | bytes 6291460
  426.8 2.2 copy-start.21
  426.9 18.2 %slice-start.1 = ((s8[12582912]{0:T(1024)(128)(4,1)}), s8[4194304]{0:T(1024)(128)(4,1)S(1)}, s32[]{:S(2)}) async-start(s8[12582912]{0:T(1024)(128)(4,1)} %bitcast.151), calls=%async_computation.10 | async-start | bytes 8388608
  429.0 16.1 %slice-start.2 = ((s8[12582912]{0:T(1024)(128)(4,1)}), s8[4194304]{0:T(1024)(128)(4,1)S(1)}, s32[]{:S(2)}) async-start(s8[12582912]{0:T(1024)(128)(4,1)} %bitcast.151), calls=%async_computation.11 | async-start | bytes 8388608
  434.4 18.7 %collective-permute-start.2 = (bf16[1024,512]{1,0:T(8,128)(2,1)}, bf16[1024,512]{1,0:T(8,128)(2,1)}, u32[]{:S(2)}, u32[]{:S(2)}) collective-permute-start(bf16[1024,512]{1,0:T(8,128)(2,1)} %get-tuple-element.64), channel_id=1, source_target_pairs={{0,0},{2,1},{4,2},{6,3},{1,4},{3,5},{5,6},{7,7},{8,8},{10,9},{12,1... | collective-permute-start | bytes 3145736 | tf_op jit(solution)/shard_map/ppermute | solution.py:507
  445.1 4.8 copy-start.36
  445.1 21.8 %collective-permute-start.3 = (bf16[1024,512]{1,0:T(8,128)(2,1)}, bf16[1024,512]{1,0:T(8,128)(2,1)}, u32[]{:S(2)}, u32[]{:S(2)}) collective-permute-start(bf16[1024,512]{1,0:T(8,128)(2,1)} %broadcast_select_fusion.11), channel_id=1, source_target_pairs={{1,0},{3,1},{5,2},{7,3},{0,4},{2,5},{4,6},{6,7},{9,8},{11,9},{13,1... | collective-permute-start | bytes 3145736 | tf_op jit(solution)/shard_map/ppermute | solution.py:508
  453.1 252.4 %reduce-scatter.10.cloned.1.call-start = ((), (), s32[]{:S(2)}) async-start(), calls=%async_computation.5 | async-start | bytes 4718592 | tf_op jit(solution)/shard_map/reduce_scatter | solution.py:667
  453.1 15.4 %copy-start.32 = (bf16[4,1,512,1024]{3,2,1,0:T(8,128)(2,1)S(1)}, bf16[4,1,512,1024]{3,2,1,0:T(8,128)(2,1)}, u32[]{:S(2)}) copy-start(bf16[4,1,512,1024]{3,2,1,0:T(8,128)(2,1)} %get-tuple-element.72) | copy-start | bytes 12582916
  468.5 13.8 %copy-start.23 = (bf16[1024,512]{1,0:T(8,128)(2,1)}, bf16[1024,512]{1,0:T(8,128)(2,1)S(1)}, u32[]{:S(2)}) copy-start(bf16[1024,512]{1,0:T(8,128)(2,1)S(1)} %get-tuple-element.80) | copy-start | bytes 3145732
  468.6 13.8 %copy-start.26 = (bf16[1024,512]{1,0:T(8,128)(2,1)}, bf16[1024,512]{1,0:T(8,128)(2,1)S(1)}, u32[]{:S(2)}) copy-start(bf16[1024,512]{1,0:T(8,128)(2,1)S(1)} %get-tuple-element.81) | copy-start | bytes 3145732
  468.6 6.9 copy-start.31
  475.5 6.9 copy-start.30
  492.3 3.6 copy-start.14
  492.3 252.2 %reduce-scatter.8.cloned.1.call-start = ((), (), s32[]{:S(2)}) async-start(), calls=%async_computation.3 | async-start | bytes 4718592 | tf_op jit(solution)/shard_map/reduce_scatter | solution.py:611
  510.7 240.6 %reduce-scatter.12.cloned.1.call-start = ((), (), s32[]{:S(2)}) async-start(), calls=%async_computation.6 | async-start | bytes 7864320 | tf_op jit(solution)/shard_map/reduce_scatter | solution.py:448
  523.9 13.1 %collective-permute-start.4 = (bf16[1024,3]{0,1:T(4,128)(2,1)S(1)}, bf16[1024,3]{0,1:T(4,128)(2,1)S(1)}, u32[]{:S(2)}, u32[]{:S(2)}) collective-permute-start(bf16[1024,3]{0,1:T(4,128)(2,1)S(1)} %convert_element_type.194), channel_id=1, source_target_pairs={{0,8},{8,0},{16,24},{24,16},{1,9},{9,1},{17,25},{25,17},{2,10},{10... | collective-permute-start | bytes 18440 | tf_op jit(solution)/shard_map/ppermute | solution.py:456
  524.0 11.9 %collective-permute-start.7 = (bf16[1024,3]{0,1:T(4,128)(2,1)S(1)}, bf16[1024,3]{0,1:T(4,128)(2,1)S(1)}, u32[]{:S(2)}, u32[]{:S(2)}) collective-permute-start(bf16[1024,3]{0,1:T(4,128)(2,1)S(1)} %convert_element_type.194), channel_id=1, source_target_pairs={{0,16},{8,24},{16,0},{24,8},{1,17},{9,25},{17,1},{25,9},{2,18},{10... | collective-permute-start | bytes 18440 | tf_op jit(solution)/shard_map/ppermute | solution.py:456
  529.0 2.7 copy-start.48
  529.0 9.2 %collective-permute-start.5 = (bf16[1024,512]{1,0:T(8,128)(2,1)}, bf16[1024,512]{1,0:T(8,128)(2,1)}, u32[]{:S(2)}, u32[]{:S(2)}) collective-permute-start(bf16[1024,512]{1,0:T(8,128)(2,1)} %get-tuple-element.78), channel_id=1, source_target_pairs={{0,8},{8,0},{16,24},{24,16},{1,9},{9,1},{17,25},{25,17},{2,10},{10... | collective-permute-start | bytes 3145736 | tf_op jit(solution)/shard_map/ppermute | solution.py:456
  529.2 25.3 %collective-permute-start.10 = (bf16[1024,512]{1,0:T(8,128)(2,1)}, bf16[1024,512]{1,0:T(8,128)(2,1)}, u32[]{:S(2)}, u32[]{:S(2)}) collective-permute-start(bf16[1024,512]{1,0:T(8,128)(2,1)} %get-tuple-element.77), channel_id=1, source_target_pairs={{0,24},{8,16},{16,8},{24,0},{1,25},{9,17},{17,9},{25,1},{2,26},{10... | collective-permute-start | bytes 3145736 | tf_op jit(solution)/shard_map/ppermute | solution.py:456
  530.2 47.7 %collective-permute-start.8 = (bf16[1024,512]{1,0:T(8,128)(2,1)}, bf16[1024,512]{1,0:T(8,128)(2,1)}, u32[]{:S(2)}, u32[]{:S(2)}) collective-permute-start(bf16[1024,512]{1,0:T(8,128)(2,1)} %get-tuple-element.76), channel_id=1, source_target_pairs={{0,16},{8,24},{16,0},{24,8},{1,17},{9,25},{17,1},{25,9},{2,18},{10... | collective-permute-start | bytes 3145736 | tf_op jit(solution)/shard_map/ppermute | solution.py:456
  531.7 2.6 copy-start.24
  531.7 2.5 copy-start.27
  535.9 141.3 %collective-permute-start.11 = (bf16[1024,1024]{1,0:T(8,128)(2,1)}, bf16[1024,1024]{1,0:T(8,128)(2,1)}, u32[]{:S(2)}, u32[]{:S(2)}) collective-permute-start(bf16[1024,1024]{1,0:T(8,128)(2,1)} %pad_maximum_fusion), channel_id=1, source_target_pairs={{0,16},{8,24},{16,0},{24,8},{1,17},{9,25},{17,1},{25,9},{2,18},{10... | collective-permute-start | bytes 6291464 | tf_op jit(solution)/shard_map/ppermute | solution.py:456
  537.0 1.2 collective-permute-start.9
  557.8 126.5 %collective-permute-start.6 = (bf16[1024,1024]{1,0:T(8,128)(2,1)}, bf16[1024,1024]{1,0:T(8,128)(2,1)}, u32[]{:S(2)}, u32[]{:S(2)}) collective-permute-start(bf16[1024,1024]{1,0:T(8,128)(2,1)} %pad_maximum_fusion), channel_id=1, source_target_pairs={{0,8},{8,0},{16,24},{24,16},{1,9},{9,1},{17,25},{25,17},{2,10},{10... | collective-permute-start | bytes 6291464 | tf_op jit(solution)/shard_map/ppermute | solution.py:456
  581.2 103.1 %copy-start.25 = (bf16[1024,512]{1,0:T(8,128)(2,1)S(1)}, bf16[1024,512]{1,0:T(8,128)(2,1)}, u32[]{:S(2)}) copy-start(bf16[1024,512]{1,0:T(8,128)(2,1)} %copy-done.23) | copy-start | bytes 3145732
  581.2 103.1 %copy-start.28 = (bf16[1024,512]{1,0:T(8,128)(2,1)S(1)}, bf16[1024,512]{1,0:T(8,128)(2,1)}, u32[]{:S(2)}) copy-start(bf16[1024,512]{1,0:T(8,128)(2,1)} %copy-done.26) | copy-start | bytes 3145732
  677.2 17.7 %collective-permute-start.12 = (bf16[1024,1024]{1,0:T(8,128)(2,1)}, bf16[1024,1024]{1,0:T(8,128)(2,1)}, u32[]{:S(2)}, u32[]{:S(2)}) collective-permute-start(bf16[1024,1024]{1,0:T(8,128)(2,1)} %collective-permute-done.11), channel_id=1, source_target_pairs={{0,8},{8,0},{16,24},{24,16},{1,9},{9,1},{17,25},{25,17},{2,10},{10... | collective-permute-start | bytes 6291464 | tf_op jit(solution)/shard_map/ppermute | solution.py:456
  684.3 10.5 %copy-start.33 = (bf16[1024,3,512]{0,2,1:T(8,128)(2,1)S(1)}, bf16[1024,3,512]{0,2,1:T(8,128)(2,1)}, u32[]{:S(2)}) copy-start(bf16[1024,3,512]{0,2,1:T(8,128)(2,1)} %broadcast_select_fusion.1) | copy-start | bytes 9437188
  684.3 10.5 %copy-start.34 = (bf16[1024,3,512]{0,2,1:T(8,128)(2,1)S(1)}, bf16[1024,3,512]{0,2,1:T(8,128)(2,1)}, u32[]{:S(2)}) copy-start(bf16[1024,3,512]{0,2,1:T(8,128)(2,1)} %broadcast_select_fusion.2) | copy-start | bytes 9437188
  694.8 10.6 %copy-start.20 = (f32[128,2048]{1,0:T(8,128)S(1)}, f32[128,2048]{1,0:T(8,128)}, u32[]{:S(2)}) copy-start(f32[128,2048]{1,0:T(8,128)} %param.14) | copy-start | bytes 3145732
  694.9 10.6 %copy-start.43 = (f32[2048]{0:T(1024)S(1)}, f32[2048]{0:T(1024)}, u32[]{:S(2)}) copy-start(f32[2048]{0:T(1024)} %param.17) | copy-start | bytes 24580
  694.9 10.6 %copy-start.46 = (f32[128]{0:T(128)S(1)}, f32[128]{0:T(128)}, u32[]{:S(2)}) copy-start(f32[128]{0:T(128)} %copy-done.45) | copy-start | bytes 1540
  705.5 39.0 %copy-start.29 = (f32[128,2048]{1,0:T(8,128)S(1)}, f32[128,2048]{1,0:T(8,128)}, u32[]{:S(2)}) copy-start(f32[128,2048]{1,0:T(8,128)} %param.27) | copy-start | bytes 3145732
  744.5 10.4 %copy-start.1 = (f32[16,4096]{1,0:T(8,128)S(1)}, f32[16,4096]{1,0:T(8,128)}, u32[]{:S(2)}) copy-start(f32[16,4096]{1,0:T(8,128)} %param.20) | copy-start | bytes 786436
  (7 other events, 9.3 us)
Sparse Core Ops, SparseCore 0:
  11.6 107.7 all-gather.3
  121.0 48.5 all-gather.5
  453.2 44.0 all-reduce.7
  501.2 94.5 reduce-scatter.9
  599.3 90.2 reduce-scatter.7
  692.1 59.2 reduce-scatter.11

commit v3 on v2

v3 whole, which is shorter than its diff:
```python
import functools

import jax
import jax.numpy as jnp
from jax import lax
from jax.experimental import pallas as pl
from jax.experimental.pallas import tpu as pltpu
from jax.sharding import PartitionSpec as P

F32 = jnp.float32
BF = jnp.bfloat16
INNER = 4096
STATE = 16
DT_RANK = 128
EPSILON = 1e-05


STEPS=32
HUGE=1e30

def scan_forward_kernel(dtp_ref,u_ref,b_ref,c_ref,keep_ref,alog_ref,skip_ref,z_ref, gated_ref,y_ref,heads_ref, st, dec, inj, ys, a2):
    T,C=u_ref.shape
    @pl.when(pl.program_id(0)==0)
    def _():
        st[...]=jnp.zeros_like(st)
        a2[...]=-jnp.exp(alog_ref[...])*1.4426950408889634
    delta=jax.nn.softplus(dtp_ref[...].astype(F32))
    u=u_ref[...].astype(F32)
    dec[...]=jnp.where(keep_ref[...]>0,delta,HUGE)
    inj[...]=delta*u
    def chunk(k,state):
        heads_ref[k]=state
        b=b_ref[k]; c=c_ref[k]
        an=a2[...]
        base=pl.multiple_of(k*STEPS,STEPS)
        for j in range(STEPS):
            d=dec[pl.ds(base+j,1),:]
            v=inj[pl.ds(base+j,1),:]
            state=jnp.exp2(d*an)*state+b[:,j:j+1]*v
            ys[pl.ds(base+j,1),:]=jnp.sum(c[:,j:j+1]*state,axis=0,keepdims=True)
        return state
    st[...]=lax.fori_loop(0,T//STEPS,chunk,st[...])
    y=ys[...]+skip_ref[...]*u
    y_ref[...]=y
    z=z_ref[...].astype(F32)
    gated_ref[...]=(y*(z*jax.nn.sigmoid(z))).astype(BF)

def scan_forward(dtp,u,b,c,keep,alog,skip,z,T=128):
    N,C=u.shape
    S=alog.shape[0]
    nk=N//STEPS; tk=T//STEPS
    row=pl.BlockSpec((T,C),lambda i:(i,0))
    col=pl.BlockSpec((tk,S,STEPS),lambda i:(i,0,0))
    whole=lambda s: pl.BlockSpec(s,lambda i:(0,0))
    return pl.pallas_call(scan_forward_kernel,grid=(N//T,),
      in_specs=[row,row,col,col,pl.BlockSpec((T,1),lambda i:(i,0)),whole((S,C)),whole((1,C)),row],
      out_specs=[row,row,pl.BlockSpec((tk,S,C),lambda i:(i,0,0))],
      out_shape=[jax.ShapeDtypeStruct((N,C),BF),jax.ShapeDtypeStruct((N,C),F32),jax.ShapeDtypeStruct((nk,S,C),F32)],
      scratch_shapes=[pltpu.VMEM((S,C),F32),pltpu.VMEM((T,C),F32),pltpu.VMEM((T,C),F32),pltpu.VMEM((T,C),F32),pltpu.VMEM((S,C),F32)],
      compiler_params=pltpu.CompilerParams(vmem_limit_bytes=48<<20),
      name="scan_forward")(dtp,u,b,c,keep,alog,skip,z)

def fold_lanes(values):
    total=values[:,:128]
    for k in range(128,values.shape[1],128):
        total=total+values[:,k:k+128]
    return total

def sum_lanes(ref):
    values=ref[...].reshape(-1,128)
    high=values.astype(BF)
    rest=(values-high.astype(F32)).astype(BF)
    ones=jnp.ones((8,128),BF)
    dims=(((1,),(1,)),((),()))
    return (lax.dot_general(ones,high,dims,preferred_element_type=F32)+lax.dot_general(ones,rest,dims,preferred_element_type=F32))[:1]

def scan_backward_kernel(dtp_ref,u_ref,b_ref,c_ref,keep_ref,alog_ref,skip_ref,z_ref,y_ref,dg_ref,heads_ref,
        ddtp_ref,dus_ref,dz_ref,dm_ref,dalog_ref,dskip_ref, run, dec, inj, dly, dys, sq, wa, sts, dcs, an2, an1, acc, pb, pc):
    T,C=u_ref.shape
    S=alog_ref.shape[0]
    first=pl.program_id(0)==0
    last=pl.program_id(0)==pl.num_programs(0)-1
    @pl.when(first)
    def _():
        run[...]=jnp.zeros_like(run)
        acc[...]=jnp.zeros_like(acc)
        dskip_ref[...]=jnp.zeros_like(dskip_ref)
        an1[...]=-jnp.exp(alog_ref[...])
        an2[...]=an1[...]*1.4426950408889634
    dtp=dtp_ref[...].astype(F32)
    delta=jax.nn.softplus(dtp)
    u=u_ref[...].astype(F32)
    dec[...]=jnp.where(keep_ref[...]>0,delta,HUGE)
    dly[...]=delta
    inj[...]=delta*u
    z=z_ref[...].astype(F32)
    sg=jax.nn.sigmoid(z)
    dg=dg_ref[...].astype(F32)
    dy=dg*(z*sg)
    dys[...]=dy
    dz_ref[...]=(dg*y_ref[...]*(sg*(1.0+z*(1.0-sg)))).astype(BF)
    dskip_ref[...]+=jnp.sum(dy*u,axis=0,keepdims=True)
    def chunk(i,running):
        k=T//STEPS-1-i
        b=b_ref[k]; c=c_ref[k]
        base=pl.multiple_of(k*STEPS,STEPS)
        state=heads_ref[k]
        an=an2[...]
        for j in range(STEPS):
            d=dec[pl.ds(base+j,1),:]
            v=inj[pl.ds(base+j,1),:]
            dc=jnp.exp2(d*an)
            sd=dc*state
            state=sd+b[:,j:j+1]*v
            dcs[j]=dc
            sts[j]=sd
        for j in range(STEPS-1,-1,-1):
            g=dys[pl.ds(base+j,1),:]
            v=inj[pl.ds(base+j,1),:]
            bj=b[:,j:j+1]
            ds=c[:,j:j+1]*g+running
            sd=sts[j]
            w=ds*sd
            sq[pl.ds(base+j,1),:]=jnp.sum(ds*bj,axis=0,keepdims=True)
            wa[pl.ds(base+j,1),:]=jnp.sum(w*an1[...],axis=0,keepdims=True)
            acc[...]+=w*dly[pl.ds(base+j,1),:]
            pb[base+j]=fold_lanes(ds*v)
            pc[base+j]=fold_lanes(g*(sd+bj*v))
            running=dcs[j]*ds
        return running
    run[...]=lax.fori_loop(0,T//STEPS,chunk,run[...])
    dm_ref[0,0:1]=sum_lanes(pb)
    dm_ref[0,1:2]=sum_lanes(pc)
    dd=wa[...]+u*sq[...]
    ddtp_ref[...]=(dd*jax.nn.sigmoid(dtp)).astype(BF)
    dus_ref[...]=delta*sq[...]+dy*skip_ref[...]
    @pl.when(last)
    def _():
        dalog_ref[...]=acc[...]*an1[...]

def scan_backward(dtp,u,b,c,keep,alog,skip,z,y,dg,heads,T=128):
    N,C=u.shape
    S=alog.shape[0]
    nk=N//STEPS; tk=T//STEPS; nb=N//T
    row=pl.BlockSpec((T,C),lambda i:(nb-1-i,0))
    col=pl.BlockSpec((tk,S,STEPS),lambda i:(nb-1-i,0,0))
    whole=lambda s: pl.BlockSpec(s,lambda i:(0,0))
    sc=lambda *s: pltpu.VMEM(s,F32)
    return pl.pallas_call(scan_backward_kernel,grid=(nb,),
      in_specs=[row,row,col,col,pl.BlockSpec((T,1),lambda i:(nb-1-i,0)),whole((S,C)),whole((1,C)),row,row,row,pl.BlockSpec((tk,S,C),lambda i:(nb-1-i,0,0))],
      out_specs=[row,row,row,pl.BlockSpec((1,2,T*S),lambda i:(nb-1-i,0,0)),whole((S,C)),whole((1,C))],
      out_shape=[jax.ShapeDtypeStruct((N,C),BF),jax.ShapeDtypeStruct((N,C),F32),jax.ShapeDtypeStruct((N,C),BF),jax.ShapeDtypeStruct((nb,2,T*S),F32),jax.ShapeDtypeStruct((S,C),F32),jax.ShapeDtypeStruct((1,C),F32)],
      scratch_shapes=[sc(S,C),sc(T,C),sc(T,C),sc(T,C),sc(T,C),sc(T,C),sc(T,C),sc(STEPS,S,C),sc(STEPS,S,C),sc(S,C),sc(S,C),sc(S,C),sc(T,S,128),sc(T,S,128)],
      compiler_params=pltpu.CompilerParams(vmem_limit_bytes=48<<20),
      name="scan_backward")(dtp,u,b,c,keep,alog,skip,z,y,dg,heads)


CUTS = 2
MESH = pl.DeviceIdType.MESH
FLIGHT = 6
TILE = 256
SMALL, OUTER = 100, 200


def ring_index(position, wide):
    if wide != 8:
        return position
    turn = position // 4
    return (1 - turn) * 2 * position + turn * (2 * (7 - position) + 1)


def ring_position(index, wide):
    if wide != 8:
        return index
    return index // 2 + index % 2 * (7 - 2 * (index // 2))


def remote(source, target, send, recv, device):
    return pltpu.make_async_remote_copy(
        src_ref=source, dst_ref=target, send_sem=send, recv_sem=recv, device_id=device, device_id_type=MESH
    )


def sum_over_wide(wide, me, place, x_ref, out_ref, got, whole, s1, r1, s2, r2):
    step = out_ref.shape[1] // wide
    peers = [lax.rem(place + k, wide) for k in range(1, wide)]

    def columns(index):
        return pl.ds(pl.multiple_of(index * step, step), step)

    def give(k):
        device = (me, peers[k - 1])
        return remote(x_ref.at[:, columns(peers[k - 1])], got.at[k], s1.at[k], r1.at[k], device)

    def spread(k):
        device = (me, peers[k - 1])
        return remote(whole, out_ref.at[:, columns(place)], s2.at[k], r2.at[k], device)

    order = sorted(range(1, wide), key=lambda k: -min(k, wide - k))
    for k in order:
        give(k).start()
    total = x_ref[:, columns(place)].astype(F32)
    for k in reversed(order):
        give(k).wait_recv()
        total = total + got[k].astype(F32)
    whole[...] = total.astype(BF)
    for k in order:
        spread(k).start()
    out_ref[:, columns(place)] = whole[...]
    for k in range(1, wide):
        spread(k).wait()
        give(k).wait_send()


class Spread:
    def __init__(self, wide, me, place, arrays, sems):
        self.wide, self.me, self.place, self.arrays = wide, me, place, arrays
        self.up_send, self.up_recv, self.down_send, self.down_recv, self.all_send, self.all_recv = sems
        self.z, self.y = place // 2, place % 2

    def copy(self, i, owner, source, send, recv, target):
        ref = self.arrays[i][0] if source else self.arrays[i][1].at[owner]
        return remote(ref, self.arrays[i][1].at[owner], send, recv, (self.me, target))

    def up(self, i, hop):
        owner = (self.z - hop) * 2 + self.y
        return self.copy(i, owner, hop == 0, self.up_send.at[hop, i], self.up_recv.at[hop, i], self.place + 2)

    def down(self, i, hop):
        owner = (self.z + hop) * 2 + self.y
        return self.copy(i, owner, hop == 0, self.down_send.at[hop, i], self.down_recv.at[hop, i], self.place - 2)

    def beside(self, i, z, own=False):
        owner = z * 2 + self.y
        return self.copy(i, owner, own, self.all_send.at[z, i], self.all_recv.at[z, i], self.place + 1 - 2 * self.y)

    def direct(self, i, k):
        target = lax.rem(self.place + k, self.wide)
        return self.copy(i, self.place, True, self.all_send.at[k, i], self.all_recv.at[k, i], target)

    def begin(self, i):
        if self.wide != 8:
            for k in range(1, self.wide):
                self.direct(i, k).start()
            return

        @pl.when(self.z < 3)
        def _():
            self.up(i, 0).start()

        @pl.when(self.z > 0)
        def _():
            self.down(i, 0).start()

        self.beside(i, self.z, True).start()

    def step(self, i, hop):
        if self.wide != 8:
            return

        @pl.when(self.z > hop)
        def _():
            self.up(i, hop).wait_recv()
            if hop < 2:

                @pl.when(self.z < 3)
                def _():
                    self.up(i, hop + 1).start()

            self.beside(i, self.z - 1 - hop).start()

        @pl.when(self.z + hop < 3)
        def _():
            self.down(i, hop).wait_recv()
            if hop < 2:

                @pl.when(self.z > 0)
                def _():
                    self.down(i, hop + 1).start()

            self.beside(i, self.z + 1 + hop).start()

    def end(self, i):
        if self.wide != 8:
            for k in range(1, self.wide):
                self.direct(i, k).wait_recv()
            return
        for z in range(4):
            self.beside(i, z).wait_recv()

    def sent(self):
        for i in range(len(self.arrays)):
            if self.wide != 8:
                for k in range(1, self.wide):
                    self.direct(i, k).wait_send()
                continue
            for hop in range(3):

                @pl.when((self.z >= hop) & (self.z < 3))
                def _():
                    self.up(i, hop).wait_send()

                @pl.when((self.z + hop <= 3) & (self.z > 0))
                def _():
                    self.down(i, hop).wait_send()

            for z in range(4):
                self.beside(i, z).wait_send()


def front_kernel(dp, wide, rank_rows, *refs):
    win_ref, wout_ref, small_ref, normed_ref, back_ref, tag_ref, masks_ref, taps_ref, bias_ref, refs = *refs[:9], refs[9:]
    wall_out, wout_out, wsmall_out, nall_out, ball_out, tags_out, xs_out, z_out, u_ref, proj_ref, refs = *refs[:10], refs[10:]
    stage, stage_out, wout_low, wall, wsmall, nall, tags, mixed, xz, part, part_low, got, whole, refs = *refs[:13], refs[13:]
    x_send, x_recv, core_send, core_recv, on_send, on_recv, refs = *refs[:6], refs[6:]
    h_send, h_recv, h_local, load, keep = refs[:5]
    s1, r1, s2, r2 = refs[5:9]
    me, place = lax.axis_index("dp"), lax.axis_index("wide")
    cuts, span, narrow = mixed.shape
    half = wide // 2
    count = normed_ref.shape[0]
    rows = win_ref.shape[1]
    lines = dp // 2
    line, core = me // 2, me % 2
    partner = (me + 1 - 2 * core, place)
    across = [(lax.rem(line + k, lines) * 2 + core, place) for k in range(1, lines)]
    barrier = pltpu.get_barrier_semaphore()
    for peer in [partner] + across + [(me, lax.rem(place + k, wide)) for k in range(1, wide)]:
        pl.semaphore_signal(barrier, inc=1, device_id=peer, device_id_type=MESH)
    pl.semaphore_wait(barrier, lines + wide - 1)

    turns = [h * (cuts // 2) + i for i in range(cuts // 2) for h in range(2)]
    pieces = [(q, kind) for q in turns for kind in range(3)]
    pieces += [(SMALL, kind) for kind in range(3)]
    pieces += [(OUTER + h, kind) for kind in range(3) for h in range(2)]
    height = wout_ref.shape[1] // 2

    def slot(j, owner):
        q, kind = pieces[j]
        if q >= OUTER:
            return wout_out.at[owner, kind, pl.ds((q - OUTER) * height, height)]
        if q == SMALL:
            return wsmall.at[owner, kind]
        return wall.at[owner, kind, :, pl.ds(q * narrow, narrow)]

    def mine(j):
        q, kind = pieces[j]
        if q >= OUTER:
            return wout_low.at[kind, pl.ds((q - OUTER) * height, height)]
        return slot(j, me)

    def cross(k, j):
        return remote(mine(j), slot(j, me), x_send.at[k, j], x_recv.at[k, j], across[k])

    def pair(j):
        return remote(mine(j), slot(j, me), core_send.at[j], core_recv.at[j], partner)

    def onward(k, j):
        owner = lax.rem(line + lines - 1 - k, lines) * 2 + core
        return remote(slot(j, owner), slot(j, owner), on_send.at[k, j], on_recv.at[k, j], partner)

    loads = []
    for q in turns:
        part_columns = pl.ds(q * narrow, narrow)
        loads.append(pltpu.make_async_copy(win_ref.at[:, :, part_columns], stage.at[:, :, part_columns], load.at[q]))
        loads[-1].start()
    loads.append(pltpu.make_async_copy(wout_ref, stage_out, load.at[cuts]))
    loads[-1].start()

    nall[place] = normed_ref[...]
    tags[place] = tag_ref[...]
    kept = [pltpu.make_async_copy(back_ref, ball_out.at[place], keep.at[0])]
    kept[-1].start()
    spread = Spread(
        wide,
        me,
        place,
        [
            (nall.at[place, pl.ds(0, count // 2)], nall.at[:, pl.ds(0, count // 2)]),
            (nall.at[place, pl.ds(count // 2, count // 2)], nall.at[:, pl.ds(count // 2, count // 2)]),
            (tags.at[place], tags),
            (back_ref, ball_out),
        ],
        refs[9:],
    )
    for i in range(3):
        spread.begin(i)
    for j, (q, kind) in enumerate(pieces):
        if q >= OUTER:
            if j == 3 * cuts + 3:
                loads[cuts].wait()
            part_rows = pl.ds((q - OUTER) * height, height)
            wout_low[kind, part_rows] = stage_out[kind, part_rows].astype(BF)
        elif q == SMALL:
            wsmall[me, kind] = small_ref[kind].astype(BF)
        else:
            if kind == 0:
                loads[turns.index(q)].wait()
            wall[me, kind, :, q * narrow : (q + 1) * narrow] = stage[
                kind, :, q * narrow : (q + 1) * narrow
            ].astype(BF)
        if j < FLIGHT:
            for k in range(lines - 1):
                cross(k, j).start()
        pair(j).start()

    kept.append(pltpu.make_async_copy(wout_low, wout_out.at[me], keep.at[1]))
    kept[-1].start()
    state = {"passed": 0}

    def pass_on(until):
        for j in range(state["passed"], min(until, len(pieces))):
            for k in range(lines - 1):
                cross(k, j).wait_recv()
                onward(k, j).start()
                if j < 3 * cuts and j + FLIGHT < len(pieces):
                    cross(k, j + FLIGHT).start()
                if j == 3 * cuts - 1:
                    for later in range(j + FLIGHT + 1, len(pieces)):
                        cross(k, later).start()
            state["passed"] = j + 1

    for hop in range(3):
        for i in range(3):
            spread.step(i, hop)
        pass_on(2 * (hop + 1))
    for i in range(3):
        spread.end(i)
    spread.begin(3)

    low = place // half
    home = place % half

    def deliver(q):
        return remote(
            mixed.at[q], xz.at[low, q % (cuts // 2)], h_send.at[q], h_recv.at[low, q % (cuts // 2)],
            (me, 2 * home + q // (cuts // 2)),
        )

    def stay(q):
        return pltpu.make_async_copy(mixed.at[q], xz.at[low, q % (cuts // 2)], h_local.at[q])

    blocks = TILE // count
    for turn, q in enumerate(turns):
        pass_on((turn + 1) * 3)
        for j in range(3 * turn, 3 * turn + 3):
            pair(j).wait_recv()
            for k in range(lines - 1):
                onward(k, j).wait_recv()

        def tile(t, carry, q=q):
            left = nall[pl.ds(t * blocks, blocks)].reshape(TILE, -1)
            tag = tags[pl.ds(t * blocks, blocks)].reshape(TILE, -1)[:, :1].astype(F32)
            total = jnp.zeros((TILE, narrow), F32)
            for kind in range(3):
                product = jnp.zeros((TILE, narrow), F32)
                for owner in range(dp):
                    product += jnp.dot(
                        left[:, owner * rows : (owner + 1) * rows],
                        wall[owner, kind, :, q * narrow : (q + 1) * narrow],
                        preferred_element_type=F32,
                    )
                total = total + jnp.where(tag == kind, product, 0.0)
            mixed[q, pl.ds(pl.multiple_of(t * TILE, TILE), TILE)] = total.astype(BF)
            return carry

        lax.fori_loop(0, span // TILE, tile, 0)
        target = 2 * home + q // (cuts // 2)

        @pl.when(target != place)
        def _(q=q):
            deliver(q).start()

        @pl.when(target == place)
        def _(q=q):
            stay(q).start()

        if turn > 0:
            spread.step(3, turn - 1)
        if turn == 0:
            for source, sink in ((nall, nall_out), (tags, tags_out)):
                kept.append(pltpu.make_async_copy(source, sink, keep.at[len(kept)]))
                kept[-1].start()
    pass_on(3 * cuts + 3)
    kept.append(pltpu.make_async_copy(wall, wall_out, keep.at[len(kept)]))
    kept[-1].start()

    def arrive(kind, i):
        source = kind * half + place // 2
        q = place % 2 * (cuts // 2) + i

        @pl.when(source != place)
        def _():
            remote(mixed.at[0], xz.at[kind, i], h_send.at[0], h_recv.at[kind, i], partner).wait_recv()

        @pl.when(source == place)
        def _():
            pltpu.make_async_copy(mixed.at[q], xz.at[kind, i], h_local.at[q]).wait()

    taps_all = taps_ref[...]
    width = taps_all.shape[0]
    for i in range(cuts // 2):
        arrive(0, i)
        taps = taps_all[:, i * narrow : (i + 1) * narrow]
        bias = bias_ref[:, i * narrow : (i + 1) * narrow]

        def conv(t, carry, i=i, taps=taps, bias=bias):
            at = pl.multiple_of(t * 128, 128)
            behind = pl.multiple_of(jnp.maximum(t * 128 - 16, 0), 16)
            here = xz[0, i, pl.ds(at, 128)].astype(F32)
            both = jnp.concatenate([xz[0, i, pl.ds(behind, 16)].astype(F32), here], axis=0)
            masks = masks_ref[pl.ds(at, 128)]
            pre = bias + taps[width - 1 : width] * here
            for offset in range(1, width):
                pre = pre + taps[width - 1 - offset : width - offset] * (
                    both[16 - offset : 144 - offset] * masks[:, offset : offset + 1]
                )
            u_ref[pl.ds(at, 128), i * narrow : (i + 1) * narrow] = (pre * jax.nn.sigmoid(pre)).astype(BF)
            return carry

        lax.fori_loop(0, span // 128, conv, 0)

    for j in range(3 * cuts, 3 * cuts + 3):
        pair(j).wait_recv()
        for k in range(lines - 1):
            onward(k, j).wait_recv()

    def project(t, carry):
        at = pl.multiple_of(t * TILE, TILE)
        inner = u_ref[pl.ds(at, TILE)].astype(F32)
        tag = tags[pl.ds(t * blocks, blocks)].reshape(TILE, -1)[:, :1].astype(F32)
        chosen = [jnp.where(tag == kind, inner, 0.0).astype(BF) for kind in range(3)]
        for owner in range(dp):
            total = jnp.zeros((wsmall.shape[2], TILE), F32)
            for kind in range(3):
                total += lax.dot_general(
                    wsmall[owner, kind], chosen[kind], (((1,), (1,)), ((), ())), preferred_element_type=F32
                )
            part[owner * rank_rows : (owner + 1) * rank_rows, pl.ds(at, TILE)] = total[:rank_rows]
        return carry

    pass_on(3 * cuts + 6)
    lax.fori_loop(0, span // TILE, project, 0)
    part_low[...] = part[...].astype(BF)
    sum_over_wide(wide, me, place, part_low, proj_ref, got, whole, s1, r1, s2, r2)

    pass_on(len(pieces))
    for hop in range(cuts - 1, 3):
        spread.step(3, hop)
    spread.end(3)
    kept.append(pltpu.make_async_copy(wsmall, wsmall_out, keep.at[len(kept)]))
    kept[-1].start()
    for i in range(cuts // 2):
        arrive(1, i)
    for i in range(cuts // 2):
        xs_out[:, i * narrow : (i + 1) * narrow] = xz[0, i]
        z_out[:, i * narrow : (i + 1) * narrow] = xz[1, i]
    for j in range(3 * cuts + 3, len(pieces)):
        pair(j).wait_recv()
        for k in range(lines - 1):
            onward(k, j).wait_recv()
    for j in range(len(pieces)):
        pair(j).wait_send()
        for k in range(lines - 1):
            cross(k, j).wait_send()
            onward(k, j).wait_send()
    spread.sent()
    for q in range(cuts):

        @pl.when(2 * home + q // (cuts // 2) != place)
        def _(q=q):
            deliver(q).wait_send()

    for copy in kept:
        copy.wait()


def front(win, wout, small, normed, back, tag, masks, taps, bias, rank_rows, collective_id):
    dp, wide = lax.axis_size("dp"), lax.axis_size("wide")
    kinds, rows, columns = win.shape
    cuts = 4 if columns >= 512 else 2
    narrow = columns // cuts
    count, depth = normed.shape
    span = count * wide
    channels = small.shape[2]
    rank = rank_rows * dp
    lines = dp // 2
    pieces = 3 * cuts + 9
    vmem = pl.BlockSpec(memory_space=pltpu.VMEM)
    anywhere = pl.BlockSpec(memory_space=pl.ANY)
    dma = pltpu.SemaphoreType.DMA
    shape = jax.ShapeDtypeStruct
    far, near = dma((lines - 1, pieces)), dma((pieces,))
    hops = dma((3, 4)) if wide == 8 else dma((1, 4))
    every = dma((4, 4)) if wide == 8 else dma((wide, 4))
    return pl.pallas_call(
        functools.partial(front_kernel, dp, wide, rank_rows),
        out_shape=[
            shape((dp, 3, rows, columns), BF),
            shape((dp,) + wout.shape, BF),
            shape((dp,) + small.shape, BF),
            shape((wide, count, depth), BF),
            shape((wide, count, depth), BF),
            shape((wide,) + tag.shape, BF),
            shape((span, channels), BF),
            shape((span, channels), BF),
            shape((span, channels), BF),
            shape((rank, span), BF),
        ],
        in_specs=[anywhere] * 2 + [vmem] * 7,
        out_specs=[anywhere] * 6 + [vmem] * 4,
        scratch_shapes=[
            pltpu.VMEM(win.shape, F32),
            pltpu.VMEM(wout.shape, F32),
            pltpu.VMEM(wout.shape, BF),
            pltpu.VMEM((dp, 3, rows, columns), BF),
            pltpu.VMEM((dp,) + small.shape, BF),
            pltpu.VMEM((wide, count, depth), BF),
            pltpu.VMEM((wide,) + tag.shape, BF),
            pltpu.VMEM((cuts, span, narrow), BF),
            pltpu.VMEM((2, cuts // 2, span, narrow), BF),
            pltpu.VMEM((rank, span), F32),
            pltpu.VMEM((rank, span), BF),
            pltpu.VMEM((wide, rank, count), BF),
            pltpu.VMEM((rank, count), BF),
            far, far, near, near, far, far,
            dma((cuts,)), dma((2, cuts // 2)), dma((cuts,)), dma((cuts + 1,)), dma((6,)),
            dma((wide,)), dma((wide,)), dma((wide,)), dma((wide,)),
            hops, hops, hops, hops, every, every,
        ],
        compiler_params=pltpu.CompilerParams(
            collective_id=collective_id, has_side_effects=True, vmem_limit_bytes=60 << 20
        ),
        name="front",
    )(win, wout, small, normed, back, tag, masks, taps, bias)


def sum_wide_kernel(wide, x_ref, out_ref, got, whole, s1, r1, s2, r2):
    me, place = lax.axis_index("dp"), lax.axis_index("wide")
    step = out_ref.shape[1] // wide
    barrier = pltpu.get_barrier_semaphore()
    peers = [lax.rem(place + k, wide) for k in range(1, wide)]
    for peer in peers:
        pl.semaphore_signal(barrier, inc=1, device_id=(me, peer), device_id_type=MESH)
    pl.semaphore_wait(barrier, wide - 1)

    def columns(index):
        return pl.ds(pl.multiple_of(index * step, step), step)

    def give(k):
        return pltpu.make_async_remote_copy(
            src_ref=x_ref.at[:, columns(peers[k - 1])],
            dst_ref=got.at[k],
            send_sem=s1.at[k],
            recv_sem=r1.at[k],
            device_id=(me, peers[k - 1]),
            device_id_type=MESH,
        )

    def spread(k):
        return pltpu.make_async_remote_copy(
            src_ref=whole,
            dst_ref=out_ref.at[:, columns(place)],
            send_sem=s2.at[k],
            recv_sem=r2.at[k],
            device_id=(me, peers[k - 1]),
            device_id_type=MESH,
        )

    order = sorted(range(1, wide), key=lambda k: -min(k, wide - k))
    for k in order:
        give(k).start()
    total = x_ref[:, columns(place)].astype(F32)
    for k in reversed(order):
        give(k).wait_recv()
        total = total + got[k].astype(F32)
    whole[...] = total.astype(BF)
    for k in order:
        spread(k).start()
    out_ref[:, columns(place)] = whole[...]
    for k in range(1, wide):
        spread(k).wait()
        give(k).wait_send()


def sum_wide(x, collective_id):
    wide = lax.axis_size("wide")
    rows, span = x.shape
    vmem = pl.BlockSpec(memory_space=pltpu.VMEM)
    dma = pltpu.SemaphoreType.DMA
    return pl.pallas_call(
        functools.partial(sum_wide_kernel, wide),
        out_shape=jax.ShapeDtypeStruct((rows, span), BF),
        in_specs=[vmem],
        out_specs=vmem,
        scratch_shapes=[
            pltpu.VMEM((wide, rows, span // wide), x.dtype),
            pltpu.VMEM((rows, span // wide), BF),
            dma((wide,)),
            dma((wide,)),
            dma((wide,)),
            dma((wide,)),
        ],
        compiler_params=pltpu.CompilerParams(
            collective_id=collective_id, has_side_effects=True, vmem_limit_bytes=32 << 20
        ),
        name="sum_wide",
    )(x)

def finish_kernel(dp, wide, part_ref, table_ref, small_ref, rows_ref, tables_ref, sums_ref, *refs):
    flow_a, flow_b, got_tables, got_small = refs[:4]
    a_send, a_recv, b_send, b_recv, t_send, t_recv, s_send, s_recv, w_send, w_recv = refs[4:]
    me, place = lax.axis_index("dp"), lax.axis_index("wide")
    position = ring_position(place, wide)
    after = (me, ring_index(lax.rem(position + 1, wide), wide))
    before = (me, ring_index(lax.rem(position + wide - 1, wide), wide))
    mates = [lax.rem(me + k, dp) for k in range(1, dp)]
    peers = [lax.rem(place + k, wide) for k in range(1, wide)]
    barrier = pltpu.get_barrier_semaphore()
    for mate in mates:
        pl.semaphore_signal(barrier, inc=1, device_id=(mate, place), device_id_type=MESH)
    for peer in peers:
        pl.semaphore_signal(barrier, inc=1, device_id=(me, peer), device_id_type=MESH)
    pl.semaphore_wait(barrier, dp + wide - 2)

    def remote(source, target, send, recv, device):
        return pltpu.make_async_remote_copy(
            src_ref=source, dst_ref=target, send_sem=send, recv_sem=recv, device_id=device, device_id_type=MESH
        )

    half = part_ref.shape[2] // 2
    cut = half // CUTS

    def columns(side, i):
        return pl.ds(side * half + i * cut, cut)

    def owner(side, hop):
        step = position + wide - 1 - hop if side == 0 else position + 1 + hop
        return ring_index(lax.rem(step, wide), wide)

    flows = ((flow_a, a_send, a_recv, after), (flow_b, b_send, b_recv, before))

    def turn(side, hop, i):
        flow, send, recv, device = flows[side]
        if hop == 0:
            source = part_ref.at[owner(side, 0), :, columns(side, i)]
        else:
            source = flow.at[hop - 1, i]
        return remote(source, flow.at[hop, i], send.at[hop, i], recv.at[hop, i], device)

    for i in range(CUTS):
        for side in range(2):
            turn(side, 0, i).start()

    def lend_table(k):
        return remote(table_ref, got_tables.at[k], t_send.at[k], t_recv.at[k], (mates[k], place))

    def lend_small(k):
        return remote(small_ref.at[mates[k]], got_small.at[k], s_send.at[k], s_recv.at[k], (mates[k], place))

    def show(k):
        return remote(tables_ref.at[place], tables_ref.at[place], w_send.at[k], w_recv.at[k], (me, peers[k]))

    for k in range(dp - 1):
        lend_table(k).start()
    for k in range(dp - 1):
        lend_small(k).start()

    for hop in range(1, wide):
        for i in range(CUTS):
            for side in range(2):
                turn(side, hop - 1, i).wait_recv()
                flow = flows[side][0]
                own = part_ref[owner(side, hop), :, columns(side, i)].astype(F32)
                total = flow[hop - 1, i].astype(F32) + own
                if hop < wide - 1:
                    flow[hop - 1, i] = total.astype(BF)
                    turn(side, hop, i).start()
                else:
                    rows_ref[:, columns(side, i)] = total
        if hop == 1:
            total = table_ref[...]
            for k in range(dp - 1):
                lend_table(k).wait_recv()
                total = total + got_tables[k]
            tables_ref[place] = total
            for k in range(wide - 1):
                show(k).start()
        if hop == min(3, wide - 1):
            for kind in range(3):
                sums_ref[kind] = small_ref[me, kind].astype(F32)
            for k in range(dp - 1):
                lend_small(k).wait_recv()
                for kind in range(3):
                    sums_ref[kind] += got_small[k, kind].astype(F32)

    for k in range(dp - 1):
        lend_table(k).wait_send()
        lend_small(k).wait_send()
    for k in range(wide - 1):
        show(k).wait()
    for hop in range(wide - 1):
        for i in range(CUTS):
            for side in range(2):
                turn(side, hop, i).wait_send()


def finish(part, table, small, collective_id):
    dp, wide = lax.axis_size("dp"), lax.axis_size("wide")
    rows, depth = part.shape[1:]
    vmem = pl.BlockSpec(memory_space=pltpu.VMEM)
    dma = pltpu.SemaphoreType.DMA
    flow = pltpu.VMEM((wide - 1, CUTS, rows, depth // 2 // CUTS), BF)
    hops = dma((wide - 1, CUTS))
    return pl.pallas_call(
        functools.partial(finish_kernel, dp, wide),
        out_shape=[
            jax.ShapeDtypeStruct((rows, depth), F32),
            jax.ShapeDtypeStruct((wide,) + table.shape, F32),
            jax.ShapeDtypeStruct(small.shape[1:], F32),
        ],
        in_specs=[vmem] * 3,
        out_specs=[vmem] * 3,
        scratch_shapes=[
            flow,
            flow,
            pltpu.VMEM((dp - 1,) + table.shape, F32),
            pltpu.VMEM((dp - 1,) + small.shape[1:], small.dtype),
            hops,
            hops,
            hops,
            hops,
            dma((dp - 1,)),
            dma((dp - 1,)),
            dma((dp - 1,)),
            dma((dp - 1,)),
            dma((wide - 1,)),
            dma((wide - 1,)),
        ],
        compiler_params=pltpu.CompilerParams(
            collective_id=collective_id, has_side_effects=True, vmem_limit_bytes=56 << 20
        ),
        name="finish",
    )(part, table, small)


def gate_kernel(back_ref, gated_ref, tag_ref, w_ref, branch_ref, dgated_ref, grad_ref, chosen):
    dp, kinds, rows, channels = w_ref.shape
    span = gated_ref.shape[0]
    blocks = TILE // tag_ref.shape[1]

    def tile(t, carry):
        at = pl.ds(pl.multiple_of(t * TILE, TILE), TILE)
        tag = tag_ref[pl.ds(t * blocks, blocks)].reshape(TILE, -1)[:, :1].astype(F32)
        gated = gated_ref[at].astype(F32)
        for kind in range(3):
            chosen[kind, at] = jnp.where(tag == kind, gated, 0.0).astype(BF)
        for owner in range(dp):
            branch = jnp.zeros((TILE, rows), F32)
            for kind in range(3):
                branch += lax.dot_general(
                    chosen[kind, at], w_ref[owner, kind], (((1,), (1,)), ((), ())), preferred_element_type=F32
                )
            branch_ref[at, owner * rows : (owner + 1) * rows] = branch.astype(BF)
        total = jnp.zeros((TILE, channels), F32)
        for kind in range(3):
            product = jnp.zeros((TILE, channels), F32)
            for owner in range(dp):
                product += jnp.dot(
                    back_ref[at, owner * rows : (owner + 1) * rows], w_ref[owner, kind], preferred_element_type=F32
                )
            total = total + jnp.where(tag == kind, product, 0.0)
        dgated_ref[at] = total.astype(BF)
        return carry

    lax.fori_loop(0, span // TILE, tile, 0)

    def grad(owner, carry):
        columns = pl.ds(pl.multiple_of(owner * rows, rows), rows)
        for kind in range(3):
            grad_ref[owner, kind] = lax.dot_general(
                back_ref[:, columns], chosen[kind], (((0,), (0,)), ((), ())), preferred_element_type=F32
            ).astype(BF)
        return carry

    lax.fori_loop(0, dp, grad, 0)


def gate(back, gated, tags, w_out):
    span, channels = gated.shape
    dp, kinds, rows, _ = w_out.shape
    vmem = pl.BlockSpec(memory_space=pltpu.VMEM)
    flops = 6 * 3 * span * channels * back.shape[1]
    return pl.pallas_call(
        gate_kernel,
        out_shape=[
            jax.ShapeDtypeStruct(back.shape, BF),
            jax.ShapeDtypeStruct(gated.shape, BF),
            jax.ShapeDtypeStruct(w_out.shape, BF),
        ],
        in_specs=[vmem] * 4,
        out_specs=[vmem] * 3,
        scratch_shapes=[pltpu.VMEM((3, span, channels), BF)],
        compiler_params=pltpu.CompilerParams(vmem_limit_bytes=58 << 20),
        cost_estimate=pl.CostEstimate(flops=flops, bytes_accessed=24 << 20, transcendentals=0),
        name="gate",
    )(back, gated, tags, w_out)


def contract(left, right, left_dim, right_dim):
    return lax.dot_general(
        left, right, (((left_dim,), (right_dim,)), ((), ())), preferred_element_type=F32
    )


def segment_of(places, bounds):
    return jnp.sum((places[:, None] >= bounds[None, :]).astype(jnp.int32), axis=1)


def conv_masks(places, bounds, width):
    segment = segment_of(places, bounds)
    return [
        ((places >= offset) & (segment_of(places - offset, bounds) == segment)).astype(F32)
        for offset in range(width)
    ]


def silu_slope(values):
    sigma = jax.nn.sigmoid(values)
    return sigma * (1.0 + values * (1.0 - sigma))


def split_kinds(rows, kinds, parts):
    count, depth = rows.shape
    pieces = rows.reshape(count, parts, 1, depth // parts)
    picked = kinds[:, None, :, None]
    return jnp.where(picked, pieces, jnp.zeros((), rows.dtype)).reshape(count, 3 * depth)


def scatter_master(grad):
    return jnp.transpose(lax.psum_scatter(grad, "dp", scatter_dimension=0), (1, 0, 2))


def hop(block, flip):
    devices = lax.axis_size("dp")
    return lax.ppermute(block, "dp", [(d, flip(d)) for d in range(devices)])


def from_partners(block):
    lines = lax.axis_size("dp") // 2
    blocks = [block, hop(block, lambda d: d ^ 1)]
    for k in range(1, lines):
        far = hop(block, lambda d: (d // 2 + k) % lines * 2 + d % 2)
        blocks += [far, hop(far, lambda d: d ^ 1)]
    return blocks


def swap_features(rows):
    devices = lax.axis_size("dp")
    lines = devices // 2
    depth = rows.shape[1] // devices
    me = lax.axis_index("dp")

    def part(owner):
        return lax.dynamic_slice_in_dim(rows, owner * depth, depth, 1)

    core = me % 2
    blocks = [part(me), hop(part(me + 1 - 2 * core), lambda d: d ^ 1)]
    for k in range(1, lines):
        line = (me // 2 + k) % lines
        blocks.append(hop(part(line * 2 + core), lambda d: (d // 2 + k) % lines * 2 + d % 2))
        blocks.append(
            hop(part(line * 2 + 1 - core), lambda d: (d // 2 + k) % lines * 2 + 1 - d % 2)
        )
    return blocks


def halves_back(xs, z, wide):
    half = wide // 2
    low = lax.axis_index("wide") < half
    even = [(2 * v, v) if v < half else (2 * (v - half) + 1, v) for v in range(wide)]
    odd = [(2 * v + 1, v) if v < half else (2 * (v - half), v) for v in range(wide)]
    is_even = lax.axis_index("wide") % 2 == 0
    got_a = lax.ppermute(jnp.where(is_even, xs, z), "wide", even)
    got_b = lax.ppermute(jnp.where(is_even, z, xs), "wide", odd)
    return jnp.concatenate([jnp.where(low, got_a, got_b), jnp.where(low, got_b, got_a)], axis=1)


def body(
    x_in,
    lengths,
    modality,
    norm_gain,
    conv_weight,
    conv_bias,
    a_log,
    d_skip,
    in_master,
    xproj_master,
    dtproj_master,
    dt_bias,
    out_master,
    cotangent,
):
    wide, dp = lax.axis_size("wide"), lax.axis_size("dp")
    place = lax.axis_index("wide")
    count = x_in.shape[0]
    span = count * wide
    channels = INNER // wide
    width = conv_weight.shape[0]
    own = lambda table: lax.dynamic_slice_in_dim(table, place * channels, channels, table.ndim - 1)

    bounds = jnp.cumsum(lengths.reshape(-1))
    places = jnp.arange(span, dtype=jnp.int32)
    living = places < bounds[-1]
    masks = conv_masks(places, bounds, width)
    later = conv_masks(jnp.arange(span + width - 1, dtype=jnp.int32), bounds, width)
    alive_here = (place * count + jnp.arange(count, dtype=jnp.int32)) < bounds[-1]

    scale = lax.rsqrt(jnp.mean(x_in * x_in, axis=1, keepdims=True) + EPSILON)
    normed = (x_in * scale * norm_gain[None, :]).astype(BF)
    d_branch = jnp.where(alive_here[:, None], cotangent, 0.0).astype(BF)
    rank_rows, step_rows = xproj_master.shape[0], dtproj_master.shape[0]
    small = jnp.concatenate([xproj_master, dtproj_master], axis=0)
    small = jnp.pad(small, ((0, -small.shape[0] % 16), (0, 0), (0, 0)))
    tag = jnp.where(alive_here, modality, 3).astype(BF)
    w_in, w_out, w_small, normed_all, d_branch_all, tags_all, xs, z, inner, proj = front(
        jnp.transpose(in_master, (1, 0, 2)),
        jnp.transpose(out_master, (1, 0, 2)),
        jnp.transpose(small, (1, 0, 2)),
        normed,
        d_branch,
        jnp.broadcast_to(tag[:, None], (count, 128)),
        jnp.stack(masks, axis=1),
        own(conv_weight),
        own(conv_bias)[None, :],
        rank_rows,
        0,
    )
    w_in = w_in.reshape(-1, in_master.shape[2])
    normed_all = normed_all.reshape(span, -1)
    kinds_all = tags_all[:, :, 0].reshape(span)
    w_x_kinds = w_small[:, :, :rank_rows].transpose(1, 0, 2, 3).reshape(3, -1, channels)
    w_dt_kinds = w_small[:, :, rank_rows : rank_rows + step_rows].transpose(1, 0, 2, 3)
    w_dt_kinds = w_dt_kinds.reshape(3, DT_RANK, channels)
    kinds = kinds_all[:, None] == jnp.arange(3, dtype=BF)[None, :]

    kinds_parts = from_partners(kinds_all[:, None])
    features = swap_features(normed_all)

    taps = own(conv_weight)
    xs_value = xs.astype(F32)
    extended = jnp.concatenate([jnp.zeros((width - 1, channels), F32), xs_value], axis=0)
    pre = own(conv_bias)[None, :]
    for offset in range(width):
        begin = width - 1 - offset
        pre = (
            pre + taps[begin][None, :] * extended[begin : begin + span] * masks[offset][:, None]
        )

    rank = w_x_kinds.shape[1]
    across = kinds.T[:, None, :]
    rates = proj[:DT_RANK].T
    maps = proj[DT_RANK:].astype(F32)
    rates_kinds = split_kinds(rates, kinds, 1)
    bias = jnp.where(kinds[:, :, None], dt_bias.astype(BF).astype(F32)[None], 0.0).sum(axis=1)
    dtp = (contract(rates_kinds, w_dt_kinds.reshape(3 * DT_RANK, channels), 1, 0) + bias).astype(BF)

    blocks = span // STEPS
    to_columns = lambda rows: rows.reshape(-1, blocks, STEPS).transpose(1, 0, 2)
    b_columns = to_columns(maps[:STATE])
    c_columns = to_columns(maps[STATE:])
    keep = masks[1][:, None]
    a_own = own(a_log)
    skip_own = own(d_skip)[None, :]
    gated, y_value, heads = scan_forward(dtp, inner, b_columns, c_columns, keep, a_own, skip_own, z)

    branch, d_gated, grad_out = gate(d_branch_all.reshape(span, -1), gated, tags_all, w_out)
    branch = lax.psum_scatter(branch, "wide", scatter_dimension=0, tiled=True)
    result = x_in + branch.astype(F32)
    out_grad = scatter_master(grad_out).astype(F32)

    d_dtp, d_scan, d_z, d_columns, alog_part, skip_part = scan_backward(
        dtp, inner, b_columns, c_columns, keep, a_own, skip_own, z, y_value, d_gated, heads
    )
    d_dtp = jnp.where(living[:, None], d_dtp, jnp.zeros((), BF))
    d_dtp, features, kinds_parts = lax.optimization_barrier((d_dtp, features, kinds_parts))
    feature_kinds = [
        split_kinds(rows, tags == jnp.arange(3, dtype=BF)[None, :], 1)
        for rows, tags in zip(features, kinds_parts)
    ]
    d_maps = d_columns.reshape(-1, 2, d_columns.shape[2] // STATE, STATE)
    d_maps = d_maps.transpose(1, 3, 0, 2).reshape(2 * STATE, span)
    by_kind = contract(w_dt_kinds.reshape(3 * DT_RANK, channels), d_dtp, 1, 1)
    d_rates = jnp.sum(jnp.where(across, by_kind.reshape(3, DT_RANK, span), 0.0), axis=0)
    d_proj = sum_wide(jnp.concatenate([d_rates, d_maps], axis=0).astype(BF), 2)
    d_proj = jnp.where(living[None], d_proj, jnp.zeros((), BF)).T
    grad_dt = contract(rates_kinds, d_dtp, 0, 0).reshape(3, dp, step_rows, channels)
    bias_part = jnp.stack(
        [jnp.sum(jnp.where(kinds[:, k : k + 1], d_dtp.astype(F32), 0.0), axis=0) for k in range(3)]
    )
    d_proj_kinds = split_kinds(d_proj, kinds, 1)
    d_inner = contract(d_proj_kinds, w_x_kinds.reshape(3 * rank, channels), 1, 0).astype(BF)
    grad_x = contract(d_proj_kinds, inner, 0, 0)
    grad_x = grad_x.reshape(3, dp, rank_rows, channels)

    d_pre = (d_inner.astype(F32) + d_scan) * silu_slope(pre)
    further = jnp.concatenate([d_pre, jnp.zeros((width - 1, channels), F32)], axis=0)
    conv_rows = []
    d_xs = jnp.zeros_like(xs_value)
    for offset in range(width):
        begin = width - 1 - offset
        conv_rows.append(
            jnp.sum(d_pre * masks[offset][:, None] * extended[begin : begin + span], axis=0)
        )
        masked = further * later[offset][:, None]
        d_xs = d_xs + taps[begin][None, :] * masked[offset : offset + span]
    conv_part = jnp.stack(conv_rows[::-1], axis=0)
    conv_bias_part = jnp.sum(d_pre, axis=0)
    d_xs = jnp.where(living[:, None], d_xs, 0.0).astype(BF)
    d_z = jnp.where(living[:, None], d_z, jnp.zeros((), BF))
    d_mixed = halves_back(d_xs, d_z, wide)
    mixed_parts = from_partners(d_mixed)
    grad_in = 0.0
    for pair in range(0, dp, 2):
        left = jnp.concatenate(feature_kinds[pair : pair + 2], axis=0)
        grad_in = grad_in + contract(left, jnp.concatenate(mixed_parts[pair : pair + 2], axis=0), 0, 0)
    in_grad = jnp.transpose(grad_in.reshape(3, -1, d_mixed.shape[1]), (1, 0, 2))

    d_normed = jnp.zeros((span, x_in.shape[1]), F32)
    w_in_kinds = w_in.reshape(dp, 3, -1, w_in.shape[1])
    for kind in range(3):
        picked = jnp.where(kinds[:, kind : kind + 1], d_mixed, jnp.zeros((), BF))
        d_normed = d_normed + contract(
            picked, w_in_kinds[:, kind].reshape(-1, w_in.shape[1]), 1, 1
        )
    d_normed = d_normed.astype(BF)
    gain_part = jnp.sum(d_normed.astype(F32) * normed_all.astype(F32), axis=0) / norm_gain
    table = [conv_part, conv_bias_part[None], alog_part, skip_part, bias_part]
    table.append(gain_part.reshape(-1, channels))
    table = jnp.concatenate(table, axis=0)
    kept = table.shape[0]
    table = jnp.pad(table, ((0, -kept % 8), (0, 0)))
    small = jnp.concatenate([grad_x, grad_dt], axis=2).transpose(1, 0, 2, 3)
    small = jnp.pad(small, ((0, 0), (0, 0), (0, -small.shape[2] % 16), (0, 0))).astype(BF)
    d_normed, tables, small = finish(d_normed.reshape(wide, count, -1), table, small, 3)
    xproj_grad = jnp.transpose(small[:, :rank_rows], (1, 0, 2))
    dtproj_grad = jnp.transpose(small[:, rank_rows : rank_rows + step_rows], (1, 0, 2))
    d_normed = d_normed.astype(BF).astype(F32)
    scaled_back = d_normed * norm_gain[None, :]
    x_grad = cotangent + scale * (
        scaled_back - x_in * scale * scale * jnp.mean(scaled_back * x_in, axis=1, keepdims=True)
    )

    edge = width + 1 + STATE + 1
    shared = tables[:, :edge].transpose(1, 0, 2).reshape(edge, INNER)
    bias_grad = lax.dynamic_index_in_dim(tables, place, 0, False)[edge : edge + 3]
    gain_grad = jnp.sum(tables[:, edge + 3 : kept], axis=0).reshape(-1)
    return (
        result,
        x_grad,
        gain_grad,
        shared[:width],
        shared[width],
        shared[width + 1 : width + 1 + STATE],
        shared[width + 1 + STATE],
        in_grad,
        xproj_grad,
        dtproj_grad,
        bias_grad,
        out_grad,
    )


def solution(mesh):
    in_specs = (
        P(("dp", "wide"), None),
        P("dp", None),
        P(("dp", "wide")),
        P(),
        P(),
        P(),
        P(),
        P(),
        P("dp", None, "wide"),
        P("dp", None, "wide"),
        P("dp", None, "wide"),
        P(None, "wide"),
        P("dp", None, "wide"),
        P(("dp", "wide"), None),
    )
    out_specs = (
        P(("dp", "wide"), None),
        P(("dp", "wide"), None),
        P(),
        P(),
        P(),
        P(),
        P(),
        P("dp", None, "wide"),
        P("dp", None, "wide"),
        P("dp", None, "wide"),
        P(None, "wide"),
        P("dp", None, "wide"),
    )
    return jax.shard_map(body, mesh=mesh, in_specs=in_specs, out_specs=out_specs, check_vma=False)
```

time: 769 us -> 561 us (0.73)
  blocking collectives: 132 us -> 0 us
  Pallas kernels: 273 us -> 372 us
  waiting for transfers between devices: 87.3 us -> 5.24 us
  matrix products: 106 us -> 58.2 us
  local copies, waits for them, and re-layouts: 66.4 us -> 44 us
  starting transfers between devices: 34 us -> 15.8 us
    pallas_call x1 -> x3, Pallas kernels: 96.3 us -> 283 us  [the longest x1 176 us: front(): pl.pallas_call(functools.partial(front_kernel, dp, wide, rank_rows), out_...]
    psum x2 -> x0, blocking collectives: 84.9 us -> none  [the longest x1 47.4 us: body(): shared = lax.psum(shared, 'dp')]
    pallas_call x1, Pallas kernels: 105 us -> 46.9 us  [scan_backward(): pl.pallas_call(scan_backward_kernel, grid=(nb,), in_specs=[row, row, col,...]
    dot_general x17 -> x10, matrix products: 106 us -> 58.2 us  [contract(): lax.dot_general(left, right, (((left_dim,), (right_dim,)), ((), ())), pre...]
    all_gather x1 -> x0, blocking collectives: 47.3 us -> none  [body(): lax.all_gather(shared[:width + STATE + 2], 'wide', axis=1, tiled=True)]
    ppermute x2 -> x0, waiting for transfers between devices: 36.6 us -> none  [the longest x1 36.6 us: halves_out(): got_b = lax.ppermute(jnp.where(low, second, first), 'wide', odd)]
    ppermute x9, waiting for transfers between devices: 33 us -> 0.02 us  [hop(): return lax.ppermute(block, 'dp', [(d, flip(d)) for d in range(devices)])]
    pallas_call x2 -> x1, Pallas kernels: 53.1 us -> 25 us  [sum_wide(): pl.pallas_call(functools.partial(sum_wide_kernel, wide), out_shape=jax.Sh...]
  transfers between devices with their start and end apart: 19 -> 13, of which waited for: 6 -> 1; matrix products, arithmetic and copies ran while one was open for 24% -> 21% of each run, Pallas kernels for 19% -> 27%
where the time goes in v3:
time: 561 us; the launch traced here: 554 us
  Pallas kernels  372 us (66%)
  matrix products  58.2 us (10%)
  local copies, waits for them, and re-layouts  44 us (8%)
  other arithmetic  43.5 us (8%)
  starting transfers between devices  15.8 us (3%)
  between operations  15.1 us (3%)
    pallas_call x1, Pallas kernels, front(): pl.pallas_call(functools.partial(front_kernel, dp, wide, rank_rows), out_...  176 us
    pallas_call x1, Pallas kernels, finish(): pl.pallas_call(functools.partial(finish_kernel, dp, wide), out_shape=[jax...  78.6 us
    dot_general x10, matrix products, contract(): lax.dot_general(left, right, (((left_dim,), (right_dim,)), ((), ())), pre...  58.2 us
    pallas_call x1, Pallas kernels, scan_backward(): pl.pallas_call(scan_backward_kernel, grid=(nb,), in_specs=[row, row, col,...  46.9 us
    pallas_call x1, Pallas kernels, gate(): pl.pallas_call(gate_kernel, out_shape=[jax.ShapeDtypeStruct(back.shape, B...  28.5 us
    pallas_call x1, Pallas kernels, sum_wide(): pl.pallas_call(functools.partial(sum_wide_kernel, wide), out_shape=jax.Sh...  25 us
    pallas_call x1, Pallas kernels, scan_forward(): pl.pallas_call(scan_forward_kernel, grid=(N // T,), in_specs=[row, row, c...  17.4 us
  transfers between devices with their start and end apart: 13, of which 1 were waited for; matrix products, arithmetic and copies ran while one was open for 21% of the time, Pallas kernels for 27%

profile of v3, /device:TPU:0, one launch (start us, length us, event | category | flops | bytes accessed | tf_op | source)
XLA Modules:
  0.0 554.3 jit_solution(1160166851185894476)
XLA Ops:
  7.3 1.5 multiply_reduce_fusion.6
  8.8 0.8 reduce-window.4
  11.0 1.3 constant_dynamic-slice_fusion.6.refs_7_
  12.3 1.3 dynamic_slice.31
  13.6 0.8 fusion.52.refs_2_
  14.5 0.9 multiply_convert_fusion.refs_3_
  16.1 2.1 select_convert_fusion.refs_4_
  18.2 1.3 pad_maximum_fusion.1.refs_6_
  20.2 176.0 %front.1 = (bf16[4,3,512,1024]{3,2,1,0:T(8,128)(2,1)}, bf16[4,3,512,512]{3,2,1,0:T(8,128)(2,1)}, bf16[4,3,80,512]{3,2,1,0:T(8,128)(2,1)}, bf16[8,128,2048]{2,1,0...) custom-call(f32[3,512,1024]{2,1,0:T(8,128)} %bitcast.124, ...), custom_call_target="tpu_custom_call" | custom-call | tf_op jit(solution)/shard_map/front/pallas_call | solution.py:596
  196.2 1.0 slice_bitcast_fusion.4
  197.2 0.9 slice_convert_fusion
  198.0 1.1 slice_reduce_fusion
  199.2 2.1 select_reduce_fusion
  201.3 1.0 broadcast_select_fusion.11
  202.2 1.0 slice_bitcast_fusion.2
  203.3 0.8 copy.88
  204.6 0.8 dynamic_slice.33
  205.4 2.8 add_convert_fusion.1.dtp_ref
  208.2 17.4 %scan_forward.1 = (bf16[1024,512]{1,0:T(8,128)(2,1)S(1)}, f32[1024,512]{1,0:T(8,128)}, f32[32,16,512]{2,1,0:T(8,128)S(1)}) custom-call(bf16[1024,512]{1,0:T(8,128)(2,1)S(1)} %add_convert_fusion.1.dtp_ref, bf16[1024,512]{1,0:T(8,128)(2,1)S(1)} %copy-done.2, f32[32,16,32]{2,1,0:T(8,128)S(1)} %bitcast.118, f32[32,16,32]{2,1,0:T(8,128)S(1)} %bitcast.120, ...), custom_call_target="tpu_custom_call" | custom-call | tf_op jit(solution)/shard_map/scan_forward/pallas_call | solution.py:55
  225.6 1.0 copy-done.5
  226.6 1.0 copy-done.6
  227.5 28.5 %gate.1 = (bf16[1024,2048]{1,0:T(8,128)(2,1)}, bf16[1024,512]{1,0:T(8,128)(2,1)}, bf16[4,3,512,512]{3,2,1,0:T(8,128)(2,1)}) custom-call(bf16[1024,2048]{1,0:T(8,128)(2,1)} %bitcast.176, bf16[1024,512]{1,0:T(8,128)(2,1)} %copy-done.6, bf16[8,128,128]{2,1,0:T(8,128)(2,1)} %get-tuple-element.47.tag_ref, bf16[4,3,512,512]{3,2,1,0:T(8,128)(2,1)} %get-tuple-element.53.w_ref), custom_call_target="tpu_custom_call" | custom-call | flops 19327352832 | bytes 25165824 | tf_op jit(solution)/shard_map/gate/pallas_call | solution.py:894
  257.1 1.8 collective-permute-start.4
  258.9 4.3 constant_dynamic-slice_fusion.1
  263.4 1.7 collective-permute-start.2
  265.8 1.9 slice_bitcast_fusion
  267.7 46.9 %scan_backward.1 = (bf16[1024,512]{1,0:T(8,128)(2,1)S(1)}, f32[1024,512]{1,0:T(8,128)}, bf16[1024,512]{1,0:T(8,128)(2,1)S(1)}, f32[8,2,2048]{2,1,0:T(2,128)S(1)}...) custom-call(bf16[1024,512]{1,0:T(8,128)(2,1)S(1)} %add_convert_fusion.1.dtp_ref, bf16[1024,512]{1,0:T(8,128)(2,1)S(1)} %copy-done.2, ...), custom_call_target="tpu_custom_call" | custom-call | tf_op jit(solution)/shard_map/scan_backward/pallas_call | solution.py:149
  315.0 9.5 %fusion.72 = (bf16[4,1,512,1024]{3,2,1,0:T(8,128)(2,1)}, bf16[4,1,512,1024]{3,2,1,0:T(8,128)(2,1)}, bf16[4,1,512,1024]{3,2,1,0:T(8,128)(2,1)}) fusion(bf16[4,3,512,1024]{3,2,1,0:T(8,128)(2,1)} %get-tuple-element.65), kind=kLoop, calls=%fused_computation.179 | loop fusion | bytes 25165824 | tf_op jit(solution)/shard_map/slice | solution.py:1135
  324.9 0.9 fusion.75
  325.9 2.9 convert_element_type.182
  329.8 1.8 select_reduce_fusion.1
  331.6 25.0 %sum_wide.1 = bf16[160,1024]{1,0:T(8,128)(2,1)S(1)} custom-call(bf16[160,1024]{1,0:T(8,128)(2,1)S(1)} %pad_maximum_fusion.2.x_ref), custom_call_target="tpu_custom_call" | custom-call | tf_op jit(solution)/shard_map/sum_wide/pallas_call | solution.py:691
  356.8 3.6 fusion.70
  360.4 2.9 broadcast_select_fusion.7
  363.3 9.5 %collective-permute-start.6 = (bf16[1024,512]{1,0:T(8,128)(2,1)}, bf16[1024,512]{1,0:T(8,128)(2,1)}, u32[]{:S(2)}, u32[]{:S(2)}) collective-permute-start(bf16[1024,512]{1,0:T(8,128)(2,1)} %get-tuple-element.102), channel_id=1, source_target_pairs={{0,0},{2,1},{4,2},{6,3},{1,4},{3,5},{5,6},{7,7},{8,8},{10,9},{12,1... | collective-permute-start | bytes 3145736 | tf_op jit(solution)/shard_map/ppermute | solution.py:984
  372.8 1.2 broadcast_select_fusion.6
  374.2 1.7 copy.99
  376.0 2.1 fusion.21
  378.1 1.8 convolution_convert_fusion.2
  380.7 1.9 broadcast_select_fusion.2
  382.6 1.3 copy.98
  383.9 1.5 copy.101
  385.4 1.5 copy.100
  386.9 1.1 pad.17.small_ref
  388.5 1.9 broadcast_select_fusion.3
  390.5 1.8 broadcast_select_fusion
  392.3 1.9 broadcast_select_fusion.1
  394.2 5.2 collective-permute-done.7
  399.4 1.7 broadcast_select_fusion.9
  401.1 1.6 pad_maximum_fusion
  402.7 1.1 collective-permute-start.9
  404.0 6.8 %fusion.33 = f32[1024,2048]{1,0:T(8,128)} fusion(bf16[2048,1024]{1,0:T(8,128)(2,1)S(1)} %bitcast.129, pred[1024]{0:T(1024)(128)(4,1)S(1)} %copy-done.35, bf16[1024,512]{1,0:T(8,128)(2,1)S(1)} %get-tuple-element.120, bf16[1024,512]{1,0:T(8,128)(2,1)S(1)} %get-tuple-element.119), kind=kOutput, calls=%fused_computation.50 | convolution fusion | flops 4300210176 | bytes 14681088 | tf_op jit(solution)/shard_map/dot_general | solution.py:911
  410.8 6.8 %fusion.31 = f32[1024,2048]{1,0:T(8,128)} fusion(bf16[2048,1024]{1,0:T(8,128)(2,1)S(1)} %bitcast.128, pred[1024]{0:T(1024)(128)(4,1)S(1)} %copy-done.33, bf16[1024,512]{1,0:T(8,128)(2,1)S(1)} %get-tuple-element.120, bf16[1024,512]{1,0:T(8,128)(2,1)S(1)} %get-tuple-element.119), kind=kOutput, calls=%fused_computation.48 | convolution fusion | flops 4300210176 | bytes 14681088 | tf_op jit(solution)/shard_map/dot_general | solution.py:911
  417.5 11.8 %multiply_reduce_fusion = (f32[2048]{0:T(1024)S(1)}, bf16[1024,2048]{1,0:T(8,128)(2,1)}) fusion(bf16[8,128,2048]{2,1,0:T(8,128)(2,1)S(1)} %copy-done.10, bf16[2048,1024]{1,0:T(8,128)(2,1)} %bitcast.127, pred[1024]{0:T(1024)(128)(4,1)S(1)} %get-tuple-element.91, bf16[1024,512]{1,0:T(8,128)(2,1)S(1)} %get-tuple-element.120, ...), kind=kOutput, calls=%fused_computation | convolution fusion | flops 4314888192 | bytes 31466496 | tf_op jit(solution)/shard_map/dot_general | solution.py:911
  430.4 78.6 %finish.1 = (f32[128,2048]{1,0:T(8,128)}, f32[8,32,512]{2,1,0:T(8,128)}, f32[3,80,512]{2,1,0:T(8,128)}) custom-call(bf16[8,128,2048]{2,1,0:T(8,128)(2,1)} %bitcast.126, f32[32,512]{1,0:T(8,128)} %pad.16.table_ref, bf16[4,3,80,512]{3,2,1,0:T(8,128)(2,1)} %pad.17.small_ref), custom_call_target="tpu_custom_call" | custom-call | tf_op jit(solution)/shard_map/finish/pallas_call | solution.py:815
  509.1 1.0 slice_reduce_fusion.1
  510.7 1.0 slice_bitcast_fusion.1
  512.4 0.7 copy.111
  513.1 1.7 multiply_reduce_fusion.5
  515.5 1.4 dynamic-slice_bitcast_fusion
  518.3 11.2 %fusion = f32[1536,1024]{1,0:T(8,128)} fusion(bf16[1024,1536]{0,1:T(8,128)(2,1)S(1)} %bitcast.130, bf16[1024,1536]{0,1:T(8,128)(2,1)S(1)} %bitcast.133, bf16[1024,1024]{1,0:T(8,128)(2,1)} %collective-permute-done.8, bf16[1024,512]{1,0:T(8,128)(2,1)S(1)} %get-tuple-element.120, bf16[1024,512]{1,0:T(8,128)(2,1)S(1)} %get-tuple-element.119), kind=kOutput, calls=%fused_computation.2 | convolution fusion | flops 6467616768 | bytes 16777216 | tf_op jit(solution)/shard_map/dot_general | solution.py:911
  529.5 11.2 %fusion.8 = f32[1536,1024]{1,0:T(8,128)} fusion(f32[1536,1024]{1,0:T(8,128)} %fusion, bf16[1024,1536]{0,1:T(8,128)(2,1)S(1)} %bitcast.131, bf16[1024,1536]{0,1:T(8,128)(2,1)S(1)} %bitcast.132, bf16[1024,1024]{1,0:T(8,128)(2,1)S(1)} %collective-permute-done.10, bf16[1024,1024]{1,0:T(8,128)(2,1)} %collective-permute-done.9), kind=kOutput, calls=%fused_computation.11 | convolution fusion | flops 6464995328 | bytes 23068672 | tf_op jit(solution)/shard_map/dot_general | solution.py:911
  540.7 3.1 multiply_add_fusion
  543.7 3.5 convert_bitcast_fusion
  (163 shorter events, 13.3 us)
Async XLA Ops:
  7.2 197.4 %copy-start = (f32[16,4096]{1,0:T(8,128)S(1)}, f32[16,4096]{1,0:T(8,128)}, u32[]{:S(2)}) copy-start(f32[16,4096]{1,0:T(8,128)} %param.20) | copy-start | bytes 786436
  7.2 7.3 %copy-start.7 = (f32[128,2048]{1,0:T(8,128)S(1)}, f32[128,2048]{1,0:T(8,128)}, u32[]{:S(2)}) copy-start(f32[128,2048]{1,0:T(8,128)} %param.14) | copy-start | bytes 3145732
  7.2 6.4 %copy-start.28 = (f32[32,3,512]{2,0,1:T(8,128)S(1)}, f32[32,3,512]{2,0,1:T(8,128)}, u32[]{:S(2)}) copy-start(f32[32,3,512]{2,0,1:T(8,128)} %param.24) | copy-start | bytes 589828
  7.2 6.4 %copy-start.27 = (f32[40,3,512]{2,0,1:T(8,128)S(1)}, f32[40,3,512]{2,0,1:T(8,128)}, u32[]{:S(2)}) copy-start(f32[40,3,512]{2,0,1:T(8,128)} %param.23) | copy-start | bytes 737284
  7.2 7.2 %copy-start.29 = (f32[2048]{0:T(1024)S(1)}, f32[2048]{0:T(1024)}, u32[]{:S(2)}) copy-start(f32[2048]{0:T(1024)} %param.17) | copy-start | bytes 24580
  7.2 533.4 %reduce-scatter.3.cloned.1.call-start = ((), (), s32[]{:S(2)}) async-start(), calls=%async_computation.2 | async-start | bytes 4718592 | tf_op jit(solution)/shard_map/reduce_scatter | solution.py:1079
  8.8 6.6 %copy-start.36 = (f32[128]{0:T(128)}, f32[128]{0:T(128)S(1)}, u32[]{:S(2)}) copy-start(f32[128]{0:T(128)S(1)} %add_rsqrt_fusion) | copy-start | bytes 1540
  10.2 5.2 copy-start.38
  20.2 179.0 %copy-start.30 = (f32[3,512]{1,0:T(4,128)S(1)}, f32[3,512]{1,0:T(4,128)}, u32[]{:S(2)}) copy-start(f32[3,512]{1,0:T(4,128)} %param.25) | copy-start | bytes 18436
  205.4 2.8 copy-start.2
  225.6 1.0 copy-start.5
  226.6 1.0 copy-start.6
  256.1 287.7 %reduce-scatter.5.cloned.1.call-start = ((), (), s32[]{:S(2)}) async-start(), calls=%async_computation.3 | async-start | bytes 7864320 | tf_op jit(solution)/shard_map/reduce_scatter | solution.py:941
  256.6 73.1 %collective-permute-start.3 = (bf16[1024,1]{0,1:T(2,128)(2,1)S(1)}, bf16[1024,1]{0,1:T(2,128)(2,1)S(1)}, u32[]{:S(2)}, u32[]{:S(2)}) collective-permute-start(bf16[1024,1]{0,1:T(2,128)(2,1)S(1)} %bitcast.151), channel_id=1, source_target_pairs={{0,8},{8,0},{16,24},{24,16},{1,9},{9,1},{17,25},{25,17},{2,10},{10... | collective-permute-start | bytes 6152 | tf_op jit(solution)/shard_map/ppermute | solution.py:946
  257.1 67.4 %collective-permute-start.4 = (bf16[1024,1]{0,1:T(2,128)(2,1)S(1)}, bf16[1024,1]{0,1:T(2,128)(2,1)S(1)}, u32[]{:S(2)}, u32[]{:S(2)}) collective-permute-start(bf16[1024,1]{0,1:T(2,128)(2,1)S(1)} %bitcast.152), channel_id=1, source_target_pairs={{0,16},{8,24},{16,0},{24,8},{1,17},{9,25},{17,1},{25,9},{2,18},{10... | collective-permute-start | bytes 6152 | tf_op jit(solution)/shard_map/ppermute | solution.py:946
  263.3 66.4 %collective-permute-start = (bf16[1024,512]{1,0:T(8,128)(2,1)}, bf16[1024,512]{1,0:T(8,128)(2,1)}, u32[]{:S(2)}, u32[]{:S(2)}) collective-permute-start(bf16[1024,512]{1,0:T(8,128)(2,1)} %get-tuple-element.117), channel_id=1, source_target_pairs={{0,8},{8,0},{16,24},{24,16},{1,9},{9,1},{17,25},{25,17},{2,10},{10... | collective-permute-start | bytes 3145736 | tf_op jit(solution)/shard_map/ppermute | solution.py:946
  263.3 66.4 %collective-permute-start.1 = (bf16[1024,512]{1,0:T(8,128)(2,1)}, bf16[1024,512]{1,0:T(8,128)(2,1)}, u32[]{:S(2)}, u32[]{:S(2)}) collective-permute-start(bf16[1024,512]{1,0:T(8,128)(2,1)} %get-tuple-element.116), channel_id=1, source_target_pairs={{0,16},{8,24},{16,0},{24,8},{1,17},{9,25},{17,1},{25,9},{2,18},{10... | collective-permute-start | bytes 3145736 | tf_op jit(solution)/shard_map/ppermute | solution.py:946
  263.4 66.3 %collective-permute-start.2 = (bf16[1024,512]{1,0:T(8,128)(2,1)}, bf16[1024,512]{1,0:T(8,128)(2,1)}, u32[]{:S(2)}, u32[]{:S(2)}) collective-permute-start(bf16[1024,512]{1,0:T(8,128)(2,1)} %get-tuple-element.115), channel_id=1, source_target_pairs={{0,24},{8,16},{16,8},{24,0},{1,25},{9,17},{17,9},{25,1},{2,26},{10... | collective-permute-start | bytes 3145736 | tf_op jit(solution)/shard_map/ppermute | solution.py:946
  314.6 9.9 %copy-start.3 = (bf16[1024,512]{1,0:T(8,128)(2,1)}, bf16[1024,512]{1,0:T(8,128)(2,1)S(1)}, u32[]{:S(2)}) copy-start(bf16[1024,512]{1,0:T(8,128)(2,1)S(1)} %get-tuple-element.64) | copy-start | bytes 3145732
  314.8 14.9 %copy-start.13 = (bf16[1024,512]{1,0:T(8,128)(2,1)}, bf16[1024,512]{1,0:T(8,128)(2,1)S(1)}, u32[]{:S(2)}) copy-start(bf16[1024,512]{1,0:T(8,128)(2,1)S(1)} %broadcast_select_fusion.5) | copy-start | bytes 3145732
  324.5 51.5 %copy-start.32 = (pred[1024]{0:T(1024)(128)(4,1)}, pred[1024]{0:T(1024)(128)(4,1)S(1)}, u32[]{:S(2)}) copy-start(pred[1024]{0:T(1024)(128)(4,1)S(1)} %get-tuple-element.92) | copy-start | bytes 3076
  324.5 51.5 %copy-start.34 = (pred[1024]{0:T(1024)(128)(4,1)}, pred[1024]{0:T(1024)(128)(4,1)S(1)}, u32[]{:S(2)}) copy-start(pred[1024]{0:T(1024)(128)(4,1)S(1)} %get-tuple-element.93) | copy-start | bytes 3076
  324.6 5.2 collective-permute-start.5
  325.9 3.6 copy-start.22
  329.7 27.0 %copy-start.39 = (f32[1024,512]{1,0:T(8,128)S(1)}, f32[1024,512]{1,0:T(8,128)}, u32[]{:S(2)}) copy-start(f32[1024,512]{1,0:T(8,128)} %get-tuple-element.62) | copy-start | bytes 6291460
  331.5 25.2 %copy-start.21 = (f32[1024,512]{1,0:T(8,128)S(1)}, f32[1024,512]{1,0:T(8,128)}, u32[]{:S(2)}) copy-start(f32[1024,512]{1,0:T(8,128)} %convert_element_type.182) | copy-start | bytes 6291460
  331.5 25.2 %copy-start.23 = (bf16[1024,512]{1,0:T(8,128)(2,1)S(1)}, bf16[1024,512]{1,0:T(8,128)(2,1)}, u32[]{:S(2)}) copy-start(bf16[1024,512]{1,0:T(8,128)(2,1)} %get-tuple-element.63) | copy-start | bytes 3145732
  331.6 25.2 %copy-start.31 = (f32[512]{0:T(512)S(1)}, f32[512]{0:T(512)}, u32[]{:S(2)}) copy-start(f32[512]{0:T(512)} %dynamic_slice.31) | copy-start | bytes 6148
  356.7 3.6 copy-start.24
  356.8 3.6 copy-start.4
  363.3 30.9 %collective-permute-start.6 = (bf16[1024,512]{1,0:T(8,128)(2,1)}, bf16[1024,512]{1,0:T(8,128)(2,1)}, u32[]{:S(2)}, u32[]{:S(2)}) collective-permute-start(bf16[1024,512]{1,0:T(8,128)(2,1)} %get-tuple-element.102), channel_id=1, source_target_pairs={{0,0},{2,1},{4,2},{6,3},{1,4},{3,5},{5,6},{7,7},{8,8},{10,9},{12,1... | collective-permute-start | bytes 3145736 | tf_op jit(solution)/shard_map/ppermute | solution.py:984
  374.0 4.2 copy-start.20
  374.0 25.4 %collective-permute-start.7 = (bf16[1024,512]{1,0:T(8,128)(2,1)}, bf16[1024,512]{1,0:T(8,128)(2,1)}, u32[]{:S(2)}, u32[]{:S(2)}) collective-permute-start(bf16[1024,512]{1,0:T(8,128)(2,1)} %broadcast_select_fusion.6), channel_id=1, source_target_pairs={{1,0},{3,1},{5,2},{7,3},{0,4},{2,5},{4,6},{6,7},{9,8},{11,9},{13,1... | collective-permute-start | bytes 3145736 | tf_op jit(solution)/shard_map/ppermute | solution.py:985
  375.9 4.0 copy-start.25
  380.6 2.0 copy-start.11
  386.9 1.6 copy-start.12
  401.1 2.9 copy-start.15
  401.1 2.9 copy-start.35
  402.7 115.5 %collective-permute-start.8 = (bf16[1024,1024]{1,0:T(8,128)(2,1)}, bf16[1024,1024]{1,0:T(8,128)(2,1)}, u32[]{:S(2)}, u32[]{:S(2)}) collective-permute-start(bf16[1024,1024]{1,0:T(8,128)(2,1)} %pad_maximum_fusion), channel_id=1, source_target_pairs={{0,8},{8,0},{16,24},{24,16},{1,9},{9,1},{17,25},{25,17},{2,10},{10... | collective-permute-start | bytes 6291464 | tf_op jit(solution)/shard_map/ppermute | solution.py:946
  402.7 112.7 %collective-permute-start.9 = (bf16[1024,1024]{1,0:T(8,128)(2,1)}, bf16[1024,1024]{1,0:T(8,128)(2,1)}, u32[]{:S(2)}, u32[]{:S(2)}) collective-permute-start(bf16[1024,1024]{1,0:T(8,128)(2,1)} %pad_maximum_fusion), channel_id=1, source_target_pairs={{0,16},{8,24},{16,0},{24,8},{1,17},{9,25},{17,1},{25,9},{2,18},{10... | collective-permute-start | bytes 6291464 | tf_op jit(solution)/shard_map/ppermute | solution.py:946
  404.0 6.8 %copy-start.14 = (bf16[4,1,512,1024]{3,2,1,0:T(8,128)(2,1)S(1)}, bf16[4,1,512,1024]{3,2,1,0:T(8,128)(2,1)}, u32[]{:S(2)}) copy-start(bf16[4,1,512,1024]{3,2,1,0:T(8,128)(2,1)} %get-tuple-element.113) | copy-start | bytes 12582916
  404.0 6.8 %copy-start.33 = (pred[1024]{0:T(1024)(128)(4,1)S(1)}, pred[1024]{0:T(1024)(128)(4,1)}, u32[]{:S(2)}) copy-start(pred[1024]{0:T(1024)(128)(4,1)} %copy-done.32) | copy-start | bytes 3076
  410.8 6.8 %copy-start.10 = (bf16[8,128,2048]{2,1,0:T(8,128)(2,1)S(1)}, bf16[8,128,2048]{2,1,0:T(8,128)(2,1)}, u32[]{:S(2)}) copy-start(bf16[8,128,2048]{2,1,0:T(8,128)(2,1)} %get-tuple-element.59) | copy-start | bytes 12582916
  430.4 87.8 %copy-start.19 = (bf16[1024,3,512]{0,2,1:T(8,128)(2,1)S(1)}, bf16[1024,3,512]{0,2,1:T(8,128)(2,1)}, u32[]{:S(2)}) copy-start(bf16[1024,3,512]{0,2,1:T(8,128)(2,1)} %broadcast_select_fusion.3) | copy-start | bytes 9437188
  509.1 4.1 copy-start.8
  510.1 6.8 %copy-start.26 = (f32[3,80,512]{2,1,0:T(8,128)S(1)}, f32[3,80,512]{2,1,0:T(8,128)}, u32[]{:S(2)}) copy-start(f32[3,80,512]{2,1,0:T(8,128)} %get-tuple-element.78) | copy-start | bytes 1474564
  512.4 5.9 %copy-start.16 = (bf16[1024,3,512]{0,2,1:T(8,128)(2,1)S(1)}, bf16[1024,3,512]{0,2,1:T(8,128)(2,1)}, u32[]{:S(2)}) copy-start(bf16[1024,3,512]{0,2,1:T(8,128)(2,1)} %broadcast_select_fusion.2) | copy-start | bytes 9437188
  515.5 14.0 %collective-permute-start.10 = (bf16[1024,1024]{1,0:T(8,128)(2,1)}, bf16[1024,1024]{1,0:T(8,128)(2,1)S(1)}, u32[]{:S(2)}, u32[]{:S(2)}) collective-permute-start(bf16[1024,1024]{1,0:T(8,128)(2,1)} %collective-permute-done.9), channel_id=1, source_target_pairs={{0,8},{8,0},{16,24},{24,16},{1,9},{9,1},{17,25},{25,17},{2,10},{10... | collective-permute-start | bytes 6291464 | tf_op jit(solution)/shard_map/ppermute | solution.py:946
  518.3 11.2 %copy-start.17 = (bf16[1024,3,512]{0,2,1:T(8,128)(2,1)S(1)}, bf16[1024,3,512]{0,2,1:T(8,128)(2,1)}, u32[]{:S(2)}) copy-start(bf16[1024,3,512]{0,2,1:T(8,128)(2,1)} %broadcast_select_fusion) | copy-start | bytes 9437188
  518.3 11.2 %copy-start.18 = (bf16[1024,3,512]{0,2,1:T(8,128)(2,1)S(1)}, bf16[1024,3,512]{0,2,1:T(8,128)(2,1)}, u32[]{:S(2)}) copy-start(bf16[1024,3,512]{0,2,1:T(8,128)(2,1)} %broadcast_select_fusion.1) | copy-start | bytes 9437188
  529.4 11.2 %copy-start.9 = (f32[128,2048]{1,0:T(8,128)S(1)}, f32[128,2048]{1,0:T(8,128)}, u32[]{:S(2)}) copy-start(f32[128,2048]{1,0:T(8,128)} %get-tuple-element.68) | copy-start | bytes 3145732
  529.5 11.2 %copy-start.37 = (f32[128]{0:T(128)S(1)}, f32[128]{0:T(128)}, u32[]{:S(2)}) copy-start(f32[128]{0:T(128)} %copy-done.36) | copy-start | bytes 1540
  540.7 6.6 %copy-start.1 = (f32[16,4096]{1,0:T(8,128)S(1)}, f32[16,4096]{1,0:T(8,128)}, u32[]{:S(2)}) copy-start(f32[16,4096]{1,0:T(8,128)} %param.20) | copy-start | bytes 786436
Sparse Core Ops, SparseCore 0:
  256.2 92.5 reduce-scatter.2
  351.5 66.3 reduce-scatter.4

commit v4 on v3

--- a/solution.py
+++ b/solution.py
@@ -18,15 +18,36 @@
 STEPS=32
 HUGE=1e30
 
-def scan_forward_kernel(dtp_ref,u_ref,b_ref,c_ref,keep_ref,alog_ref,skip_ref,z_ref, gated_ref,y_ref,heads_ref, st, dec, inj, ys, a2):
+def own_lanes(channels):
+    return pl.ds(pl.multiple_of(lax.axis_index("wide")*channels,channels),channels)
+
+def split_columns(proj_ref,first,cols):
+    rows=proj_ref[first:first+cols.shape[1]].astype(F32)
+    for k in range(cols.shape[0]):
+        cols[k]=rows[:,k*STEPS:(k+1)*STEPS]
+
+def scan_forward_kernel(proj_ref,wdt_ref,dtb_ref,tag_ref,u_ref,masks_ref,alog_ref,skip_ref,z_ref, dtp_ref,gated_ref,y_ref,heads_ref, st, dec, inj, ys, a2, b_ref, c_ref):
     T,C=u_ref.shape
+    R=wdt_ref.shape[1]
+    S=alog_ref.shape[0]
     @pl.when(pl.program_id(0)==0)
     def _():
         st[...]=jnp.zeros_like(st)
-        a2[...]=-jnp.exp(alog_ref[...])*1.4426950408889634
-    delta=jax.nn.softplus(dtp_ref[...].astype(F32))
+        a2[...]=-jnp.exp(alog_ref[:,own_lanes(C)])*1.4426950408889634
+    split_columns(proj_ref,R,b_ref)
+    split_columns(proj_ref,R+S,c_ref)
+    tag=tag_ref[:,:1].astype(F32)
+    rates=proj_ref[:R]
+    dtp=jnp.zeros((T,C),F32)
+    for kind in range(3):
+        step=lax.dot_general(rates,wdt_ref[kind],(((0,),(0,)),((),())),preferred_element_type=F32)
+        step=step+dtb_ref[kind:kind+1].astype(BF).astype(F32)
+        dtp=dtp+jnp.where(tag==kind,step,0.0)
+    dtp=dtp.astype(BF)
+    dtp_ref[...]=dtp
+    delta=jax.nn.softplus(dtp.astype(F32))
     u=u_ref[...].astype(F32)
-    dec[...]=jnp.where(keep_ref[...]>0,delta,HUGE)
+    dec[...]=jnp.where(masks_ref[:,1:2]>0,delta,HUGE)
     inj[...]=delta*u
     def chunk(k,state):
         heads_ref[k]=state
@@ -40,25 +61,26 @@
             ys[pl.ds(base+j,1),:]=jnp.sum(c[:,j:j+1]*state,axis=0,keepdims=True)
         return state
     st[...]=lax.fori_loop(0,T//STEPS,chunk,st[...])
-    y=ys[...]+skip_ref[...]*u
+    y=ys[...]+skip_ref[:,own_lanes(C)]*u
     y_ref[...]=y
     z=z_ref[...].astype(F32)
     gated_ref[...]=(y*(z*jax.nn.sigmoid(z))).astype(BF)
 
-def scan_forward(dtp,u,b,c,keep,alog,skip,z,T=128):
+def scan_forward(proj,wdt,dtb,tags,u,masks,alog,skip,z,T=128):
     N,C=u.shape
     S=alog.shape[0]
     nk=N//STEPS; tk=T//STEPS
     row=pl.BlockSpec((T,C),lambda i:(i,0))
-    col=pl.BlockSpec((tk,S,STEPS),lambda i:(i,0,0))
-    whole=lambda s: pl.BlockSpec(s,lambda i:(0,0))
+    whole=lambda s: pl.BlockSpec(s,lambda i:(0,)*len(s))
+    tile=lambda lanes: pl.BlockSpec((T,lanes),lambda i:(i,0))
     return pl.pallas_call(scan_forward_kernel,grid=(N//T,),
-      in_specs=[row,row,col,col,pl.BlockSpec((T,1),lambda i:(i,0)),whole((S,C)),whole((1,C)),row],
-      out_specs=[row,row,pl.BlockSpec((tk,S,C),lambda i:(i,0,0))],
-      out_shape=[jax.ShapeDtypeStruct((N,C),BF),jax.ShapeDtypeStruct((N,C),F32),jax.ShapeDtypeStruct((nk,S,C),F32)],
-      scratch_shapes=[pltpu.VMEM((S,C),F32),pltpu.VMEM((T,C),F32),pltpu.VMEM((T,C),F32),pltpu.VMEM((T,C),F32),pltpu.VMEM((S,C),F32)],
+      in_specs=[pl.BlockSpec((proj.shape[0],T),lambda i:(0,i)),whole(wdt.shape),whole(dtb.shape),tile(tags.shape[1]),row,tile(masks.shape[1]),whole(alog.shape),whole(skip.shape),row],
+      out_specs=[row,row,row,pl.BlockSpec((tk,S,C),lambda i:(i,0,0))],
+      out_shape=[jax.ShapeDtypeStruct((N,C),BF),jax.ShapeDtypeStruct((N,C),BF),jax.ShapeDtypeStruct((N,C),F32),jax.ShapeDtypeStruct((nk,S,C),F32)],
+      scratch_shapes=[pltpu.VMEM((S,C),F32),pltpu.VMEM((T,C),F32),pltpu.VMEM((T,C),F32),pltpu.VMEM((T,C),F32),pltpu.VMEM((S,C),F32),pltpu.VMEM((tk,S,STEPS),F32),pltpu.VMEM((tk,S,STEPS),F32)],
       compiler_params=pltpu.CompilerParams(vmem_limit_bytes=48<<20),
-      name="scan_forward")(dtp,u,b,c,keep,alog,skip,z)
+      cost_estimate=pl.CostEstimate(flops=2500*N*C*S,bytes_accessed=16<<20,transcendentals=N*C*S),
+      name="scan_forward")(proj,wdt,dtb,tags,u,masks,alog,skip,z)
 
 def fold_lanes(values):
     total=values[:,:128]
@@ -74,8 +96,8 @@
     dims=(((1,),(1,)),((),()))
     return (lax.dot_general(ones,high,dims,preferred_element_type=F32)+lax.dot_general(ones,rest,dims,preferred_element_type=F32))[:1]
 
-def scan_backward_kernel(dtp_ref,u_ref,b_ref,c_ref,keep_ref,alog_ref,skip_ref,z_ref,y_ref,dg_ref,heads_ref,
-        ddtp_ref,dus_ref,dz_ref,dm_ref,dalog_ref,dskip_ref, run, dec, inj, dly, dys, sq, wa, sts, dcs, an2, an1, acc, pb, pc):
+def scan_backward_kernel(dtp_ref,u_ref,proj_ref,masks_ref,alog_ref,skip_ref,z_ref,y_ref,dg_ref,heads_ref,
+        ddtp_ref,dus_ref,dz_ref,dm_ref,extra_ref, run, dec, inj, dly, dys, sq, wa, sts, dcs, an2, an1, acc, pb, pc, b_ref, c_ref):
     T,C=u_ref.shape
     S=alog_ref.shape[0]
     first=pl.program_id(0)==0
@@ -84,13 +106,16 @@
     def _():
         run[...]=jnp.zeros_like(run)
         acc[...]=jnp.zeros_like(acc)
-        dskip_ref[...]=jnp.zeros_like(dskip_ref)
-        an1[...]=-jnp.exp(alog_ref[...])
+        extra_ref[...]=jnp.zeros_like(extra_ref)
+        an1[...]=-jnp.exp(alog_ref[:,own_lanes(C)])
         an2[...]=an1[...]*1.4426950408889634
+    R=proj_ref.shape[0]-2*S
+    split_columns(proj_ref,R,b_ref)
+    split_columns(proj_ref,R+S,c_ref)
     dtp=dtp_ref[...].astype(F32)
     delta=jax.nn.softplus(dtp)
     u=u_ref[...].astype(F32)
-    dec[...]=jnp.where(keep_ref[...]>0,delta,HUGE)
+    dec[...]=jnp.where(masks_ref[:,1:2]>0,delta,HUGE)
     dly[...]=delta
     inj[...]=delta*u
     z=z_ref[...].astype(F32)
@@ -99,7 +124,7 @@
     dy=dg*(z*sg)
     dys[...]=dy
     dz_ref[...]=(dg*y_ref[...]*(sg*(1.0+z*(1.0-sg)))).astype(BF)
-    dskip_ref[...]+=jnp.sum(dy*u,axis=0,keepdims=True)
+    extra_ref[S:S+1]+=jnp.sum(dy*u,axis=0,keepdims=True)
     def chunk(i,running):
         k=T//STEPS-1-i
         b=b_ref[k]; c=c_ref[k]
@@ -133,26 +158,26 @@
     dm_ref[0,1:2]=sum_lanes(pc)
     dd=wa[...]+u*sq[...]
     ddtp_ref[...]=(dd*jax.nn.sigmoid(dtp)).astype(BF)
-    dus_ref[...]=delta*sq[...]+dy*skip_ref[...]
+    dus_ref[...]=delta*sq[...]+dy*skip_ref[:,own_lanes(C)]
     @pl.when(last)
     def _():
-        dalog_ref[...]=acc[...]*an1[...]
-
-def scan_backward(dtp,u,b,c,keep,alog,skip,z,y,dg,heads,T=128):
+        extra_ref[:S]=acc[...]*an1[...]
+
+def scan_backward(dtp,u,proj,masks,alog,skip,z,y,dg,heads,T=128):
     N,C=u.shape
     S=alog.shape[0]
     nk=N//STEPS; tk=T//STEPS; nb=N//T
     row=pl.BlockSpec((T,C),lambda i:(nb-1-i,0))
-    col=pl.BlockSpec((tk,S,STEPS),lambda i:(nb-1-i,0,0))
     whole=lambda s: pl.BlockSpec(s,lambda i:(0,0))
     sc=lambda *s: pltpu.VMEM(s,F32)
     return pl.pallas_call(scan_backward_kernel,grid=(nb,),
-      in_specs=[row,row,col,col,pl.BlockSpec((T,1),lambda i:(nb-1-i,0)),whole((S,C)),whole((1,C)),row,row,row,pl.BlockSpec((tk,S,C),lambda i:(nb-1-i,0,0))],
-      out_specs=[row,row,row,pl.BlockSpec((1,2,T*S),lambda i:(nb-1-i,0,0)),whole((S,C)),whole((1,C))],
-      out_shape=[jax.ShapeDtypeStruct((N,C),BF),jax.ShapeDtypeStruct((N,C),F32),jax.ShapeDtypeStruct((N,C),BF),jax.ShapeDtypeStruct((nb,2,T*S),F32),jax.ShapeDtypeStruct((S,C),F32),jax.ShapeDtypeStruct((1,C),F32)],
-      scratch_shapes=[sc(S,C),sc(T,C),sc(T,C),sc(T,C),sc(T,C),sc(T,C),sc(T,C),sc(STEPS,S,C),sc(STEPS,S,C),sc(S,C),sc(S,C),sc(S,C),sc(T,S,128),sc(T,S,128)],
+      in_specs=[row,row,pl.BlockSpec((proj.shape[0],T),lambda i:(0,nb-1-i)),pl.BlockSpec((T,masks.shape[1]),lambda i:(nb-1-i,0)),whole(alog.shape),whole(skip.shape),row,row,row,pl.BlockSpec((tk,S,C),lambda i:(nb-1-i,0,0))],
+      out_specs=[row,row,row,pl.BlockSpec((1,2,T*S),lambda i:(nb-1-i,0,0)),whole((S+1,C))],
+      out_shape=[jax.ShapeDtypeStruct((N,C),BF),jax.ShapeDtypeStruct((N,C),F32),jax.ShapeDtypeStruct((N,C),BF),jax.ShapeDtypeStruct((nb,2,T*S),F32),jax.ShapeDtypeStruct((S+1,C),F32)],
+      scratch_shapes=[sc(S,C),sc(T,C),sc(T,C),sc(T,C),sc(T,C),sc(T,C),sc(T,C),sc(STEPS,S,C),sc(STEPS,S,C),sc(S,C),sc(S,C),sc(S,C),sc(T,S,128),sc(T,S,128),sc(tk,S,STEPS),sc(tk,S,STEPS)],
       compiler_params=pltpu.CompilerParams(vmem_limit_bytes=48<<20),
-      name="scan_backward")(dtp,u,b,c,keep,alog,skip,z,y,dg,heads)
+      cost_estimate=pl.CostEstimate(flops=6000*N*C*S,bytes_accessed=24<<20,transcendentals=N*C*S),
+      name="scan_backward")(dtp,u,proj,masks,alog,skip,z,y,dg,heads)
 
 
 CUTS = 2
@@ -309,16 +334,25 @@
 
 
 def front_kernel(dp, wide, rank_rows, *refs):
-    win_ref, wout_ref, small_ref, normed_ref, back_ref, tag_ref, masks_ref, taps_ref, bias_ref, refs = *refs[:9], refs[9:]
-    wall_out, wout_out, wsmall_out, nall_out, ball_out, tags_out, xs_out, z_out, u_ref, proj_ref, refs = *refs[:10], refs[10:]
-    stage, stage_out, wout_low, wall, wsmall, nall, tags, mixed, xz, part, part_low, got, whole, refs = *refs[:13], refs[13:]
+    win_ref, wout_ref, small_ref, x_ref, cot_ref, gain_ref, tag_ref, masks_ref, taps_ref, bias_ref, refs = (
+        *refs[:10],
+        refs[10:],
+    )
+    wall_out, wout_out, nall_out, ball_out, tags_out, wx_ref, wdt_ref, xs_out, z_out, u_ref, proj_ref, refs = (
+        *refs[:11],
+        refs[11:],
+    )
+    stage, stage_out, wout_low, wall, wsmall, nall, back_ref, tags, mixed, xz, part, part_low, got, whole, tall, refs = (
+        *refs[:15],
+        refs[15:],
+    )
     x_send, x_recv, core_send, core_recv, on_send, on_recv, refs = *refs[:6], refs[6:]
     h_send, h_recv, h_local, load, keep = refs[:5]
     s1, r1, s2, r2 = refs[5:9]
     me, place = lax.axis_index("dp"), lax.axis_index("wide")
     cuts, span, narrow = mixed.shape
     half = wide // 2
-    count = normed_ref.shape[0]
+    count = x_ref.shape[0]
     rows = win_ref.shape[1]
     lines = dp // 2
     line, core = me // 2, me % 2
@@ -367,8 +401,11 @@
     loads.append(pltpu.make_async_copy(wout_ref, stage_out, load.at[cuts]))
     loads[-1].start()
 
-    nall[place] = normed_ref[...]
+    x = x_ref[...]
+    scale = lax.rsqrt(jnp.mean(x * x, axis=1, keepdims=True) + EPSILON)
+    nall[place] = (x * scale * gain_ref[...]).astype(BF)
     tags[place] = tag_ref[...]
+    back_ref[...] = jnp.where(tag_ref[:, :1].astype(F32) < 3.0, cot_ref[...], 0.0).astype(BF)
     kept = [pltpu.make_async_copy(back_ref, ball_out.at[place], keep.at[0])]
     kept[-1].start()
     spread = Spread(
@@ -497,12 +534,14 @@
         def _():
             pltpu.make_async_copy(mixed.at[q], xz.at[kind, i], h_local.at[q]).wait()
 
-    taps_all = taps_ref[...]
+    channels = u_ref.shape[1]
+    own = pl.ds(pl.multiple_of(place * channels, channels), channels)
+    taps_all, bias_all = taps_ref[:, own], bias_ref[:, own]
     width = taps_all.shape[0]
     for i in range(cuts // 2):
         arrive(0, i)
         taps = taps_all[:, i * narrow : (i + 1) * narrow]
-        bias = bias_ref[:, i * narrow : (i + 1) * narrow]
+        bias = bias_all[:, i * narrow : (i + 1) * narrow]
 
         def conv(t, carry, i=i, taps=taps, bias=bias):
             at = pl.multiple_of(t * 128, 128)
@@ -548,8 +587,15 @@
     for hop in range(cuts - 1, 3):
         spread.step(3, hop)
     spread.end(3)
-    kept.append(pltpu.make_async_copy(wsmall, wsmall_out, keep.at[len(kept)]))
-    kept[-1].start()
+    step_rows = wdt_ref.shape[1] // dp
+    rank = rank_rows * dp
+    for kind in range(3):
+        for owner in range(dp):
+            rows_here = wsmall[owner, kind].astype(F32)
+            tall[owner * rank_rows : (owner + 1) * rank_rows] = rows_here[:rank_rows]
+            tall[rank + owner * step_rows : rank + (owner + 1) * step_rows] = rows_here[rank_rows : rank_rows + step_rows]
+        wx_ref[kind] = tall[:rank].astype(BF)
+        wdt_ref[kind] = tall[rank:].astype(BF)
     for i in range(cuts // 2):
         arrive(1, i)
     for i in range(cuts // 2):
@@ -575,12 +621,12 @@
         copy.wait()
 
 
-def front(win, wout, small, normed, back, tag, masks, taps, bias, rank_rows, collective_id):
+def front(win, wout, small, x, cotangent, gain, tag, masks, taps, bias, rank_rows, step_rows, collective_id):
     dp, wide = lax.axis_size("dp"), lax.axis_size("wide")
     kinds, rows, columns = win.shape
     cuts = 4 if columns >= 512 else 2
     narrow = columns // cuts
-    count, depth = normed.shape
+    count, depth = x.shape
     span = count * wide
     channels = small.shape[2]
     rank = rank_rows * dp
@@ -598,17 +644,18 @@
         out_shape=[
             shape((dp, 3, rows, columns), BF),
             shape((dp,) + wout.shape, BF),
-            shape((dp,) + small.shape, BF),
             shape((wide, count, depth), BF),
             shape((wide, count, depth), BF),
             shape((wide,) + tag.shape, BF),
+            shape((3, rank, channels), BF),
+            shape((3, step_rows * dp, channels), BF),
             shape((span, channels), BF),
             shape((span, channels), BF),
             shape((span, channels), BF),
             shape((rank, span), BF),
         ],
-        in_specs=[anywhere] * 2 + [vmem] * 7,
-        out_specs=[anywhere] * 6 + [vmem] * 4,
+        in_specs=[anywhere] * 2 + [vmem] * 8,
+        out_specs=[anywhere] * 5 + [vmem] * 6,
         scratch_shapes=[
             pltpu.VMEM(win.shape, F32),
             pltpu.VMEM(wout.shape, F32),
@@ -616,6 +663,7 @@
             pltpu.VMEM((dp, 3, rows, columns), BF),
             pltpu.VMEM((dp,) + small.shape, BF),
             pltpu.VMEM((wide, count, depth), BF),
+            pltpu.VMEM((count, depth), BF),
             pltpu.VMEM((wide,) + tag.shape, BF),
             pltpu.VMEM((cuts, span, narrow), BF),
             pltpu.VMEM((2, cuts // 2, span, narrow), BF),
@@ -623,6 +671,7 @@
             pltpu.VMEM((rank, span), BF),
             pltpu.VMEM((wide, rank, count), BF),
             pltpu.VMEM((rank, count), BF),
+            pltpu.VMEM((rank + step_rows * dp, channels), F32),
             far, far, near, near, far, far,
             dma((cuts,)), dma((2, cuts // 2)), dma((cuts,)), dma((cuts + 1,)), dma((6,)),
             dma((wide,)), dma((wide,)), dma((wide,)), dma((wide,)),
@@ -632,7 +681,7 @@
             collective_id=collective_id, has_side_effects=True, vmem_limit_bytes=60 << 20
         ),
         name="front",
-    )(win, wout, small, normed, back, tag, masks, taps, bias)
+    )(win, wout, small, x, cotangent, gain, tag, masks, taps, bias)
 
 
 def sum_wide_kernel(wide, x_ref, out_ref, got, whole, s1, r1, s2, r2):
@@ -844,24 +893,499 @@
     )(part, table, small)
 
 
-def gate_kernel(back_ref, gated_ref, tag_ref, w_ref, branch_ref, dgated_ref, grad_ref, chosen):
+def back_kernel(dp, wide, rank_rows, step_rows, *refs):
+    feat_refs, kind_refs, refs = refs[:dp], refs[dp : 2 * dp], refs[2 * dp :]
+    win_ref, normed_ref, ddtp_ref, dscan_ref, dz_ref, xs_ref, u_ref, refs = *refs[:7], refs[7:]
+    dmaps_ref, rates_ref, wx_ref, wdt_ref, tags_ref, line_ref, masks_ref, taps_ref, bias_ref, extra_ref, refs = (
+        *refs[:10],
+        refs[10:],
+    )
+    ingrad_ref, rows_ref, tables_ref, sums_ref, refs = *refs[:4], refs[4:]
+    wall, feats, nbuf, part, got, whole, dproj, dpre, leave, gm, dn, refs = *refs[:11], refs[11:]
+    first, flow_a, flow_b, stage, table, got_tables, dt_grad, small, got_small, refs = *refs[:9], refs[9:]
+    s1, r1, s2, r2, load, nload, d_send, d_recv, d_local, refs = *refs[:9], refs[9:]
+    x_send, x_recv, core_send, core_recv, on_send, on_recv, o_send, refs = *refs[:7], refs[7:]
+    a_send, a_recv, b_send, b_recv, t_send, t_recv, l_send, l_recv, w_send, w_recv = refs
+    me, place = lax.axis_index("dp"), lax.axis_index("wide")
+    _, cuts, span, narrow = gm.shape
+    channels = xs_ref.shape[1]
+    rows = win_ref.shape[2]
+    count, depth = rows_ref.shape
+    half = wide // 2
+    quarters = cuts // 2
+    low, home = place // half, place % half
+    lines = dp // 2
+    line, core = me // 2, me % 2
+    partner = (me + 1 - 2 * core, place)
+    across = [(lax.rem(line + k, lines) * 2 + core, place) for k in range(1, lines)]
+    mates = [lax.rem(me + k, dp) for k in range(1, dp)]
+    peers = [lax.rem(place + k, wide) for k in range(1, wide)]
+    position = ring_position(place, wide)
+    after = (me, ring_index(lax.rem(position + 1, wide), wide))
+    before = (me, ring_index(lax.rem(position + wide - 1, wide), wide))
+    barrier = pltpu.get_barrier_semaphore()
+    for peer in [(mate, place) for mate in mates] + [(me, peer) for peer in peers]:
+        pl.semaphore_signal(barrier, inc=1, device_id=peer, device_id_type=MESH)
+    pl.semaphore_wait(barrier, dp + wide - 2)
+
+    loads = [pltpu.make_async_copy(win_ref, wall, load.at[dp])]
+    for k in range(dp):
+        loads.append(pltpu.make_async_copy(feat_refs[k], feats.at[k], load.at[k]))
+    for copy in loads:
+        copy.start()
+
+    def slot(i):
+        return place % 2 * quarters + i
+
+    def source(kind, i):
+        if kind == 0:
+            return leave.at[i]
+        return dz_ref.at[:, pl.ds(i * narrow, narrow)]
+
+    def deliver(kind, i):
+        target = (me, kind * half + place // 2)
+        return remote(source(kind, i), gm.at[me, slot(i)], d_send.at[kind, i], d_recv.at[slot(i)], target)
+
+    def stay(kind, i):
+        return pltpu.make_async_copy(source(kind, i), gm.at[me, slot(i)], d_local.at[i])
+
+    def hand_over(kind, i):
+        @pl.when(kind * half + place // 2 != place)
+        def _():
+            deliver(kind, i).start()
+
+        @pl.when(kind * half + place // 2 == place)
+        def _():
+            stay(kind, i).start()
+
+    def arrive(q):
+        sender = 2 * home + q // quarters
+
+        @pl.when(sender != place)
+        def _():
+            remote(leave.at[0], gm.at[me, q], d_send.at[0, 0], d_recv.at[q], partner).wait_recv()
+
+        @pl.when(sender == place)
+        def _():
+            pltpu.make_async_copy(leave.at[0], gm.at[me, q], d_local.at[q % quarters]).wait()
+
+    blocks = TILE // count
+    steps = wdt_ref.shape[1]
+
+    def columns(index):
+        return pl.ds(pl.multiple_of(index * count, count), count)
+
+    def give(k):
+        device = (me, peers[k - 1])
+        return remote(part.at[:, columns(peers[k - 1])], got.at[k], s1.at[k], r1.at[k], device)
+
+    def share(k):
+        device = (me, peers[k - 1])
+        return remote(whole, dproj.at[:, columns(place)], s2.at[k], r2.at[k], device)
+
+    def rates_back(t, carry):
+        at = pl.ds(pl.multiple_of(t * TILE, TILE), TILE)
+        tag = tags_ref[pl.ds(t * blocks, blocks)].reshape(TILE, -1)[:, :1].astype(F32)
+        value = ddtp_ref[at].astype(F32)
+        total = jnp.zeros((steps, TILE), F32)
+        for kind in range(3):
+            total += lax.dot_general(
+                wdt_ref[kind],
+                jnp.where(tag == kind, value, 0.0).astype(BF),
+                (((1,), (1,)), ((), ())),
+                preferred_element_type=F32,
+            )
+        part[:steps, at] = total.astype(BF)
+        return carry
+
+    lax.fori_loop(0, span // TILE, rates_back, 0)
+    part[steps:] = dmaps_ref[...].astype(BF)
+    order = sorted(range(1, wide), key=lambda k: -min(k, wide - k))
+    for k in order:
+        give(k).start()
+    dn[...] = jnp.zeros_like(dn)
+    dpre[span:] = jnp.zeros_like(dpre[span:])
+    width = taps_ref.shape[0]
+    states = extra_ref.shape[0] - 1
+    table[...] = jnp.zeros_like(table)
+    table[width + 1 : width + 2 + states] = extra_ref[...]
+    dead = line_ref[0:1].astype(F32)
+    for kind in range(3):
+        chosen_rates = jnp.where(dead == kind, rates_ref[:steps].astype(F32), 0.0).astype(BF)
+        grad = jnp.dot(chosen_rates, ddtp_ref[...], preferred_element_type=F32)
+        dt_grad[kind] = grad
+        picked = jnp.where(line_ref[...].astype(F32) == kind, 1.0, 0.0).astype(BF)
+        at = width + 2 + states + kind
+        table[at : at + 1] = jnp.dot(picked, ddtp_ref[...], preferred_element_type=F32)[:1]
+    total = part[:, columns(place)].astype(F32)
+    for k in reversed(order):
+        give(k).wait_recv()
+        total = total + got[k].astype(F32)
+    whole[...] = total.astype(BF)
+    for k in order:
+        share(k).start()
+    dproj[:, columns(place)] = whole[...]
+    for k in range(1, wide):
+        share(k).wait_recv()
+    for i in range(quarters):
+        hand_over(1, i)
+
+    own = pl.ds(pl.multiple_of(place * channels, channels), channels)
+    taps_all, conv_bias = taps_ref[:, own], bias_ref[:, own]
+
+    def through(t, carry):
+        at = pl.multiple_of(t * 128, 128)
+        behind = pl.multiple_of(jnp.maximum(t * 128 - 16, 0), 16)
+        tag = tags_ref[pl.ds(t * 128 // count, 128 // count)].reshape(128, -1)[:, :1].astype(F32)
+        piece = dproj[:, pl.ds(at, 128)]
+        du = jnp.zeros((128, channels), F32)
+        for kind in range(3):
+            product = lax.dot_general(
+                piece, wx_ref[kind], (((0,), (0,)), ((), ())), preferred_element_type=F32
+            )
+            du = du + jnp.where(tag == kind, product, 0.0)
+        du = du.astype(BF).astype(F32) + dscan_ref[pl.ds(at, 128)]
+        here = xs_ref[pl.ds(at, 128)].astype(F32)
+        both = jnp.concatenate([xs_ref[pl.ds(behind, 16)].astype(F32), here], axis=0)
+        masks = masks_ref[pl.ds(at, 128)]
+        terms = [here] + [both[16 - k : 144 - k] * masks[:, k : k + 1] for k in range(1, width)]
+        pre = conv_bias
+        for k in range(width):
+            pre = pre + taps_all[width - 1 - k : width - k] * terms[k]
+        sigma = jax.nn.sigmoid(pre)
+        slope = du * (sigma * (1.0 + pre * (1.0 - sigma)))
+        dpre[pl.ds(at, 128)] = slope
+        for k in range(width):
+            table[width - 1 - k : width - k] += jnp.sum(slope * terms[k], axis=0, keepdims=True)
+        table[width : width + 1] += jnp.sum(slope, axis=0, keepdims=True)
+        return carry
+
+    lax.fori_loop(0, span // 128, through, 0)
+
+    for i in range(quarters):
+        lanes = slice(i * narrow, (i + 1) * narrow)
+
+        def conv_back(t, carry, i=i, lanes=lanes):
+            at = pl.multiple_of(t * 128, 128)
+            ahead = pl.multiple_of(t * 128 + 128, 16)
+            known = pl.multiple_of(jnp.minimum(t * 128 + 128, span - 16), 16)
+            here = dpre[pl.ds(at, 128), lanes]
+            both = jnp.concatenate([here, dpre[pl.ds(ahead, 16), lanes]], axis=0)
+            masks = jnp.concatenate([masks_ref[pl.ds(at, 128)], masks_ref[pl.ds(known, 16)]], axis=0)
+            back = taps_all[width - 1 : width, lanes] * here
+            for k in range(1, width):
+                masked = both * masks[:, k : k + 1]
+                back = back + taps_all[width - 1 - k : width - k, lanes] * masked[k : 128 + k]
+            leave[i, pl.ds(at, 128)] = back.astype(BF)
+            return carry
+
+        lax.fori_loop(0, span // 128, conv_back, 0)
+        hand_over(0, i)
+
+    for kind in range(3):
+        chosen_proj = jnp.where(dead == kind, dproj[...].astype(F32), 0.0).astype(BF)
+        grad = jnp.dot(chosen_proj, u_ref[...], preferred_element_type=F32)
+        filler = jnp.zeros((small.shape[2] - rank_rows - step_rows, channels), F32)
+        for owner in range(dp):
+            ranks = grad[owner * rank_rows : (owner + 1) * rank_rows]
+            sizes = dt_grad[kind, owner * step_rows : (owner + 1) * step_rows]
+            small[owner, kind] = jnp.concatenate([ranks, sizes, filler], axis=0).astype(BF)
+
+    def lend_table(k):
+        return remote(table, got_tables.at[k], t_send.at[k], t_recv.at[k], (mates[k], place))
+
+    def lend_small(k):
+        return remote(small.at[mates[k]], got_small.at[k], l_send.at[k], l_recv.at[k], (mates[k], place))
+
+    for k in range(dp - 1):
+        lend_small(k).start()
+
+    def cross(k, q):
+        return remote(gm.at[me, q], gm.at[me, q], x_send.at[k, q], x_recv.at[k, q], across[k])
+
+    def pair(q):
+        return remote(gm.at[me, q], gm.at[me, q], core_send.at[q], core_recv.at[q], partner)
+
+    def onward(k, q):
+        owner = lax.rem(line + lines - 1 - k, lines) * 2 + core
+        return remote(gm.at[owner, q], gm.at[owner, q], on_send.at[k, q], on_recv.at[k, q], partner)
+
+    def pass_on(q):
+        for k in range(lines - 1):
+            cross(k, q).wait_recv()
+            onward(k, q).start()
+
+    owners = [me, me + 1 - 2 * core]
+    for k in range(1, lines):
+        far = lax.rem(line + k, lines) * 2
+        owners += [far + core, far + 1 - core]
+
+    outs = []
+
+    def master_grad(number, q):
+        pair(q).wait_recv()
+        for k in range(lines - 1):
+            onward(k, q).wait_recv()
+        if len(outs) >= 2:
+            outs[number - 2].wait()
+
+        def one_kind(kind, carry):
+            total = jnp.zeros((rows, narrow), F32)
+            for k, owner in enumerate(owners):
+                tag = kind_refs[k][...].astype(F32)
+                right = jnp.where(tag == kind.astype(F32), gm[owner, q].astype(F32), 0.0).astype(BF)
+                total += lax.dot_general(feats[k], right, (((0,), (0,)), ((), ())), preferred_element_type=F32)
+            stage[number % 2, kind] = total
+            return carry
+
+        lax.fori_loop(0, 3, one_kind, 0)
+        out = pltpu.make_async_copy(
+            stage.at[number % 2], ingrad_ref.at[:, :, pl.ds(q * narrow, narrow)], o_send.at[number % 2]
+        )
+        out.start()
+        outs.append(out)
+
+    turns = [h * quarters + i for i in range(quarters) for h in range(2)]
+    for copy in loads:
+        copy.wait()
+    for number, q in enumerate(turns):
+        arrive(q)
+        for k in range(lines - 1):
+            cross(k, q).start()
+        pair(q).start()
+
+        def pick(t, carry, q=q):
+            at = pl.ds(pl.multiple_of(t * TILE, TILE), TILE)
+            tag = tags_ref[pl.ds(t * blocks, blocks)].reshape(TILE, -1)[:, :1].astype(F32)
+            value = gm[me, q, at].astype(F32)
+            left = [jnp.where(tag == kind, value, 0.0).astype(BF) for kind in range(3)]
+            for owner in range(dp):
+                total = dn[at, owner * rows : (owner + 1) * rows]
+                for kind in range(3):
+                    total += lax.dot_general(
+                        left[kind],
+                        wall[owner, kind, :, q * narrow : (q + 1) * narrow],
+                        (((1,), (1,)), ((), ())),
+                        preferred_element_type=F32,
+                    )
+                dn[at, owner * rows : (owner + 1) * rows] = total
+            return carry
+
+        lax.fori_loop(0, span // TILE, pick, 0)
+        if 0 < number < cuts - 1:
+            pass_on(turns[number - 1])
+        if 1 < number < cuts - 1:
+            master_grad(number - 2, turns[number - 2])
+
+    half_columns = depth // 2
+    cut = half_columns // CUTS
+
+    def lanes_of(side, i):
+        return slice(side * half_columns + i * cut, side * half_columns + (i + 1) * cut)
+
+    def block(side, hop):
+        step = position + wide - 1 - hop if side == 0 else position + 1 + hop
+        owner = ring_index(lax.rem(step, wide), wide)
+        return pl.ds(pl.multiple_of(owner * count, count), count)
+
+    flows = ((flow_a, a_send, a_recv, after), (flow_b, b_send, b_recv, before))
+
+    def turn(side, hop, i):
+        flow, send, recv, device = flows[side]
+        origin = first.at[side, i] if hop == 0 else flow.at[hop - 1, i]
+        return remote(origin, flow.at[hop, i], send.at[hop, i], recv.at[hop, i], device)
+
+    for i in range(CUTS):
+        for side in range(2):
+            first[side, i] = dn[block(side, 0), lanes_of(side, i)].astype(BF)
+            turn(side, 0, i).start()
+
+    def normed_copy(b):
+        return pltpu.make_async_copy(normed_ref.at[b], nbuf.at[b % 2], nload.at[b % 2])
+
+    normed_copy(0).start()
+    pass_on(turns[cuts - 2])
+    gain = jnp.zeros((1, depth), F32)
+    for b in range(wide):
+        if b + 1 < wide:
+            normed_copy(b + 1).start()
+        normed_copy(b).wait()
+        gain = gain + jnp.sum(
+            dn[b * count : (b + 1) * count] * nbuf[b % 2].astype(F32), axis=0, keepdims=True
+        )
+    for k in range(depth // channels):
+        at = width + 5 + states + k
+        table[at : at + 1] = gain[:, k * channels : (k + 1) * channels]
+    for k in range(dp - 1):
+        lend_table(k).start()
+
+    def show(k):
+        return remote(tables_ref.at[place], tables_ref.at[place], w_send.at[k], w_recv.at[k], (me, peers[k]))
+
+    for hop in range(1, wide):
+        for i in range(CUTS):
+            for side in range(2):
+                turn(side, hop - 1, i).wait_recv()
+                flow = flows[side][0]
+                total = flow[hop - 1, i].astype(F32) + dn[block(side, hop), lanes_of(side, i)]
+                if hop < wide - 1:
+                    flow[hop - 1, i] = total.astype(BF)
+                    turn(side, hop, i).start()
+                else:
+                    rows_ref[:, lanes_of(side, i)] = total
+        if hop == 1:
+            master_grad(cuts - 3, turns[cuts - 3])
+            pass_on(turns[cuts - 1])
+        if hop == 2:
+            total = table[...]
+            for k in range(dp - 1):
+                lend_table(k).wait_recv()
+                total = total + got_tables[k]
+            tables_ref[place] = total
+            for k in range(wide - 1):
+                show(k).start()
+        if hop == 3:
+            master_grad(cuts - 2, turns[cuts - 2])
+        if hop == 5:
+            master_grad(cuts - 1, turns[cuts - 1])
+        if hop == 4:
+            for kind in range(3):
+                sums_ref[kind] = small[me, kind].astype(F32)
+            for k in range(dp - 1):
+                lend_small(k).wait_recv()
+                for kind in range(3):
+                    sums_ref[kind] += got_small[k, kind].astype(F32)
+
+    for k in range(dp - 1):
+        lend_table(k).wait_send()
+        lend_small(k).wait_send()
+    for k in range(wide - 1):
+        show(k).wait()
+    for k in range(1, wide):
+        share(k).wait_send()
+        give(k).wait_send()
+    for hop in range(wide - 1):
+        for i in range(CUTS):
+            for side in range(2):
+                turn(side, hop, i).wait_send()
+    for q in range(cuts):
+        pair(q).wait_send()
+        for k in range(lines - 1):
+            cross(k, q).wait_send()
+            onward(k, q).wait_send()
+    for kind in range(2):
+        for i in range(quarters):
+
+            @pl.when(kind * half + place // 2 != place)
+            def _(kind=kind, i=i):
+                deliver(kind, i).wait_send()
+
+    for out in outs[-2:]:
+        out.wait()
+
+
+def back(win, feats, normed, kinds, vmem_args, rank_rows, step_rows, collective_id):
+    dp, wide = lax.axis_size("dp"), lax.axis_size("wide")
+    _, _, rows, columns = win.shape
+    _, count, depth = normed.shape
+    cuts = 4
+    narrow = columns // cuts
+    quarters = cuts // 2
+    span, channels = vmem_args[0].shape
+    rank, steps = vmem_args[6].shape[0], vmem_args[8].shape[1]
+    extra, width = vmem_args[14], vmem_args[12].shape[0]
+    lines = dp // 2
+    table_rows = width + 4 + extra.shape[0] + depth // channels
+    table_rows += -table_rows % 8
+    small_rows = rank_rows + step_rows
+    small_rows += -small_rows % 16
+    vmem = pl.BlockSpec(memory_space=pltpu.VMEM)
+    anywhere = pl.BlockSpec(memory_space=pl.ANY)
+    dma = pltpu.SemaphoreType.DMA
+    shape = jax.ShapeDtypeStruct
+    flow = pltpu.VMEM((wide - 1, CUTS, count, depth // 2 // CUTS), BF)
+    hops, far, near = dma((wide - 1, CUTS)), dma((lines - 1, cuts)), dma((cuts,))
+    mates, peers = dma((dp - 1,)), dma((wide,))
+    return pl.pallas_call(
+        functools.partial(back_kernel, dp, wide, rank_rows, step_rows),
+        out_shape=[
+            shape((3, rows, columns), F32),
+            shape((count, depth), F32),
+            shape((wide, table_rows, channels), F32),
+            shape((3, small_rows, channels), F32),
+        ],
+        in_specs=[anywhere] * dp + [vmem] * dp + [anywhere] * 2 + [vmem] * len(vmem_args),
+        out_specs=[anywhere] + [vmem] * 3,
+        scratch_shapes=[
+            pltpu.VMEM(win.shape, BF),
+            pltpu.VMEM((dp,) + feats[0].shape, BF),
+            pltpu.VMEM((2, count, depth), BF),
+            pltpu.VMEM((rank, span), BF),
+            pltpu.VMEM((wide, rank, count), BF),
+            pltpu.VMEM((rank, count), BF),
+            pltpu.VMEM((rank, span), BF),
+            pltpu.VMEM((span + 16, channels), F32),
+            pltpu.VMEM((quarters, span, narrow), BF),
+            pltpu.VMEM((dp, cuts, span, narrow), BF),
+            pltpu.VMEM((span, depth), F32),
+            pltpu.VMEM((2, CUTS, count, depth // 2 // CUTS), BF),
+            flow,
+            flow,
+            pltpu.VMEM((2, 3, rows, narrow), F32),
+            pltpu.VMEM((table_rows, channels), F32),
+            pltpu.VMEM((dp - 1, table_rows, channels), F32),
+            pltpu.VMEM((3, steps, channels), F32),
+            pltpu.VMEM((dp, 3, small_rows, channels), BF),
+            pltpu.VMEM((dp - 1, 3, small_rows, channels), BF),
+            peers, peers, peers, peers, dma((dp + 1,)), dma((2,)), dma((2, quarters)), near, dma((quarters,)),
+            far, far, near, near, far, far, dma((2,)),
+            hops, hops, hops, hops, mates, mates, mates, mates, peers, peers,
+        ],
+        compiler_params=pltpu.CompilerParams(
+            collective_id=collective_id, has_side_effects=True, vmem_limit_bytes=62 << 20
+        ),
+        name="back",
+    )(*feats, *kinds, win, normed, *vmem_args)
+
+
+def branch_kernel(gated_ref, tag_ref, w_ref, branch_ref):
+    dp, kinds, rows, channels = w_ref.shape
+    tag = tag_ref[...][:, :1].astype(F32)
+    gated = gated_ref[...].astype(F32)
+    chosen = [jnp.where(tag == kind, gated, 0.0).astype(BF) for kind in range(3)]
+    for owner in range(dp):
+        branch = jnp.zeros((gated.shape[0], rows), F32)
+        for kind in range(3):
+            branch += lax.dot_general(
+                chosen[kind], w_ref[owner, kind], (((1,), (1,)), ((), ())), preferred_element_type=F32
+            )
+        branch_ref[:, owner * rows : (owner + 1) * rows] = branch.astype(BF)
+
+
+def branch_of(gated, tags, w_out, depth):
+    span, channels = gated.shape
+    tile = lambda lanes: pl.BlockSpec((TILE, lanes), lambda t: (t, 0))
+    return pl.pallas_call(
+        branch_kernel,
+        grid=(span // TILE,),
+        out_shape=jax.ShapeDtypeStruct((span, depth), BF),
+        in_specs=[tile(channels), tile(tags.shape[1]), pl.BlockSpec(memory_space=pltpu.VMEM)],
+        out_specs=tile(depth),
+        compiler_params=pltpu.CompilerParams(vmem_limit_bytes=40 << 20),
+        cost_estimate=pl.CostEstimate(
+            flops=6 * span * channels * depth, bytes_accessed=12 << 20, transcendentals=0
+        ),
+        name="branch",
+    )(gated, tags, w_out)
+
+
+def gate_kernel(back_ref, gated_ref, tag_ref, w_ref, dgated_ref, grad_ref):
     dp, kinds, rows, channels = w_ref.shape
     span = gated_ref.shape[0]
-    blocks = TILE // tag_ref.shape[1]
 
     def tile(t, carry):
         at = pl.ds(pl.multiple_of(t * TILE, TILE), TILE)
-        tag = tag_ref[pl.ds(t * blocks, blocks)].reshape(TILE, -1)[:, :1].astype(F32)
-        gated = gated_ref[at].astype(F32)
-        for kind in range(3):
-            chosen[kind, at] = jnp.where(tag == kind, gated, 0.0).astype(BF)
-        for owner in range(dp):
-            branch = jnp.zeros((TILE, rows), F32)
-            for kind in range(3):
-                branch += lax.dot_general(
-                    chosen[kind, at], w_ref[owner, kind], (((1,), (1,)), ((), ())), preferred_element_type=F32
-                )
-            branch_ref[at, owner * rows : (owner + 1) * rows] = branch.astype(BF)
+        tag = tag_ref[at][:, :1].astype(F32)
         total = jnp.zeros((TILE, channels), F32)
         for kind in range(3):
             product = jnp.zeros((TILE, channels), F32)
@@ -878,8 +1402,10 @@
     def grad(owner, carry):
         columns = pl.ds(pl.multiple_of(owner * rows, rows), rows)
         for kind in range(3):
+            tag = tag_ref[...][:, :1].astype(F32)
+            chosen = jnp.where(tag == kind, gated_ref[...].astype(F32), 0.0).astype(BF)
             grad_ref[owner, kind] = lax.dot_general(
-                back_ref[:, columns], chosen[kind], (((0,), (0,)), ((), ())), preferred_element_type=F32
+                back_ref[:, columns], chosen, (((0,), (0,)), ((), ())), preferred_element_type=F32
             ).astype(BF)
         return carry
 
@@ -888,21 +1414,19 @@
 
 def gate(back, gated, tags, w_out):
     span, channels = gated.shape
-    dp, kinds, rows, _ = w_out.shape
     vmem = pl.BlockSpec(memory_space=pltpu.VMEM)
-    flops = 6 * 3 * span * channels * back.shape[1]
     return pl.pallas_call(
         gate_kernel,
         out_shape=[
-            jax.ShapeDtypeStruct(back.shape, BF),
             jax.ShapeDtypeStruct(gated.shape, BF),
             jax.ShapeDtypeStruct(w_out.shape, BF),
         ],
         in_specs=[vmem] * 4,
-        out_specs=[vmem] * 3,
-        scratch_shapes=[pltpu.VMEM((3, span, channels), BF)],
+        out_specs=[vmem] * 2,
         compiler_params=pltpu.CompilerParams(vmem_limit_bytes=58 << 20),
-        cost_estimate=pl.CostEstimate(flops=flops, bytes_accessed=24 << 20, transcendentals=0),
+        cost_estimate=pl.CostEstimate(
+            flops=12 * span * channels * back.shape[1], bytes_accessed=20 << 20, transcendentals=0
+        ),
         name="gate",
     )(back, gated, tags, w_out)
 
@@ -1010,140 +1534,161 @@
     width = conv_weight.shape[0]
     own = lambda table: lax.dynamic_slice_in_dim(table, place * channels, channels, table.ndim - 1)
 
-    bounds = jnp.cumsum(lengths.reshape(-1))
+    pieces = lengths.reshape(-1)
+    ends = [pieces[0]]
+    for at in range(1, pieces.shape[0]):
+        ends.append(ends[-1] + pieces[at])
+    bounds = jnp.stack(ends)
     places = jnp.arange(span, dtype=jnp.int32)
     living = places < bounds[-1]
     masks = conv_masks(places, bounds, width)
-    later = conv_masks(jnp.arange(span + width - 1, dtype=jnp.int32), bounds, width)
     alive_here = (place * count + jnp.arange(count, dtype=jnp.int32)) < bounds[-1]
 
     scale = lax.rsqrt(jnp.mean(x_in * x_in, axis=1, keepdims=True) + EPSILON)
-    normed = (x_in * scale * norm_gain[None, :]).astype(BF)
-    d_branch = jnp.where(alive_here[:, None], cotangent, 0.0).astype(BF)
     rank_rows, step_rows = xproj_master.shape[0], dtproj_master.shape[0]
     small = jnp.concatenate([xproj_master, dtproj_master], axis=0)
     small = jnp.pad(small, ((0, -small.shape[0] % 16), (0, 0), (0, 0)))
     tag = jnp.where(alive_here, modality, 3).astype(BF)
-    w_in, w_out, w_small, normed_all, d_branch_all, tags_all, xs, z, inner, proj = front(
+    mask_table = jnp.stack(masks, axis=1)
+    w_in, w_out, normed_all, d_branch_all, tags_all, w_x_kinds, w_dt_kinds, xs, z, inner, proj = front(
         jnp.transpose(in_master, (1, 0, 2)),
         jnp.transpose(out_master, (1, 0, 2)),
         jnp.transpose(small, (1, 0, 2)),
-        normed,
-        d_branch,
+        x_in,
+        cotangent,
+        norm_gain[None, :],
         jnp.broadcast_to(tag[:, None], (count, 128)),
-        jnp.stack(masks, axis=1),
-        own(conv_weight),
-        own(conv_bias)[None, :],
+        mask_table,
+        conv_weight,
+        conv_bias[None, :],
         rank_rows,
+        step_rows,
         0,
     )
     w_in = w_in.reshape(-1, in_master.shape[2])
     normed_all = normed_all.reshape(span, -1)
     kinds_all = tags_all[:, :, 0].reshape(span)
-    w_x_kinds = w_small[:, :, :rank_rows].transpose(1, 0, 2, 3).reshape(3, -1, channels)
-    w_dt_kinds = w_small[:, :, rank_rows : rank_rows + step_rows].transpose(1, 0, 2, 3)
-    w_dt_kinds = w_dt_kinds.reshape(3, DT_RANK, channels)
     kinds = kinds_all[:, None] == jnp.arange(3, dtype=BF)[None, :]
 
     kinds_parts = from_partners(kinds_all[:, None])
     features = swap_features(normed_all)
 
-    taps = own(conv_weight)
-    xs_value = xs.astype(F32)
-    extended = jnp.concatenate([jnp.zeros((width - 1, channels), F32), xs_value], axis=0)
-    pre = own(conv_bias)[None, :]
-    for offset in range(width):
-        begin = width - 1 - offset
-        pre = (
-            pre + taps[begin][None, :] * extended[begin : begin + span] * masks[offset][:, None]
-        )
-
     rank = w_x_kinds.shape[1]
-    across = kinds.T[:, None, :]
-    rates = proj[:DT_RANK].T
-    maps = proj[DT_RANK:].astype(F32)
-    rates_kinds = split_kinds(rates, kinds, 1)
-    bias = jnp.where(kinds[:, :, None], dt_bias.astype(BF).astype(F32)[None], 0.0).sum(axis=1)
-    dtp = (contract(rates_kinds, w_dt_kinds.reshape(3 * DT_RANK, channels), 1, 0) + bias).astype(BF)
-
-    blocks = span // STEPS
-    to_columns = lambda rows: rows.reshape(-1, blocks, STEPS).transpose(1, 0, 2)
-    b_columns = to_columns(maps[:STATE])
-    c_columns = to_columns(maps[STATE:])
-    keep = masks[1][:, None]
-    a_own = own(a_log)
-    skip_own = own(d_skip)[None, :]
-    gated, y_value, heads = scan_forward(dtp, inner, b_columns, c_columns, keep, a_own, skip_own, z)
-
-    branch, d_gated, grad_out = gate(d_branch_all.reshape(span, -1), gated, tags_all, w_out)
+    tags_flat = tags_all.reshape(span, -1)
+    skip_row = d_skip[None, :]
+    dtp, gated, y_value, heads = scan_forward(
+        proj, w_dt_kinds, dt_bias, tags_flat, inner, mask_table, a_log, skip_row, z
+    )
+    branch = branch_of(gated, tags_flat, w_out, x_in.shape[1])
     branch = lax.psum_scatter(branch, "wide", scatter_dimension=0, tiled=True)
     result = x_in + branch.astype(F32)
+    d_gated, grad_out = gate(d_branch_all.reshape(span, -1), gated, tags_flat, w_out)
     out_grad = scatter_master(grad_out).astype(F32)
-
-    d_dtp, d_scan, d_z, d_columns, alog_part, skip_part = scan_backward(
-        dtp, inner, b_columns, c_columns, keep, a_own, skip_own, z, y_value, d_gated, heads
+    d_dtp, d_scan, d_z, d_columns, extra = scan_backward(
+        dtp, inner, proj, mask_table, a_log, skip_row, z, y_value, d_gated, heads
     )
-    d_dtp = jnp.where(living[:, None], d_dtp, jnp.zeros((), BF))
     d_dtp, features, kinds_parts = lax.optimization_barrier((d_dtp, features, kinds_parts))
-    feature_kinds = [
-        split_kinds(rows, tags == jnp.arange(3, dtype=BF)[None, :], 1)
-        for rows, tags in zip(features, kinds_parts)
-    ]
     d_maps = d_columns.reshape(-1, 2, d_columns.shape[2] // STATE, STATE)
     d_maps = d_maps.transpose(1, 3, 0, 2).reshape(2 * STATE, span)
-    by_kind = contract(w_dt_kinds.reshape(3 * DT_RANK, channels), d_dtp, 1, 1)
-    d_rates = jnp.sum(jnp.where(across, by_kind.reshape(3, DT_RANK, span), 0.0), axis=0)
-    d_proj = sum_wide(jnp.concatenate([d_rates, d_maps], axis=0).astype(BF), 2)
-    d_proj = jnp.where(living[None], d_proj, jnp.zeros((), BF)).T
-    grad_dt = contract(rates_kinds, d_dtp, 0, 0).reshape(3, dp, step_rows, channels)
-    bias_part = jnp.stack(
-        [jnp.sum(jnp.where(kinds[:, k : k + 1], d_dtp.astype(F32), 0.0), axis=0) for k in range(3)]
-    )
-    d_proj_kinds = split_kinds(d_proj, kinds, 1)
-    d_inner = contract(d_proj_kinds, w_x_kinds.reshape(3 * rank, channels), 1, 0).astype(BF)
-    grad_x = contract(d_proj_kinds, inner, 0, 0)
-    grad_x = grad_x.reshape(3, dp, rank_rows, channels)
-
-    d_pre = (d_inner.astype(F32) + d_scan) * silu_slope(pre)
-    further = jnp.concatenate([d_pre, jnp.zeros((width - 1, channels), F32)], axis=0)
-    conv_rows = []
-    d_xs = jnp.zeros_like(xs_value)
-    for offset in range(width):
-        begin = width - 1 - offset
-        conv_rows.append(
-            jnp.sum(d_pre * masks[offset][:, None] * extended[begin : begin + span], axis=0)
+    if span * x_in.shape[1] * 4 <= 12 << 20:
+        in_grad, d_normed, tables, small = back(
+            w_in.reshape(dp, 3, -1, w_in.shape[1]),
+            features,
+            normed_all.reshape(wide, count, -1),
+            kinds_parts,
+            (
+                d_dtp,
+                d_scan,
+                d_z,
+                xs,
+                inner,
+                d_maps,
+                proj,
+                w_x_kinds,
+                w_dt_kinds,
+                tags_all,
+                jnp.broadcast_to(kinds_all.astype(F32)[None], (8, span)),
+                mask_table,
+                conv_weight,
+                conv_bias[None, :],
+                extra,
+            ),
+            rank_rows,
+            step_rows,
+            2,
         )
-        masked = further * later[offset][:, None]
-        d_xs = d_xs + taps[begin][None, :] * masked[offset : offset + span]
-    conv_part = jnp.stack(conv_rows[::-1], axis=0)
-    conv_bias_part = jnp.sum(d_pre, axis=0)
-    d_xs = jnp.where(living[:, None], d_xs, 0.0).astype(BF)
-    d_z = jnp.where(living[:, None], d_z, jnp.zeros((), BF))
-    d_mixed = halves_back(d_xs, d_z, wide)
-    mixed_parts = from_partners(d_mixed)
-    grad_in = 0.0
-    for pair in range(0, dp, 2):
-        left = jnp.concatenate(feature_kinds[pair : pair + 2], axis=0)
-        grad_in = grad_in + contract(left, jnp.concatenate(mixed_parts[pair : pair + 2], axis=0), 0, 0)
-    in_grad = jnp.transpose(grad_in.reshape(3, -1, d_mixed.shape[1]), (1, 0, 2))
-
-    d_normed = jnp.zeros((span, x_in.shape[1]), F32)
-    w_in_kinds = w_in.reshape(dp, 3, -1, w_in.shape[1])
-    for kind in range(3):
-        picked = jnp.where(kinds[:, kind : kind + 1], d_mixed, jnp.zeros((), BF))
-        d_normed = d_normed + contract(
-            picked, w_in_kinds[:, kind].reshape(-1, w_in.shape[1]), 1, 1
+        in_grad = jnp.transpose(in_grad, (1, 0, 2))
+    else:
+        taps = own(conv_weight)
+        across = kinds.T[:, None, :]
+        rates_kinds = split_kinds(proj[:DT_RANK].T, kinds, 1)
+        d_dtp = jnp.where(living[:, None], d_dtp, jnp.zeros((), BF))
+        xs_value = xs.astype(F32)
+        extended = jnp.concatenate([jnp.zeros((width - 1, channels), F32), xs_value], axis=0)
+        pre = own(conv_bias)[None, :]
+        for offset in range(width):
+            begin = width - 1 - offset
+            pre = (
+                pre + taps[begin][None, :] * extended[begin : begin + span] * masks[offset][:, None]
+            )
+
+        feature_kinds = [
+            split_kinds(rows, tags == jnp.arange(3, dtype=BF)[None, :], 1)
+            for rows, tags in zip(features, kinds_parts)
+        ]
+        by_kind = contract(w_dt_kinds.reshape(3 * DT_RANK, channels), d_dtp, 1, 1)
+        d_rates = jnp.sum(jnp.where(across, by_kind.reshape(3, DT_RANK, span), 0.0), axis=0)
+        d_proj = sum_wide(jnp.concatenate([d_rates, d_maps], axis=0).astype(BF), 3)
+        d_proj = jnp.where(living[None], d_proj, jnp.zeros((), BF)).T
+        grad_dt = contract(rates_kinds, d_dtp, 0, 0).reshape(3, dp, step_rows, channels)
+        bias_part = jnp.stack(
+            [jnp.sum(jnp.where(kinds[:, k : k + 1], d_dtp.astype(F32), 0.0), axis=0) for k in range(3)]
         )
-    d_normed = d_normed.astype(BF)
-    gain_part = jnp.sum(d_normed.astype(F32) * normed_all.astype(F32), axis=0) / norm_gain
-    table = [conv_part, conv_bias_part[None], alog_part, skip_part, bias_part]
-    table.append(gain_part.reshape(-1, channels))
-    table = jnp.concatenate(table, axis=0)
-    kept = table.shape[0]
-    table = jnp.pad(table, ((0, -kept % 8), (0, 0)))
-    small = jnp.concatenate([grad_x, grad_dt], axis=2).transpose(1, 0, 2, 3)
-    small = jnp.pad(small, ((0, 0), (0, 0), (0, -small.shape[2] % 16), (0, 0))).astype(BF)
-    d_normed, tables, small = finish(d_normed.reshape(wide, count, -1), table, small, 3)
+        d_proj_kinds = split_kinds(d_proj, kinds, 1)
+        d_inner = contract(d_proj_kinds, w_x_kinds.reshape(3 * rank, channels), 1, 0).astype(BF)
+        grad_x = contract(d_proj_kinds, inner, 0, 0)
+        grad_x = grad_x.reshape(3, dp, rank_rows, channels)
+
+        d_pre = (d_inner.astype(F32) + d_scan) * silu_slope(pre)
+        later = conv_masks(jnp.arange(span + width - 1, dtype=jnp.int32), bounds, width)
+        further = jnp.concatenate([d_pre, jnp.zeros((width - 1, channels), F32)], axis=0)
+        conv_rows = []
+        d_xs = jnp.zeros_like(xs_value)
+        for offset in range(width):
+            begin = width - 1 - offset
+            conv_rows.append(
+                jnp.sum(d_pre * masks[offset][:, None] * extended[begin : begin + span], axis=0)
+            )
+            masked = further * later[offset][:, None]
+            d_xs = d_xs + taps[begin][None, :] * masked[offset : offset + span]
+        conv_part = jnp.stack(conv_rows[::-1], axis=0)
+        conv_bias_part = jnp.sum(d_pre, axis=0)
+        d_xs = jnp.where(living[:, None], d_xs, 0.0).astype(BF)
+        d_z = jnp.where(living[:, None], d_z, jnp.zeros((), BF))
+        d_mixed = halves_back(d_xs, d_z, wide)
+        mixed_parts = from_partners(d_mixed)
+        grad_in = 0.0
+        for pair in range(0, dp, 2):
+            left = jnp.concatenate(feature_kinds[pair : pair + 2], axis=0)
+            grad_in = grad_in + contract(left, jnp.concatenate(mixed_parts[pair : pair + 2], axis=0), 0, 0)
+        in_grad = jnp.transpose(grad_in.reshape(3, -1, d_mixed.shape[1]), (1, 0, 2))
+
+        d_normed = jnp.zeros((span, x_in.shape[1]), F32)
+        w_in_kinds = w_in.reshape(dp, 3, -1, w_in.shape[1])
+        for kind in range(3):
+            picked = jnp.where(kinds[:, kind : kind + 1], d_mixed, jnp.zeros((), BF))
+            d_normed = d_normed + contract(
+                picked, w_in_kinds[:, kind].reshape(-1, w_in.shape[1]), 1, 1
+            )
+        d_normed = d_normed.astype(BF)
+        gain_part = jnp.sum(d_normed.astype(F32) * normed_all.astype(F32), axis=0)
+        table = [conv_part, conv_bias_part[None], extra, bias_part]
+        table.append(gain_part.reshape(-1, channels))
+        table = jnp.concatenate(table, axis=0)
+        table = jnp.pad(table, ((0, -table.shape[0] % 8), (0, 0)))
+        small = jnp.concatenate([grad_x, grad_dt], axis=2).transpose(1, 0, 2, 3)
+        small = jnp.pad(small, ((0, 0), (0, 0), (0, -small.shape[2] % 16), (0, 0))).astype(BF)
+        d_normed, tables, small = finish(d_normed.reshape(wide, count, -1), table, small, 4)
     xproj_grad = jnp.transpose(small[:, :rank_rows], (1, 0, 2))
     dtproj_grad = jnp.transpose(small[:, rank_rows : rank_rows + step_rows], (1, 0, 2))
     d_normed = d_normed.astype(BF).astype(F32)
@@ -1155,7 +1700,8 @@
     edge = width + 1 + STATE + 1
     shared = tables[:, :edge].transpose(1, 0, 2).reshape(edge, INNER)
     bias_grad = lax.dynamic_index_in_dim(tables, place, 0, False)[edge : edge + 3]
-    gain_grad = jnp.sum(tables[:, edge + 3 : kept], axis=0).reshape(-1)
+    kept = edge + 3 + x_in.shape[1] // channels
+    gain_grad = jnp.sum(tables[:, edge + 3 : kept], axis=0).reshape(-1) / norm_gain
     return (
         result,
         x_grad,

time: 561 us -> 514 us (0.916)
  Pallas kernels: 372 us -> 438 us
  matrix products: 58.2 us -> 0 us
  other arithmetic: 43.5 us -> 13.2 us
  starting transfers between devices: 15.8 us -> 4.59 us
  local copies, waits for them, and re-layouts: 44 us -> 33.7 us
    pallas_call x5, Pallas kernels: 196 us -> 261 us  [the longest x1 165 us: back(): pl.pallas_call(functools.partial(back_kernel, dp, wide, rank_rows, step_r...]
    dot_general x10 -> x0, matrix products: 58.2 us -> none  [contract(): lax.dot_general(left, right, (((left_dim,), (right_dim,)), ((), ())), pre...]
    unnamed x84 -> x56, local copies, waits for them, and re-layouts: 3.46 us -> 19 us
    select_n x10 -> x0, other arithmetic: 14.6 us -> none  [the longest x6 8.59 us: split_kinds(): jnp.where(picked, pieces, jnp.zeros((), rows.dtype))]
    slice x9 -> x1, local copies, waits for them, and re-layouts: 12.4 us -> 1.4 us  [body(): ends.append(ends[-1] + pieces[at])]
    ppermute x2 -> x0, starting transfers between devices: 9.62 us -> none  [the longest x1 9.47 us: halves_back(): got_a = lax.ppermute(jnp.where(is_even, xs, z), 'wide', even)]
    convert_element_type x5 -> x1, other arithmetic: 6.85 us -> 0.14 us  [body(): kinds_all.astype(F32)[None]]
    optimization_barrier x4 -> x0, local copies, waits for them, and re-layouts: 5.97 us -> none  [body(): lax.optimization_barrier((d_dtp, features, kinds_parts))]
  transfers between devices with their start and end apart: 13 -> 8, of which waited for: 1 -> 0; matrix products, arithmetic and copies ran while one was open for 21% -> 4% of each run, Pallas kernels for 27% -> 46%
where the time goes in v4:
time: 514 us; the launch traced here: 507 us
  Pallas kernels  438 us (85%)
  local copies, waits for them, and re-layouts  33.7 us (7%)
  between operations  17.4 us (3%)
  other arithmetic  13.2 us (3%)
    pallas_call x1, Pallas kernels, front(): pl.pallas_call(functools.partial(front_kernel, dp, wide, rank_rows), out_...  177 us
    pallas_call x1, Pallas kernels, back(): pl.pallas_call(functools.partial(back_kernel, dp, wide, rank_rows, step_r...  165 us
    pallas_call x1, Pallas kernels, scan_backward(): pl.pallas_call(scan_backward_kernel, grid=(nb,), in_specs=[row, row, pl.B...  47 us
    pallas_call x1, Pallas kernels, gate(): pl.pallas_call(gate_kernel, out_shape=[jax.ShapeDtypeStruct(gated.shape,...  21.9 us
    pallas_call x1, Pallas kernels, scan_forward(): pl.pallas_call(scan_forward_kernel, grid=(N // T,), in_specs=[pl.BlockSpe...  19.9 us
    unnamed x56, local copies, waits for them, and re-layouts  19 us
  transfers between devices with their start and end apart: 8, of which 0 were waited for; matrix products, arithmetic and copies ran while one was open for 4% of the time, Pallas kernels for 46%

profile of v4, /device:TPU:0, one launch (start us, length us, event | category | flops | bytes accessed | tf_op | source)
XLA Modules:
  0.0 506.6 jit_solution(4677860701852628138)
XLA Ops:
  7.2 0.0 reduce-scatter.3.cloned.1.call-start
  7.2 1.4 fusion.4
  11.2 0.7 pad_add_fusion
  12.0 0.1 convert_reduce_fusion.4
  12.2 0.1 pad_maximum_fusion
  12.2 1.0 copy.40.refs_7_.masks_ref.refs_21_
  13.3 1.9 fusion.refs_2_
  15.1 0.7 fusion.1
  15.8 0.7 broadcast_in_dim.16.refs_6_
  16.5 177.0 %front.1 = (bf16[4,3,512,1024]{3,2,1,0:T(8,128)(2,1)}, bf16[4,3,512,512]{3,2,1,0:T(8,128)(2,1)}, bf16[8,128,2048]{2,1,0:T(8,128)(2,1)}, bf16[8,128,2048]{2,1,0:T...) custom-call(f32[3,512,1024]{2,1,0:T(8,128)} %bitcast.59, ...), custom_call_target="tpu_custom_call" | custom-call | tf_op jit(solution)/shard_map/front/pallas_call | solution.py:642
  193.5 0.0 copy-done
  193.5 0.0 copy-done.13
  193.5 0.9 copy-done.2
  194.5 1.2 copy-done.4
  195.7 1.0 copy-done.8
  196.7 1.0 copy-done.9
  197.7 19.9 %scan_forward.1 = (bf16[1024,512]{1,0:T(8,128)(2,1)S(1)}, bf16[1024,512]{1,0:T(8,128)(2,1)S(1)}, f32[1024,512]{1,0:T(8,128)}, f32[32,16,512]{2,1,0:T(8,128)S(1)}) custom-call(bf16[160,1024]{1,0:T(8,128)(2,1)S(1)} %copy-done.9, bf16[3,128,512]{2,1,0:T(8,128)(2,1)S(1)} %copy-done.8, f32[3,512]{1,0:T(4,128)S(1)} %copy-done.15, bf16[1024,128]{1,0:T(8,128)(2,1)S(1)} %bitcast.51, ...), custom_call_target="tpu_custom_call" | custom-call | flops 20971520000 | bytes 16777216 | tf_op jit(solution)/shard_map/scan_forward/pallas_call | solution.py:76
  217.6 1.0 copy-done.17
  218.6 1.0 copy-done.19
  219.5 7.3 %branch.1 = bf16[1024,2048]{1,0:T(8,128)(2,1)S(1)} custom-call(bf16[1024,512]{1,0:T(8,128)(2,1)S(1)} %get-tuple-element.52.gated_ref, bf16[1024,128]{1,0:T(8,128)(2,1)S(1)} %bitcast.52, bf16[4,3,512,512]{3,2,1,0:T(8,128)(2,1)S(1)} %copy-done.12), custom_call_target="tpu_custom_call" | custom-call | flops 6442450944 | bytes 12582912 | tf_op jit(solution)/shard_map/branch/pallas_call | solution.py:1368
  226.9 2.0 copy-done.1
  228.9 0.0 reduce-scatter.3.cloned.1.call-update
  228.9 0.2 reduce-scatter.5.cloned.1.call-start
  229.1 21.9 %gate.1 = (bf16[1024,512]{1,0:T(8,128)(2,1)}, bf16[4,3,512,512]{3,2,1,0:T(8,128)(2,1)}) custom-call(bf16[1024,2048]{1,0:T(8,128)(2,1)} %bitcast.74, bf16[1024,512]{1,0:T(8,128)(2,1)} %copy-done.16, bf16[1024,128]{1,0:T(8,128)(2,1)} %bitcast.49, bf16[4,3,512,512]{3,2,1,0:T(8,128)(2,1)} %get-tuple-element.53.w_ref), custom_call_target="tpu_custom_call" | custom-call | flops 12884901888 | bytes 20971520 | tf_op jit(solution)/shard_map/gate/pallas_call | solution.py:1418
  251.0 0.0 reduce-scatter.5.cloned.1.call-update
  251.0 0.9 copy-done.3
  252.0 1.8 collective-permute-start.4
  253.7 0.2 collective-permute-start.3
  254.0 4.2 constant_dynamic-slice_fusion
  258.2 0.2 collective-permute-start
  258.4 0.3 collective-permute-start.1
  258.7 1.3 collective-permute-start.2
  260.0 47.0 %scan_backward.1 = (bf16[1024,512]{1,0:T(8,128)(2,1)S(1)}, f32[1024,512]{1,0:T(8,128)}, bf16[1024,512]{1,0:T(8,128)(2,1)S(1)}, f32[8,2,2048]{2,1,0:T(2,128)S(1)}, f32[17,512]{1,0:T(8,128)S(1)}) custom-call(bf16[1024,512]{1,0:T(8,128)(2,1)S(1)} %copy-done.18, bf16[1024,512]{1,0:T(8,128)(2,1)S(1)} %copy-done.5, bf16[160,1024]{1,0:T(8,128)(2,1)S(1)} %copy-done.10, ...), custom_call_target="tpu_custom_call" | custom-call | flops 50331648000 | bytes 25165824 | tf_op jit(solution)/shard_map/scan_backward/pallas_call | solution.py:173
  307.0 1.0 copy-done.6
  308.0 1.1 copy-done.7
  309.0 0.6 copy-done.11
  309.7 0.0 collective-permute-done.4.refs_6_
  309.7 0.5 collective-permute-start.5
  310.2 0.1 convert_reduce_fusion
  310.3 0.1 copy.43
  310.4 0.4 reshape.179
  310.7 0.3 copy.44
  311.1 0.7 copy.51
  311.8 0.0 collective-permute-done.3.refs_5_
  311.8 0.0 collective-permute-done.5.refs_7_
  311.8 0.0 collective-permute-done.refs_1_
  311.8 0.0 collective-permute-done.1.refs_2_
  311.8 0.0 collective-permute-done.2.refs_3_
  311.8 0.7 broadcast_in_dim.19.refs_20_
  312.5 0.0 copy-done.24
  312.5 164.6 %back.1 = (f32[3,512,1024]{2,1,0:T(8,128)}, f32[128,2048]{1,0:T(8,128)}, f32[8,32,512]{2,1,0:T(8,128)}, f32[3,80,512]{2,1,0:T(8,128)}) custom-call(bf16[1024,512]{1,0:T(8,128)(2,1)} %get-tuple-element.61.refs_0_, bf16[1024,512]{1,0:T(8,128)(2,1)} %collective-permute-done.refs_1_, bf16[1024,512]{1,0:T(8,128)(2,1)} %collective-permute-done.1.refs_2_, ...), custom_call_target="tpu_custom_call" | custom-call | tf_op jit(solution)/shard_map/back/pallas_call | solution.py:1309
  477.1 1.1 slice_bitcast_fusion
  478.3 0.6 slice.77
  479.0 0.7 copy.47
  479.7 0.9 slice_reduce_fusion
  480.6 0.6 div.22
  481.2 1.4 dynamic-slice_bitcast_fusion
  482.6 1.5 multiply_reduce_fusion.1
  484.1 0.6 fusion.2
  484.7 0.7 slice_bitcast_fusion.3
  485.4 0.7 slice_bitcast_fusion.2
  486.2 3.0 multiply_add_fusion
  489.2 3.5 convert_bitcast_fusion
  492.7 6.6 %copy.53 = f32[512,3,1024]{2,0,1:T(8,128)} copy(f32[512,3,1024]{2,0,1:T(8,128)} %bitcast.58) | data formatting | bytes 12582912
  (51 shorter events, 0.2 us)
Async XLA Ops:
  7.2 479.0 %reduce-scatter.3.cloned.1.call-start = ((), (), s32[]{:S(2)}) async-start(), calls=%async_computation.2 | async-start | bytes 4718592 | tf_op jit(solution)/shard_map/reduce_scatter | solution.py:1583
  16.5 177.0 %copy-start = (f32[1024,4]{1,0:T(8,128)S(1)}, f32[1024,4]{1,0:T(8,128)}, u32[]{:S(2)}) copy-start(f32[1024,4]{1,0:T(8,128)} %copy.40.refs_7_.masks_ref.refs_21_) | copy-start | bytes 49156
  16.5 177.0 %copy-start.13 = (f32[16,4096]{1,0:T(8,128)S(1)}, f32[16,4096]{1,0:T(8,128)}, u32[]{:S(2)}) copy-start(f32[16,4096]{1,0:T(8,128)} %alog_ref.3) | copy-start | bytes 786436
  16.5 177.0 %copy-start.14 = (f32[4096]{0:T(1024)S(1)}, f32[4096]{0:T(1024)}, u32[]{:S(2)}) copy-start(f32[4096]{0:T(1024)} %param.21) | copy-start | bytes 49156
  16.5 177.0 %copy-start.15 = (f32[3,512]{1,0:T(4,128)S(1)}, f32[3,512]{1,0:T(4,128)}, u32[]{:S(2)}) copy-start(f32[3,512]{1,0:T(4,128)} %dtb_ref.1) | copy-start | bytes 18436
  193.5 1.0 copy-start.2
  194.5 1.2 copy-start.4
  195.7 1.0 copy-start.8
  196.7 1.0 copy-start.9
  197.7 21.9 %copy-start.12 = (bf16[4,3,512,512]{3,2,1,0:T(8,128)(2,1)S(1)}, bf16[4,3,512,512]{3,2,1,0:T(8,128)(2,1)}, u32[]{:S(2)}) copy-start(bf16[4,3,512,512]{3,2,1,0:T(8,128)(2,1)} %get-tuple-element.53.w_ref) | copy-start | bytes 18874372
  217.6 1.0 copy-start.17
  218.6 1.0 copy-start.19
  219.5 7.4 %copy-start.16 = (bf16[1024,512]{1,0:T(8,128)(2,1)}, bf16[1024,512]{1,0:T(8,128)(2,1)S(1)}, u32[]{:S(2)}) copy-start(bf16[1024,512]{1,0:T(8,128)(2,1)S(1)} %get-tuple-element.52.gated_ref) | copy-start | bytes 3145732
  226.9 2.0 copy-start.1
  228.9 260.3 %reduce-scatter.5.cloned.1.call-start = ((), (), s32[]{:S(2)}) async-start(), calls=%async_computation.3 | async-start | bytes 7864320 | tf_op jit(solution)/shard_map/reduce_scatter | solution.py:1465
  251.0 0.9 copy-start.3
  252.0 57.7 %collective-permute-start.4 = (bf16[1024,1]{1,0:T(8,128)(2,1)S(1)}, bf16[1024,1]{1,0:T(8,128)(2,1)S(1)}, u32[]{:S(2)}, u32[]{:S(2)}) collective-permute-start(bf16[1024,1]{1,0:T(8,128)(2,1)S(1)} %bitcast.53), channel_id=1, source_target_pairs={{0,16},{8,24},{16,0},{24,8},{1,17},{9,25},{17,1},{25,9},{2,18},{10... | collective-permute-start | bytes 6152 | tf_op jit(solution)/shard_map/ppermute | solution.py:1470
  253.7 58.0 %collective-permute-start.3 = (bf16[1024,1]{1,0:T(8,128)(2,1)S(1)}, bf16[1024,1]{1,0:T(8,128)(2,1)}, u32[]{:S(2)}, u32[]{:S(2)}) collective-permute-start(bf16[1024,1]{1,0:T(8,128)(2,1)S(1)} %bitcast.54), channel_id=1, source_target_pairs={{0,8},{8,0},{16,24},{24,16},{1,9},{9,1},{17,25},{25,17},{2,10},{10... | collective-permute-start | bytes 6152 | tf_op jit(solution)/shard_map/ppermute | solution.py:1470
  253.9 6.1 %copy-start.5 = (bf16[1024,512]{1,0:T(8,128)(2,1)S(1)}, bf16[1024,512]{1,0:T(8,128)(2,1)}, u32[]{:S(2)}) copy-start(bf16[1024,512]{1,0:T(8,128)(2,1)} %get-tuple-element.50.u_ref.refs_14_) | copy-start | bytes 3145732
  253.9 6.1 %copy-start.10 = (bf16[160,1024]{1,0:T(8,128)(2,1)S(1)}, bf16[160,1024]{1,0:T(8,128)(2,1)}, u32[]{:S(2)}) copy-start(bf16[160,1024]{1,0:T(8,128)(2,1)} %get-tuple-element.47.proj_ref.refs_16_) | copy-start | bytes 983044
  253.9 6.1 %copy-start.18 = (bf16[1024,512]{1,0:T(8,128)(2,1)S(1)}, bf16[1024,512]{1,0:T(8,128)(2,1)}, u32[]{:S(2)}) copy-start(bf16[1024,512]{1,0:T(8,128)(2,1)} %copy-done.17) | copy-start | bytes 3145732
  258.2 53.6 %collective-permute-start = (bf16[1024,512]{1,0:T(8,128)(2,1)}, bf16[1024,512]{1,0:T(8,128)(2,1)}, u32[]{:S(2)}, u32[]{:S(2)}) collective-permute-start(bf16[1024,512]{1,0:T(8,128)(2,1)} %get-tuple-element.90), channel_id=1, source_target_pairs={{0,8},{8,0},{16,24},{24,16},{1,9},{9,1},{17,25},{25,17},{2,10},{10... | collective-permute-start | bytes 3145736 | tf_op jit(solution)/shard_map/ppermute | solution.py:1470
  258.4 53.4 %collective-permute-start.1 = (bf16[1024,512]{1,0:T(8,128)(2,1)}, bf16[1024,512]{1,0:T(8,128)(2,1)}, u32[]{:S(2)}, u32[]{:S(2)}) collective-permute-start(bf16[1024,512]{1,0:T(8,128)(2,1)} %get-tuple-element.89), channel_id=1, source_target_pairs={{0,16},{8,24},{16,0},{24,8},{1,17},{9,25},{17,1},{25,9},{2,18},{10... | collective-permute-start | bytes 3145736 | tf_op jit(solution)/shard_map/ppermute | solution.py:1470
  258.7 53.1 %collective-permute-start.2 = (bf16[1024,512]{1,0:T(8,128)(2,1)S(1)}, bf16[1024,512]{1,0:T(8,128)(2,1)}, u32[]{:S(2)}, u32[]{:S(2)}) collective-permute-start(bf16[1024,512]{1,0:T(8,128)(2,1)S(1)} %get-tuple-element.88), channel_id=1, source_target_pairs={{0,24},{8,16},{16,8},{24,0},{1,25},{9,17},{17,9},{25,1},{2,26},{10... | collective-permute-start | bytes 3145736 | tf_op jit(solution)/shard_map/ppermute | solution.py:1470
  307.0 1.0 copy-start.6
  308.0 1.1 copy-start.7
  309.0 0.6 copy-start.11
  309.7 2.8 copy-start.23
  309.7 2.1 collective-permute-start.5
  311.8 0.7 copy-start.24
  312.5 168.1 %copy-start.25 = (f32[2048]{0:T(1024)S(1)}, f32[2048]{0:T(1024)}, u32[]{:S(2)}) copy-start(f32[2048]{0:T(1024)} %param.17) | copy-start | bytes 24580
  312.5 170.1 %copy-start.20 = (f32[128,2048]{1,0:T(8,128)S(1)}, f32[128,2048]{1,0:T(8,128)}, u32[]{:S(2)}) copy-start(f32[128,2048]{1,0:T(8,128)} %refs_3_.1) | copy-start | bytes 3145732
  477.1 7.6 %copy-start.22 = (f32[3,80,512]{2,1,0:T(8,128)S(1)}, f32[3,80,512]{2,1,0:T(8,128)}, u32[]{:S(2)}) copy-start(f32[3,80,512]{2,1,0:T(8,128)} %get-tuple-element.80) | copy-start | bytes 1474564
  477.1 9.0 %copy-start.21 = (f32[128,2048]{1,0:T(8,128)S(1)}, f32[128,2048]{1,0:T(8,128)}, u32[]{:S(2)}) copy-start(f32[128,2048]{1,0:T(8,128)} %get-tuple-element.77) | copy-start | bytes 3145732
Sparse Core Ops, SparseCore 0:
  229.0 85.6 reduce-scatter.2
  317.9 87.0 reduce-scatter.4
